TPU v7x, 32 devices: a whole 2x2x4 slice. The times are simulated.
32 devices in a mesh: fsdp: 16 (over z, y, x), rep: 2 (over core).
Axes of the slice: x: 2, y: 2, z: 4, core: 2. Of those that a mesh axis runs over, the one named last changes fastest.
Arguments:
- input_fine: bfloat16 [32, 48, 48, 256], P(('fsdp', 'rep')), may hold values from -6 to 6
- input_coarse: bfloat16 [32, 24, 24, 128], P(('fsdp', 'rep')), may hold values from -6 to 6
- upstream_fine: bfloat16 [32, 48, 48, 256], P(('fsdp', 'rep')), may hold values from -6 to 6
- upstream_coarse: bfloat16 [32, 24, 24, 128], P(('fsdp', 'rep')), may hold values from -6 to 6
- extents: int32 [32, 2], P(('fsdp', 'rep')), may hold values from 24 to 48
- master: float32 [1065728], P('fsdp'), may hold values from -5 to 5, as said below
- first_moment: float32 [1065728], P('fsdp'), may hold values from -0.0014648438 to 0.0014648438
- second_moment: float32 [1065728], P('fsdp'), may hold values from 9.383258e-10 to 3.753303e-09
- average: float32 [1065728], P('fsdp'), may hold values from -9 to 9, as said below
Outputs:
- out_fine: float32 [32, 48, 48, 256], P(('fsdp', 'rep'))
- out_coarse: float32 [32, 24, 24, 128], P(('fsdp', 'rep'))
- grad_input_fine: float32 [32, 48, 48, 256], P(('fsdp', 'rep'))
- grad_input_coarse: float32 [32, 24, 24, 128], P(('fsdp', 'rep'))
- grad_norm: float32 [], replicated
- new_master: float32 [1065728], P('fsdp')
- new_first: float32 [1065728], P('fsdp')
- new_second: float32 [1065728], P('fsdp')
- new_average: float32 [1065728], P('fsdp')
- norm_grads: float32 [768], replicated
Inputs may be any that keep to these rules, and one draw needn't show every extreme that they name: `extents`: first column the valid height, second the valid width; the valid region is the top left corner of the padded image. `master`: the flat weight vector in the order of the steps. A running average of the flat weight vector.
All inputs are finite; a program needn't handle non-finite values.
Results may differ from a plain program's by a relative error of at most 0.024.
Values may be sent and summed in bfloat16 or wider, within the bound.
A program may use at most 64 MiB of HBM per device.

v0:
```python
import jax
import jax.numpy as jnp
from jax import lax
from jax.sharding import PartitionSpec as P

C1 = 256
C2 = 128
GROUPS = 8
ITERS = 12
STEP = 10


row_plan = ((1, -1), (0, 0), (1, 0))
clip_norm = 1.0
learn_rate = 0.02
beta_one = 0.9
beta_two = 0.999
adam_eps = 1e-08
decay_rate = 0.1


def shifted_field(values, down_by, right_by):
    height, breadth = (values.shape[1], values.shape[2])
    padded = jnp.pad(values, ((0, 0), (1, 1), (1, 1), (0, 0)))
    return padded[:, 1 + down_by : 1 + down_by + height, 1 + right_by : 1 + right_by + breadth, :]


def conv_same(values, kernel):
    summed = None
    for position in range(9):
        moved_values = shifted_field(values, position // 3 - 1, position % 3 - 1)
        product = jnp.einsum(
            "bhwc,cd->bhwd",
            moved_values,
            kernel[:, position, :],
            preferred_element_type=jnp.float32,
        )
        summed = product if summed is None else summed + product
    return summed


def kernel_grad(values, grad_out):
    columns = []
    for position in range(9):
        moved_values = shifted_field(values, position // 3 - 1, position % 3 - 1)
        columns.append(
            jnp.einsum("bhwc,bhwd->cd", moved_values, grad_out, preferred_element_type=jnp.float32)
        )
    return jnp.stack(columns, axis=1)


def paired_rows(values):
    images, height, breadth, channels = values.shape
    return values.reshape(images, height // 2, 2, breadth // 2, 2 * channels)


def phase_pick(paired, row_phase, col_phase, channels):
    return paired[:, :, row_phase, :, col_phase * channels : (col_phase + 1) * channels]


def conv_down(values, kernel):
    channels = values.shape[3]
    paired = paired_rows(values)
    summed = None
    for position in range(9):
        row_phase, row_shift = row_plan[position // 3]
        col_phase, col_shift = row_plan[position % 3]
        moved_values = shifted_field(
            phase_pick(paired, row_phase, col_phase, channels), row_shift, col_shift
        )
        product = jnp.einsum(
            "bhwc,cd->bhwd",
            moved_values,
            kernel[:, position, :],
            preferred_element_type=jnp.float32,
        )
        summed = product if summed is None else summed + product
    return summed


def conv_down_back(values, kernel, grad_out):
    channels = values.shape[3]
    paired = paired_rows(values)
    spread_all = jnp.einsum("bhwd,ctd->bhwtc", grad_out, kernel, preferred_element_type=jnp.float32)
    columns = []
    phase_parts = [[None, None], [None, None]]
    for position in range(9):
        row_phase, row_shift = row_plan[position // 3]
        col_phase, col_shift = row_plan[position % 3]
        moved_values = shifted_field(
            phase_pick(paired, row_phase, col_phase, channels), row_shift, col_shift
        )
        columns.append(
            jnp.einsum("bhwc,bhwd->cd", moved_values, grad_out, preferred_element_type=jnp.float32)
        )
        returned = shifted_field(spread_all[:, :, :, position, :], -row_shift, -col_shift)
        current = phase_parts[row_phase][col_phase]
        phase_parts[row_phase][col_phase] = returned if current is None else current + returned
    rows_joined = [jnp.concatenate(phase_parts[phase_row], axis=-1) for phase_row in range(2)]
    assembled = jnp.stack(rows_joined, axis=2).reshape(values.shape)
    return (jnp.stack(columns, axis=1), assembled)


def add_lifted(fine_values, lifted):
    paired_lift = jnp.concatenate([lifted, lifted], axis=-1)
    joined = paired_rows(fine_values) + paired_lift[:, :, None, :, :]
    return joined.reshape(fine_values.shape)


def fold_down(values):
    channels = values.shape[3]
    paired = paired_rows(values)
    rows_added = paired[:, :, 0] + paired[:, :, 1]
    return rows_added[..., :channels] + rows_added[..., channels:]


def group_total(per_channel):
    images, channels = per_channel.shape
    group_width = channels // GROUPS
    totals = jnp.sum(per_channel.reshape(images, GROUPS, group_width), axis=2)
    return jnp.repeat(totals, group_width, axis=1)


def normalize(values, validity):
    channels = values.shape[3]
    weights = validity[..., None]
    members = jnp.sum(validity, axis=(1, 2)) * (channels // GROUPS)
    centre = group_total(jnp.sum(values * weights, axis=(1, 2))) / members[:, None]
    centered = values - centre[:, None, None, :]
    spread = group_total(jnp.sum(centered * centered * weights, axis=(1, 2))) / members[:, None]
    inverse = lax.rsqrt(spread + 1e-05)
    return (centered * inverse[:, None, None, :], inverse)


def group_back(grad_hat, normed, inverse, validity):
    channels = grad_hat.shape[3]
    weights = validity[..., None]
    members = jnp.sum(validity, axis=(1, 2)) * (channels // GROUPS)
    mean_grad = group_total(jnp.sum(grad_hat * weights, axis=(1, 2))) / members[:, None]
    mean_cross = group_total(jnp.sum(grad_hat * normed * weights, axis=(1, 2))) / members[:, None]
    result = grad_hat - mean_grad[:, None, None, :] - normed * mean_cross[:, None, None, :]
    return result * inverse[:, None, None, :] * weights


def unpack(params):
    lengths = (9 * C1 * C1, 9 * C1 * C2, 9 * C2 * C2, C2 * C1, C1, C1, C2, C2)
    layouts = ((C1, 9, C1), (C1, 9, C2), (C2, 9, C2), (C2, C1), (C1,), (C1,), (C2,), (C2,))
    pieces = []
    offset = 0
    for length, layout in zip(lengths, layouts):
        pieces.append(params[offset : offset + length].reshape(layout))
        offset = offset + length
    return pieces


def masks_from(extents, height):
    row_index = jnp.arange(height)
    half_index = 2 * jnp.arange(height // 2)
    heights_of = extents[:, 0][:, None, None]
    widths_of = extents[:, 1][:, None, None]
    mask_fine = (
        (row_index[None, :, None] < heights_of) & (row_index[None, None, :] < widths_of)
    ).astype(jnp.float32)
    mask_coarse = (
        (half_index[None, :, None] < heights_of) & (half_index[None, None, :] < widths_of)
    ).astype(jnp.float32)
    return (mask_fine, mask_coarse)


def forward_layer(
    params, state_fine, state_coarse, input_fine, input_coarse, mask_fine, mask_coarse
):
    (
        kernel_fine,
        kernel_down,
        kernel_coarse,
        kernel_up,
        gain_fine,
        bias_fine,
        gain_coarse,
        bias_coarse,
    ) = unpack(params)
    normed_fine, inverse_fine = normalize(conv_same(state_fine, kernel_fine), mask_fine)
    normed_coarse, inverse_coarse = normalize(conv_same(state_coarse, kernel_coarse), mask_coarse)
    pre_fine = normed_fine * gain_fine.astype(jnp.float32) + bias_fine.astype(jnp.float32)
    pre_coarse = normed_coarse * gain_coarse.astype(jnp.float32) + bias_coarse.astype(jnp.float32)
    branch_fine = (
        (jax.nn.silu(pre_fine) + input_fine.astype(jnp.float32)) * mask_fine[..., None]
    ).astype(jnp.bfloat16)
    branch_coarse = (
        (jax.nn.silu(pre_coarse) + input_coarse.astype(jnp.float32)) * mask_coarse[..., None]
    ).astype(jnp.bfloat16)
    lifted = jnp.einsum(
        "bhwc,cd->bhwd", branch_coarse, kernel_up, preferred_element_type=jnp.float32
    )
    lowered = conv_down(branch_fine, kernel_down)
    out_fine = add_lifted(branch_fine.astype(jnp.float32), lifted) * mask_fine[..., None]
    out_coarse = (branch_coarse.astype(jnp.float32) + lowered) * mask_coarse[..., None]
    kept_values = (
        normed_fine,
        inverse_fine,
        pre_fine,
        branch_fine,
        normed_coarse,
        inverse_coarse,
        pre_coarse,
        branch_coarse,
    )
    return (out_fine, out_coarse, kept_values)


def branch_back(grad_input, pre_values, normed, inverse, gain, validity, state):
    logistic = jax.nn.sigmoid(pre_values)
    grad_pre = grad_input * logistic * (1.0 + pre_values * (1.0 - logistic))
    grad_gain = jnp.sum(grad_pre * normed, axis=(0, 1, 2))
    grad_bias = jnp.sum(grad_pre, axis=(0, 1, 2))
    grad_conv = group_back(grad_pre * gain.astype(jnp.float32), normed, inverse, validity).astype(
        jnp.bfloat16
    )
    return (kernel_grad(state, grad_conv), grad_gain, grad_bias)


def backward_layer(
    params,
    kept_values,
    state_fine,
    state_coarse,
    upstream_fine,
    upstream_coarse,
    mask_fine,
    mask_coarse,
):
    (
        kernel_fine,
        kernel_down,
        kernel_coarse,
        kernel_up,
        gain_fine,
        bias_fine,
        gain_coarse,
        bias_coarse,
    ) = unpack(params)
    (
        normed_fine,
        inverse_fine,
        pre_fine,
        branch_fine,
        normed_coarse,
        inverse_coarse,
        pre_coarse,
        branch_coarse,
    ) = kept_values
    cover_fine = mask_fine[..., None]
    cover_coarse = mask_coarse[..., None]
    seed_fine = upstream_fine.astype(jnp.float32) * cover_fine
    seed_coarse = upstream_coarse.astype(jnp.float32) * cover_coarse
    grad_lifted = fold_down(seed_fine).astype(jnp.bfloat16)
    grad_lowered = seed_coarse.astype(jnp.bfloat16)
    grad_up = jnp.einsum(
        "bhwc,bhwd->cd", branch_coarse, grad_lifted, preferred_element_type=jnp.float32
    )
    back_coarse = seed_coarse + jnp.einsum(
        "bhwd,cd->bhwc", grad_lifted, kernel_up, preferred_element_type=jnp.float32
    )
    grad_down, back_lowered = conv_down_back(branch_fine, kernel_down, grad_lowered)
    back_fine = seed_fine + back_lowered
    grad_input_fine = back_fine * cover_fine
    grad_input_coarse = back_coarse * cover_coarse
    grad_kernel_fine, grad_gain_fine, grad_bias_fine = branch_back(
        grad_input_fine, pre_fine, normed_fine, inverse_fine, gain_fine, mask_fine, state_fine
    )
    grad_kernel_coarse, grad_gain_coarse, grad_bias_coarse = branch_back(
        grad_input_coarse,
        pre_coarse,
        normed_coarse,
        inverse_coarse,
        gain_coarse,
        mask_coarse,
        state_coarse,
    )
    small_grad = jnp.concatenate(
        [grad_gain_fine, grad_bias_fine, grad_gain_coarse, grad_bias_coarse]
    )
    flat_grad = jnp.concatenate(
        [
            grad_kernel_fine.reshape(-1),
            grad_down.reshape(-1),
            grad_kernel_coarse.reshape(-1),
            grad_up.reshape(-1),
            small_grad,
        ]
    )
    return (flat_grad, small_grad, grad_input_fine, grad_input_coarse)


def per_device(
    input_fine,
    input_coarse,
    upstream_fine,
    upstream_coarse,
    extents,
    master,
    first_moment,
    second_moment,
    average,
):
    mask_fine, mask_coarse = masks_from(extents, input_fine.shape[1])
    shard_low = master.astype(jnp.bfloat16)
    resident = lax.all_gather(shard_low, "fsdp", axis=0, tiled=True)

    def fetch_params():
        return resident

    def iterate(step_index, states):
        next_fine, next_coarse, unused_values = forward_layer(
            fetch_params(), states[0], states[1], input_fine, input_coarse, mask_fine, mask_coarse
        )
        return (next_fine.astype(jnp.bfloat16), next_coarse.astype(jnp.bfloat16))

    initial = (
        jnp.zeros(input_fine.shape, jnp.bfloat16),
        jnp.zeros(input_coarse.shape, jnp.bfloat16),
    )
    state_fine, state_coarse = lax.fori_loop(0, ITERS, iterate, initial)
    params = fetch_params()
    out_fine, out_coarse, kept_values = forward_layer(
        params, state_fine, state_coarse, input_fine, input_coarse, mask_fine, mask_coarse
    )
    flat_grad, small_grad, grad_input_fine, grad_input_coarse = backward_layer(
        params,
        kept_values,
        state_fine,
        state_coarse,
        upstream_fine,
        upstream_coarse,
        mask_fine,
        mask_coarse,
    )
    small_total = lax.psum(small_grad, ("fsdp", "rep"))
    full_length = master.shape[0] * lax.axis_size("fsdp")
    flat_grad = jnp.concatenate(
        [flat_grad, jnp.zeros((full_length - flat_grad.shape[0],), jnp.float32)]
    )
    shard_grad = lax.psum_scatter(flat_grad, "fsdp", scatter_dimension=0, tiled=True)
    shard_grad = lax.psum(shard_grad.astype(jnp.bfloat16), "rep").astype(jnp.float32)
    total_square = lax.psum(jnp.sum(shard_grad * shard_grad), "fsdp")
    grad_norm = jnp.sqrt(total_square)
    factor = jnp.minimum(1.0, clip_norm / (grad_norm + 1e-06))
    clipped = shard_grad * factor
    new_first = beta_one * first_moment + (1.0 - beta_one) * clipped
    new_second = beta_two * second_moment + (1.0 - beta_two) * clipped * clipped
    corrected_first = new_first / (1.0 - beta_one**STEP)
    corrected_second = new_second / (1.0 - beta_two**STEP)
    new_master = master - learn_rate * (
        corrected_first / (jnp.sqrt(corrected_second) + adam_eps) + decay_rate * master
    )
    ema_rate = min(0.999, (1.0 + STEP) / (10.0 + STEP))
    new_average = ema_rate * average + (1.0 - ema_rate) * new_master
    norm_grads = small_total * factor
    return (
        out_fine,
        out_coarse,
        grad_input_fine,
        grad_input_coarse,
        grad_norm,
        new_master,
        new_first,
        new_second,
        new_average,
        norm_grads,
    )


def solution(mesh):
    in_specs = (
        P(("fsdp", "rep"), None, None, None),
        P(("fsdp", "rep"), None, None, None),
        P(("fsdp", "rep"), None, None, None),
        P(("fsdp", "rep"), None, None, None),
        P(("fsdp", "rep"), None),
        P("fsdp"),
        P("fsdp"),
        P("fsdp"),
        P("fsdp"),
    )
    out_specs = (
        P(("fsdp", "rep"), None, None, None),
        P(("fsdp", "rep"), None, None, None),
        P(("fsdp", "rep"), None, None, None),
        P(("fsdp", "rep"), None, None, None),
        P(),
        P("fsdp"),
        P("fsdp"),
        P("fsdp"),
        P("fsdp"),
        P(),
    )
    return jax.shard_map(
        per_device, mesh=mesh, in_specs=in_specs, out_specs=out_specs, check_vma=False
    )
```

profile of v0, /device:TPU:0, one launch (start us, length us, event | category | flops | bytes accessed | tf_op | source)
XLA Modules:
  0.0 1078.1 jit_solution(3631558685726777330)
XLA Ops:
  24.8 119.7 %all-reduce.23.cloned.1.call-done = bf16[1065728]{0:T(1024)(128)(2,1)} async-done(((bf16[1065728]{0:T(1024)(128)(2,1)}), bf16[1065728]{0:T(1024)(128)(2,1)}) %all-reduce.23.cloned.1.call-update) | async-done | bytes 2131472
  144.7 504.7 %while.15 = (s32[]{:T(128)}, bf16[1,48,48,256]{3,2,1,0:T(8,128)(2,1)S(1)}, bf16[1,24,24,128]{3,2,1,0:T(8,128)(2,1)S(1)}, bf16[1065728]{0:T(1024)(128)(2,1)}, f32...) while((s32[]{:T(128)}, ...), condition=%wide.region_11.12_spmd.clone, body=%wide.region_2.11_spmd.clone.sunk | while | flops 3286948352 | bytes 115754416 | solution.py:324
  176.4 3.5 fusion.482
  218.5 3.5 fusion.482
  260.5 3.5 fusion.482
  302.6 3.5 fusion.482
  344.6 3.5 fusion.482
  386.6 3.5 fusion.482
  428.7 3.5 fusion.482
  470.7 3.5 fusion.482
  512.8 3.5 fusion.482
  554.8 3.5 fusion.482
  596.8 3.5 fusion.482
  638.9 3.5 fusion.482
  664.4 3.6 reshape.1284
  667.9 6.5 fusion.376
  679.5 4.9 fusion.377
  706.2 8.2 fusion.108
  714.3 3.5 reshape.1321
  748.9 4.5 reshape.1326
  771.9 190.9 %all-reduce.24 = bf16[1065728]{0:T(1024)(128)(2,1)} all-reduce(f32[1065728]{0:T(1024)} %constant_dynamic-update-slice_fusion.1), channel_id=2, replica_groups=mesh['fsdp'=16,'rep'=2] {'fsdp'}, use_global_device_ids=true, to_apply=%region_32.33.clone | all-reduce | flops 1065728 | bytes 6394368
  967.7 15.6 %all-reduce.21.cloned.1.call-done = bf16[66608]{0:T(1024)(128)(2,1)} async-done(((bf16[66608]{0:T(1024)(128)(2,1)}), bf16[66608]{0:T(1024)(128)(2,1)}) %all-reduce.21.cloned.1.call-update) | async-done | bytes 133232 | tf_op jit(solution)/shard_map/psum | solution.py:345
  984.9 40.6 %psum.23 = f32[768]{0:T(1024)S(1)} all-reduce(f32[768]{0:T(1024)S(1)} %pad_maximum_fusion.1), channel_id=1, replica_groups=mesh['fsdp'=16,'rep'=2] {'fsdp','rep'}, use_global_device_ids=true, to_apply=%region_36.37 | all-reduce | flops 768 | bytes 6144 | tf_op jit(solution)/shard_map/psum | solution.py:339
  1025.4 41.1 %psum.22 = f32[]{:T(128)} all-reduce(f32[]{:T(128)} %fusion.256), channel_id=1, replica_groups=mesh['fsdp'=16,'rep'=2] {'fsdp'}, use_global_device_ids=true, to_apply=%region_35.36 | all-reduce | flops 1 | bytes 8 | tf_op jit(solution)/shard_map/psum | solution.py:346
  (1625 shorter events, 572.8 us)
Async XLA Ops:
  7.2 137.4 %all-reduce.23.cloned.1.call-start = ((), (), s32[]{:S(2)}) async-start(), calls=%async_computation.1 | async-start | bytes 4263936
  13.2 970.0 %all-reduce.21.cloned.1.call-start = ((), (), s32[]{:S(2)}) async-start(), calls=%async_computation | async-start | bytes 270336 | tf_op jit(solution)/shard_map/psum | solution.py:345
  145.4 9.0 copy-start.63
  187.5 9.0 copy-start.63
  229.5 9.0 copy-start.63
  271.6 9.0 copy-start.63
  313.6 9.0 copy-start.63
  355.6 9.0 copy-start.63
  397.7 9.0 copy-start.63
  439.7 9.0 copy-start.63
  481.7 9.0 copy-start.63
  523.8 9.0 copy-start.63
  565.8 9.0 copy-start.63
  655.0 66.5 %copy-start.69 = (f32[128]{0:T(128)}, f32[128]{0:T(128)S(1)}, u32[]{:S(2)}) copy-start(f32[128]{0:T(128)S(1)} %div.263) | copy-start | bytes 1540
  656.5 65.0 %copy-start.67 = (f32[128]{0:T(128)}, f32[128]{0:T(128)S(1)}, u32[]{:S(2)}) copy-start(f32[128]{0:T(128)S(1)} %rsqrt.61) | copy-start | bytes 1540
  656.5 65.0 %copy-start.71 = (f32[128]{0:T(128)}, f32[128]{0:T(128)S(1)}, u32[]{:S(2)}) copy-start(f32[128]{0:T(128)S(1)} %get-tuple-element.253) | copy-start | bytes 1540
  771.9 192.7 %copy-start.22 = (bf16[1,24,24,256]{3,2,1,0:T(8,128)(2,1)S(1)}, bf16[1,24,24,256]{3,2,1,0:T(8,128)(2,1)}, u32[]{:S(2)}) copy-start(bf16[1,24,24,256]{3,2,1,0:T(8,128)(2,1)} %copy-done.21) | copy-start | bytes 884740
  771.9 192.7 %copy-start.23 = (f32[24,24,128]{2,1,0:T(8,128)S(1)}, f32[24,24,128]{2,1,0:T(8,128)}, u32[]{:S(2)}) copy-start(f32[24,24,128]{2,1,0:T(8,128)} %fusion.269) | copy-start | bytes 884740
  771.9 192.7 %copy-start.47 = (bf16[256,1,128]{2,1,0:T(2,128)(2,1)S(1)}, bf16[256,1,128]{2,1,0:T(2,128)(2,1)}, u32[]{:S(2)}) copy-start(bf16[256,1,128]{2,1,0:T(2,128)(2,1)} %get-tuple-element.275) | copy-start | bytes 196612
  771.9 193.0 %copy-start.46 = (bf16[256,1,128]{2,1,0:T(2,128)(2,1)S(1)}, bf16[256,1,128]{2,1,0:T(2,128)(2,1)}, u32[]{:S(2)}) copy-start(bf16[256,1,128]{2,1,0:T(2,128)(2,1)} %get-tuple-element.274) | copy-start | bytes 196612
  966.1 101.8 %copy-start.24 = (f32[66608]{0:T(1024)S(1)}, f32[66608]{0:T(1024)}, u32[]{:S(2)}) copy-start(f32[66608]{0:T(1024)} %param.16) | copy-start | bytes 799300
  966.1 101.8 %copy-start.48 = (f32[66608]{0:T(1024)S(1)}, f32[66608]{0:T(1024)}, u32[]{:S(2)}) copy-start(f32[66608]{0:T(1024)} %param.19) | copy-start | bytes 799300
  966.1 101.8 %copy-start.49 = (f32[66608]{0:T(1024)S(1)}, f32[66608]{0:T(1024)}, u32[]{:S(2)}) copy-start(f32[66608]{0:T(1024)} %param.17) | copy-start | bytes 799300
  966.1 101.8 %copy-start.50 = (f32[66608]{0:T(1024)S(1)}, f32[66608]{0:T(1024)}, u32[]{:S(2)}) copy-start(f32[66608]{0:T(1024)} %param.18) | copy-start | bytes 799300
  (289 other events, 557.7 us)
Sparse Core Ops, SparseCore 0:
  14.2 130.2 all-reduce.22
  964.7 18.4 all-reduce.20
where the time goes:
time: 1090 us; the launch traced here: 1080 us
  local copies, waits for them, and re-layouts  316 us (29%)
  blocking collectives  273 us (25%)
  matrix products  168 us (15%)
  other arithmetic  162 us (15%)
  waiting for transfers between devices  135 us (12%)
  between operations  19.7 us (2%)
    unnamed x1, blocking collectives  191 us
    unnamed x3, waiting for transfers between devices  120 us
    dot_general x234, matrix products, conv_same(): jnp.einsum('bhwc,cd->bhwd', moved_values, kernel[:, position, :], preferr...  97.2 us
    slice x65, local copies, waits for them, and re-layouts, unpack(): pieces.append(params[offset:offset + length].reshape(layout))  67.6 us
    convert_element_type x12, other arithmetic, iterate(): return (next_fine.astype(jnp.bfloat16), next_coarse.astype(jnp.bfloat16))  41.7 us
    dot_general x117, matrix products, conv_down(): jnp.einsum('bhwc,cd->bhwd', moved_values, kernel[:, position, :], preferr...  41.1 us
    psum x1, blocking collectives, per_device(): total_square = lax.psum(jnp.sum(shard_grad * shard_grad), 'fsdp')  41.1 us
    psum x1, blocking collectives, per_device(): small_total = lax.psum(small_grad, ('fsdp', 'rep'))  40.6 us
  transfers between devices with their start and end apart: 2, of which 2 were waited for; matrix products, arithmetic and copies ran while one was open for 1% of the time, Pallas kernels for 0%

commit v1 on v0

v1 whole, which is shorter than its diff:
```python
import functools

import jax
import jax.numpy as jnp
from jax import lax
from jax.experimental import pallas as pl
from jax.experimental.pallas import tpu as pltpu
from jax.sharding import PartitionSpec as P

F32, BF = jnp.float32, jnp.bfloat16
C1, C2, GROUPS, ITERS, STEP = 256, 128, 8, 12, 10
HEIGHT, HALF = 48, 24
PIX, CPIX = HEIGHT * HEIGHT, HALF * HALF
FLAT_ROWS = 8326
ROW_DOWN, ROW_COARSE, ROW_UP, ROW_VEC = 4608, 6912, 8064, 8320

clip_norm = 1.0
learn_rate = 0.02
beta_one = 0.9
beta_two = 0.999
adam_eps = 1e-08
decay_rate = 0.1


def dot(a, b):
    return jnp.dot(a, b, preferred_element_type=F32)


def dot_rows(a, b):
    return lax.dot_general(a, b, (((0,), (0,)), ((), ())), preferred_element_type=F32)


def run_sum(x, width):
    lane = lax.broadcasted_iota(jnp.int32, x.shape, 1)
    step = 1
    while step < width:
        up = pltpu.roll(x, 128 - step, 1)
        down = pltpu.roll(x, step, 1)
        x = x + jnp.where((lane & step) == 0, up, down)
        step *= 2
    return x


def shift_down(x):
    row = lax.broadcasted_iota(jnp.int32, x.shape, 0)
    return jnp.where(row == 0, 0.0, pltpu.roll(x, 1, 0))


def shift_up(x):
    last = x.shape[0] - 1
    row = lax.broadcasted_iota(jnp.int32, x.shape, 0)
    return jnp.where(row == last, 0.0, pltpu.roll(x, last, 0))


def tile_sum(x):
    total = x[0:8]
    for i in range(1, x.shape[0] // 8):
        total = total + x[8 * i : 8 * i + 8]
    return total


def twice(m):
    return jnp.concatenate([m, m], axis=1)


def interleave(ref, r, even, odd):
    for p in range(2):
        at = slice(128 * p, 128 * p + 128)
        ref[p, pl.ds(r * 48, 24, stride=2), :] = even[:, at]
        ref[p, pl.ds(r * 48 + 1, 24, stride=2), :] = odd[:, at]


def rows_of(r, count, unit):
    return pl.ds(pl.multiple_of(r * unit, unit if unit % 16 == 0 else 8), count)


def layer_kernel(
    ext_ref, inp_ref, inc_ref, upf_ref, upc_ref,
    wf_ref, wdo_ref, wde_ref, wdt_ref, wc01_ref, wc2_ref, wu_ref, wut_ref,
    gf_ref, bf_ref, gc_ref, bc_ref,
    outf_ref, outc_ref, gif_ref, gic_ref, grad_ref,
    s_ref, do_ref, de_ref, c_ref, x_ref, xc_ref, lift_ref, mf_ref, mc_ref, scf_ref, scc_ref,
    gl_ref, glo_ref, back_ref, gp_ref, g_ref, row_ref, stage_ref, sem_ref,
):
    hh, ww = ext_ref[0, 0], ext_ref[0, 1]
    pos = lax.broadcasted_iota(jnp.int32, (48, 128), 0)
    col = jnp.where(pos < 24, 2 * pos, 2 * pos - 47)
    colm = jnp.where(col < ww, 1.0, 0.0).astype(F32)

    def setup(r, _):
        at = rows_of(r, 48, 48)
        mf_ref[at, :] = jnp.where(r < hh, colm, 0.0)
        x_ref[at, :] = jnp.zeros((48, 256), F32)
        return 0

    lax.fori_loop(0, 48, setup, 0)

    def setup_coarse(r, _):
        mc_ref[rows_of(r, 24, 24), :] = jnp.where(2 * r < hh, colm[0:24], 0.0)
        return 0

    lax.fori_loop(0, 24, setup_coarse, 0)
    nf = (hh * ww).astype(F32) * (C1 // GROUPS)
    nc = (((hh + 1) // 2) * ((ww + 1) // 2)).astype(F32) * (C2 // GROUPS)
    s_ref[0:48, :] = jnp.zeros((48, 768), BF)
    s_ref[49 * 48 : 50 * 48, :] = jnp.zeros((48, 768), BF)
    xc_ref[...] = jnp.zeros((576, 128), F32)
    scf_ref[...] = jnp.zeros((8, 256), F32)
    scc_ref[...] = jnp.zeros((8, 128), F32)
    scf_ref[1:2, :] = 0.5 * bf_ref[...]
    scc_ref[1:2, :] = 0.5 * bc_ref[...]

    def coarse_branch():
        h = xc_ref[...] * scc_ref[0:1, :] + scc_ref[1:2, :]
        y = h * jnp.tanh(h) + h
        branch = ((y + inc_ref[...].astype(F32)) * mc_ref[...]).astype(BF)
        lift_ref[...] = dot(branch, wu_ref[...])
        return branch

    def fine_rows(g, final):
        scale, shift = scf_ref[0:1, :], scf_ref[1:2, :]
        pieces = ([], [])
        for j in range(4):
            r = 4 * g + j
            at = rows_of(r, 48, 48)
            m = twice(mf_ref[at, :])
            h = x_ref[at, :] * scale + shift
            y = h * jnp.tanh(h) + h
            branch = ((y + inp_ref[at, :].astype(F32)) * m).astype(BF).astype(F32)
            even, odd = branch[0:24], branch[24:48]
            pieces[j % 2].append((shift_down(odd), even, odd))
            lift = lift_ref[rows_of(2 * g + j // 2, 24, 24), :]
            z = (branch + jnp.concatenate([lift, lift], axis=0)) * m
            even, odd = z[0:24], z[24:48]
            if final:
                interleave(stage_ref.at[0], r, even, odd)
            else:
                to = pl.ds(pl.multiple_of(r * 48 + 48, 48), 48)
                s_ref[to, 0:256] = jnp.concatenate([shift_down(odd), even], axis=0).astype(BF)
                s_ref[to, 256:512] = z.astype(BF)
                s_ref[to, 512:768] = jnp.concatenate([odd, shift_up(even)], axis=0).astype(BF)
        at = rows_of(g, 48, 48)
        for ref, (p0, p1) in ((de_ref, pieces[0]), (do_ref, pieces[1])):
            for q in range(3):
                ref[at, 256 * q : 256 * q + 256] = jnp.concatenate([p0[q], p1[q]], axis=0).astype(BF)

    def lowered():
        po = dot(do_ref[...], wdo_ref[...])
        pe = dot(de_ref[...], wde_ref[...])
        return pe + po[:, 128:] + jnp.concatenate([jnp.zeros((24, 128), F32), po[:552, :128]], axis=0)

    def finish(s, q, width, n, gain, bias, to_ref):
        s, q = jnp.sum(s, axis=0, keepdims=True), jnp.sum(q, axis=0, keepdims=True)
        for p in range(s.shape[1] // 128):
            at = slice(128 * p, 128 * p + 128)
            mean = run_sum(s[:, at], width) / n
            var = jnp.maximum(run_sum(q[:, at], width) / n - mean * mean, 0.0)
            inv = lax.rsqrt(var + 1e-5)
            to_ref[0:1, at] = 0.5 * inv * gain[:, at]
            to_ref[1:2, at] = 0.5 * (bias[:, at] - mean * inv * gain[:, at])
            to_ref[2:3, at] = mean
            to_ref[3:4, at] = inv

    def iterate(t, _):
        branch_c = coarse_branch()

        def fine(g, _):
            fine_rows(g, False)
            return 0

        lax.fori_loop(0, 12, fine, 0)
        zc = (branch_c.astype(F32) + lowered()) * mc_ref[...]
        rows = [zc[24 * r : 24 * r + 24] for r in range(24)]
        c_ref[:, 0:128] = jnp.concatenate([shift_down(v) for v in rows], axis=0).astype(BF)
        c_ref[:, 128:256] = zc.astype(BF)
        c_ref[:, 256:384] = jnp.concatenate([shift_up(v) for v in rows], axis=0).astype(BF)
        p01 = dot(c_ref[...], wc01_ref[...])
        p2 = dot(c_ref[...], wc2_ref[...])
        none = jnp.zeros((24, 128), F32)
        xc = (
            p01[:, 128:]
            + jnp.concatenate([none, p01[:552, :128]], axis=0)
            + jnp.concatenate([p2[24:], none], axis=0)
        )
        xc_ref[...] = xc
        xcm = xc * mc_ref[...]
        sums_c = tile_sum(xcm), tile_sum(xcm * xcm)
        for b in range(4):
            at = 576 * b
            total = None
            for dy in range(3):
                p = dot(s_ref[at + 48 * dy : at + 48 * dy + 576, :], wf_ref[768 * dy : 768 * dy + 768, :])
                total = p if total is None else total + p
            x_ref[at : at + 576, :] = total

        def stats(r, carry):
            at = rows_of(r, 48, 48)
            xm = x_ref[at, :] * twice(mf_ref[at, :])
            return carry[0] + tile_sum(xm), carry[1] + tile_sum(xm * xm)

        none = jnp.zeros((8, 256), F32)
        sums_f = lax.fori_loop(0, 48, stats, (none, none), unroll=4)
        finish(*sums_f, C1 // GROUPS, nf, gf_ref[...], bf_ref[...], scf_ref)
        finish(*sums_c, C2 // GROUPS, nc, gc_ref[...], bc_ref[...], scc_ref)
        return 0

    lax.fori_loop(0, ITERS, iterate, 0)
    branch_c = coarse_branch()

    def fine_last(g, _):
        fine_rows(g, True)
        return 0

    lax.fori_loop(0, 12, fine_last, 0)
    sends = [
        pltpu.make_async_copy(stage_ref.at[i, p], ref.at[:, 128 * p : 128 * p + 128], sem_ref.at[i, p])
        for i, ref in enumerate((outf_ref, gif_ref))
        for p in range(2)
    ]
    sends[0].start()
    sends[1].start()
    outc_ref[...] = (branch_c.astype(F32) + lowered()) * mc_ref[...]

    seed_c = upc_ref[...].astype(F32) * mc_ref[...]
    none = jnp.zeros((24, 128), F32)
    rows = [seed_c[24 * r : 24 * r + 24] for r in range(24)]
    right = jnp.concatenate([shift_up(v) for v in rows], axis=0)
    glo_ref[:, 0:128] = seed_c.astype(BF)
    glo_ref[:, 128:256] = jnp.concatenate([seed_c[24:], none], axis=0).astype(BF)
    glo_ref[:, 256:384] = right.astype(BF)
    glo_ref[:, 384:512] = jnp.concatenate([right[24:], none], axis=0).astype(BF)

    def fold(g, _):
        both = []
        for i in range(2):
            total = None
            for j in range(2):
                at = rows_of(4 * g + 2 * i + j, 48, 48)
                seed = upf_ref[at, :].astype(F32) * twice(mf_ref[at, :])
                part = seed[0:24] + seed[24:48]
                total = part if total is None else total + part
            both.append(total)
        gl_ref[rows_of(g, 48, 48), :] = jnp.concatenate(both, axis=0).astype(BF)
        return 0

    lax.fori_loop(0, 12, fold, 0)
    up_grad = dot_rows(branch_c, gl_ref[...])
    for j in range(2):
        grad_ref[pl.ds(ROW_UP + j, 128, stride=2), :] = up_grad[:, 128 * j : 128 * j + 128]
    down_even = dot_rows(de_ref[...], glo_ref[:, 0:128])
    down_odd = dot_rows(do_ref[...], glo_ref[:, 0:256])
    for dx in range(3):
        at = slice(256 * dx, 256 * dx + 256)
        grad_ref[pl.ds(ROW_DOWN + dx, 256, stride=9), :] = down_odd[at, 128:256]
        grad_ref[pl.ds(ROW_DOWN + 3 + dx, 256, stride=9), :] = down_even[at]
        grad_ref[pl.ds(ROW_DOWN + 6 + dx, 256, stride=9), :] = down_odd[at, 0:128]

    back_c = (seed_c + dot(gl_ref[...], wut_ref[...])) * mc_ref[...]
    gic_ref[...] = back_c

    def pre_grad(gi, x, scale, shift, mean, inv):
        h = x * scale + shift
        t = jnp.tanh(h)
        sig = 0.5 * t + 0.5
        normed = (x - mean) * inv
        return gi * sig * (1.0 + 2.0 * h * (1.0 - sig)), normed

    def back_means(sum_bias, sum_gain, gain, width, n):
        return run_sum(sum_bias * gain, width) / n, run_sum(sum_gain * gain, width) / n

    gp_c, normed_c = pre_grad(
        back_c, xc_ref[...], scc_ref[0:1, :], scc_ref[1:2, :], scc_ref[2:3, :], scc_ref[3:4, :]
    )
    gain_c = jnp.sum(gp_c * normed_c, axis=0, keepdims=True)
    bias_c = jnp.sum(gp_c, axis=0, keepdims=True)
    grad_ref[ROW_VEC + 4 : ROW_VEC + 5, :] = gain_c
    grad_ref[ROW_VEC + 5 : ROW_VEC + 6, :] = bias_c
    grad_ref[ROW_VEC + 6 : ROW_VEC + 8, :] = jnp.zeros((2, 128), F32)
    mean_h, mean_hn = back_means(bias_c, gain_c, gc_ref[...], C2 // GROUPS, nc)
    gconv_c = (gp_c * gc_ref[...] - mean_h - normed_c * mean_hn) * scc_ref[3:4, :] * mc_ref[...]
    around = jnp.concatenate(
        [
            jnp.concatenate([gconv_c[24:], none], axis=0),
            gconv_c,
            jnp.concatenate([none, gconv_c[:552]], axis=0),
        ],
        axis=1,
    ).astype(BF)
    coarse_grad = dot_rows(c_ref[...], around)
    for dy in range(3):
        for dx in range(3):
            grad_ref[pl.ds(ROW_COARSE + 3 * dy + dx, 128, stride=9), :] = coarse_grad[
                128 * dx : 128 * dx + 128, 128 * dy : 128 * dy + 128
            ]

    back_ref[0] = dot(glo_ref[:, 0:128], wdt_ref[0:128, :])
    g00, g10, g01, g11 = (glo_ref[:, 128 * i : 128 * i + 128] for i in range(4))
    back_ref[1] = dot(jnp.concatenate([g00, g01], axis=1), wdt_ref[128:384, :])
    back_ref[2] = dot(jnp.concatenate([g00, g10], axis=1), wdt_ref[384:640, :])
    back_ref[3] = dot(jnp.concatenate([g00, g01, g10, g11], axis=1), wdt_ref[640:1152, :])

    def fine_back(i, carry):
        sums = list(carry)
        for j in range(2):
            r = 2 * i + j
            at = rows_of(r, 48, 48)
            half = rows_of(i, 24, 24)
            m = twice(mf_ref[at, :])
            back = jnp.concatenate([back_ref[2 * j, half, :], back_ref[2 * j + 1, half, :]], axis=0)
            gi = (upf_ref[at, :].astype(F32) + back) * m
            interleave(stage_ref.at[1], r, gi[0:24], gi[24:48])
            gp, normed = pre_grad(
                gi, x_ref[at, :], scf_ref[0:1, :], scf_ref[1:2, :], scf_ref[2:3, :], scf_ref[3:4, :]
            )
            gp_ref[at, :] = gp
            sums[0] = sums[0] + tile_sum(gp * normed)
            sums[1] = sums[1] + tile_sum(gp)
        return tuple(sums)

    none8 = jnp.zeros((8, 256), F32)
    gain_f, bias_f = lax.fori_loop(0, 24, fine_back, (none8, none8))
    sends[2].start()
    sends[3].start()
    gain_f = jnp.sum(gain_f, axis=0, keepdims=True)
    bias_f = jnp.sum(bias_f, axis=0, keepdims=True)
    mean_h, mean_hn = [], []
    for p in range(2):
        at = slice(128 * p, 128 * p + 128)
        grad_ref[ROW_VEC + p : ROW_VEC + p + 1, :] = gain_f[:, at]
        grad_ref[ROW_VEC + 2 + p : ROW_VEC + 3 + p, :] = bias_f[:, at]
        a, b = back_means(bias_f[:, at], gain_f[:, at], gf_ref[:, at], C1 // GROUPS, nf)
        mean_h.append(a)
        mean_hn.append(b)
    row_ref[0:1, :] = jnp.concatenate(mean_h, axis=1)
    row_ref[1:2, :] = jnp.concatenate(mean_hn, axis=1)
    g_ref[0:48, :] = jnp.zeros((48, 256), BF)
    g_ref[49 * 48 : 50 * 48, :] = jnp.zeros((48, 256), BF)

    def fine_conv_grad(r, _):
        at = rows_of(r, 48, 48)
        normed = (x_ref[at, :] - scf_ref[2:3, :]) * scf_ref[3:4, :]
        g = (gp_ref[at, :] * gf_ref[...] - row_ref[0:1, :] - normed * row_ref[1:2, :]) * scf_ref[3:4, :]
        g_ref[pl.ds(pl.multiple_of(r * 48 + 48, 48), 48), :] = (g * twice(mf_ref[at, :])).astype(BF)
        return 0

    lax.fori_loop(0, 48, fine_conv_grad, 0)
    for dx in range(3):
        states = s_ref[48:2352, 256 * dx : 256 * dx + 256]
        for dy in range(3):
            grad = dot_rows(states, g_ref[48 * (2 - dy) : 48 * (2 - dy) + 2304, :])
            for j in range(2):
                grad_ref[pl.ds(2 * (3 * dy + dx) + j, 256, stride=18), :] = grad[:, 128 * j : 128 * j + 128]
    for send in sends:
        send.wait()


def layer_call(*args):
    whole = pl.BlockSpec(memory_space=pltpu.VMEM)
    return pl.pallas_call(
        layer_kernel,
        out_shape=[
            jax.ShapeDtypeStruct((PIX, 256), F32),
            jax.ShapeDtypeStruct((CPIX, 128), F32),
            jax.ShapeDtypeStruct((PIX, 256), F32),
            jax.ShapeDtypeStruct((CPIX, 128), F32),
            jax.ShapeDtypeStruct((8328, 128), F32),
        ],
        in_specs=[pl.BlockSpec(memory_space=pltpu.SMEM)] + [whole] * 16,
        out_specs=[pl.BlockSpec(memory_space=pl.ANY), whole, pl.BlockSpec(memory_space=pl.ANY), whole, whole],
        scratch_shapes=[
            pltpu.VMEM((2400, 768), BF),
            pltpu.VMEM((576, 768), BF),
            pltpu.VMEM((576, 768), BF),
            pltpu.VMEM((576, 384), BF),
            pltpu.VMEM((PIX, 256), F32),
            pltpu.VMEM((CPIX, 128), F32),
            pltpu.VMEM((CPIX, 256), F32),
            pltpu.VMEM((PIX, 128), F32),
            pltpu.VMEM((CPIX, 128), F32),
            pltpu.VMEM((8, 256), F32),
            pltpu.VMEM((8, 128), F32),
            pltpu.VMEM((CPIX, 256), BF),
            pltpu.VMEM((CPIX, 512), BF),
            pltpu.VMEM((4, CPIX, 256), F32),
            pltpu.VMEM((PIX, 256), F32),
            pltpu.VMEM((2400, 256), BF),
            pltpu.VMEM((8, 256), F32),
            pltpu.VMEM((2, 2, PIX, 128), F32),
            pltpu.SemaphoreType.DMA((2, 2)),
        ],
        compiler_params=pltpu.CompilerParams(vmem_limit_bytes=62 * 2**20),
        name="layer",
    )(*args)


def by_parity(x):
    _, h, w, c = x.shape
    return x.reshape(h, w // 2, 2, c).transpose(0, 2, 1, 3).reshape(h * w, c)


def unpack(params):
    layouts = ((C1, 9, C1), (C1, 9, C2), (C2, 9, C2), (C2, C1), (1, C1), (1, C1), (1, C2), (1, C2))
    pieces = []
    offset = 0
    for layout in layouts:
        length = 1
        for size in layout:
            length *= size
        pieces.append(params[offset : offset + length].reshape(layout))
        offset = offset + length
    return pieces


def weight_forms(params):
    kf, kd, kc, ku, gf, bf, gc, bc = unpack(params)
    wf = kf.transpose(1, 0, 2).reshape(9 * C1, C1)
    kd = kd.transpose(1, 0, 2)
    turned = kd.transpose(0, 2, 1)
    wdt = jnp.concatenate([turned[t] for t in (4, 5, 3, 7, 1, 8, 6, 2, 0)], axis=0)
    kd = kd.reshape(3, 3 * C1, C2)
    kc = kc.transpose(1, 0, 2).reshape(3, 3 * C2, C2)
    return (
        wf,
        jnp.concatenate([kd[0], kd[2]], axis=1),
        kd[1],
        wdt,
        jnp.concatenate([kc[0], kc[1]], axis=1),
        kc[2],
        ku,
        ku.T,
        gf.astype(F32),
        bf.astype(F32),
        gc.astype(F32),
        bc.astype(F32),
    )


def per_device(
    input_fine, input_coarse, upstream_fine, upstream_coarse, extents, master, first_moment, second_moment, average
):
    resident = lax.all_gather(master.astype(BF), "fsdp", axis=0, tiled=True)
    out_fine, out_coarse, gi_fine, gi_coarse, grad = layer_call(
        extents,
        by_parity(input_fine),
        input_coarse.reshape(CPIX, C2),
        by_parity(upstream_fine),
        upstream_coarse.reshape(CPIX, C2),
        *weight_forms(resident),
    )
    flat_grad = grad[:FLAT_ROWS].reshape(-1)
    small_total = lax.psum(flat_grad[-2 * (C1 + C2) :], ("fsdp", "rep"))
    shard_grad = lax.psum_scatter(flat_grad, "fsdp", scatter_dimension=0, tiled=True)
    shard_grad = lax.psum(shard_grad.astype(BF), "rep").astype(F32)
    total_square = lax.psum(jnp.sum(shard_grad * shard_grad), "fsdp")
    grad_norm = jnp.sqrt(total_square)
    factor = jnp.minimum(1.0, clip_norm / (grad_norm + 1e-06))
    clipped = shard_grad * factor
    new_first = beta_one * first_moment + (1.0 - beta_one) * clipped
    new_second = beta_two * second_moment + (1.0 - beta_two) * clipped * clipped
    corrected_first = new_first / (1.0 - beta_one**STEP)
    corrected_second = new_second / (1.0 - beta_two**STEP)
    new_master = master - learn_rate * (
        corrected_first / (jnp.sqrt(corrected_second) + adam_eps) + decay_rate * master
    )
    ema_rate = min(0.999, (1.0 + STEP) / (10.0 + STEP))
    new_average = ema_rate * average + (1.0 - ema_rate) * new_master
    norm_grads = small_total * factor
    return (
        out_fine.reshape(input_fine.shape),
        out_coarse.reshape(input_coarse.shape),
        gi_fine.reshape(input_fine.shape),
        gi_coarse.reshape(input_coarse.shape),
        grad_norm,
        new_master,
        new_first,
        new_second,
        new_average,
        norm_grads,
    )


def solution(mesh):
    images = P(("fsdp", "rep"), None, None, None)
    flat = P("fsdp")
    in_specs = (images,) * 4 + (P(("fsdp", "rep"), None),) + (flat,) * 4
    out_specs = (images,) * 4 + (P(),) + (flat,) * 4 + (P(),)
    return jax.shard_map(per_device, mesh=mesh, in_specs=in_specs, out_specs=out_specs, check_vma=False)
```

time: 1090 us -> 555 us (0.51); the launches traced: 1080 us -> 555 us
  local copies, waits for them, and re-layouts: 316 us -> 24 us
  matrix products: 168 us -> 0 us
  other arithmetic: 162 us -> 7.79 us
  Pallas kernels: 0 us -> 89.8 us
    dot_general x394 -> x0, matrix products: 168 us -> none  [the longest x234 97.2 us: conv_same(): jnp.einsum('bhwc,cd->bhwd', moved_values, kernel[:, position, :], preferr...]
    pallas_call x0 -> x1, Pallas kernels: none -> 89.8 us  [layer_call(): pl.pallas_call(layer_kernel, out_shape=[jax.ShapeDtypeStruct((PIX, 256),...]
    convert_element_type x42 -> x3, other arithmetic: 71.7 us -> 2.06 us  [the longest x1 0.97 us: per_device(): resident = lax.all_gather(master.astype(BF), 'fsdp', axis=0, tiled=True)]
    slice x65 -> x8, local copies, waits for them, and re-layouts: 67.6 us -> 2.58 us  [unpack(): pieces.append(params[offset:offset + length].reshape(layout))]
    slice x40 -> x9, local copies, waits for them, and re-layouts: 62.6 us -> 4.6 us  [the longest x2 1.05 us: weight_forms(): kd[1]]
    reshape x74 -> x5, local copies, waits for them, and re-layouts: 49 us -> 7.18 us  [the longest x1 3.77 us: per_device(): flat_grad = grad[:FLAT_ROWS].reshape(-1)]
    reshape x39 -> x4, local copies, waits for them, and re-layouts: 39.8 us -> 1.73 us  [unpack(): pieces.append(params[offset:offset + length].reshape(layout))]
    reduce_sum x85 -> x0, other arithmetic: 36.4 us -> none  [the longest x26 18.8 us: normalize(): jnp.sum(centered * centered * weights, axis=(1, 2))]
where the time goes in v1:
time: 555 us
  blocking collectives  271 us (49%)
  waiting for transfers between devices  145 us (26%)
  Pallas kernels  89.8 us (16%)
  local copies, waits for them, and re-layouts  24 us (4%)
  between operations  17.5 us (3%)
  other arithmetic  7.79 us (1%)
    unnamed x1, blocking collectives  189 us
    unnamed x3, waiting for transfers between devices  127 us
    pallas_call x1, Pallas kernels, layer_call(): pl.pallas_call(layer_kernel, out_shape=[jax.ShapeDtypeStruct((PIX, 256),...  89.8 us
    psum x1, blocking collectives, per_device(): total_square = lax.psum(jnp.sum(shard_grad * shard_grad), 'fsdp')  41.1 us
    psum x1, blocking collectives, per_device(): small_total = lax.psum(flat_grad[-2 * (C1 + C2):], ('fsdp', 'rep'))  40.6 us
    psum x1, waiting for transfers between devices, per_device(): shard_grad = lax.psum(shard_grad.astype(BF), 'rep').astype(F32)  17.9 us
  transfers between devices with their start and end apart: 2, of which 2 were waited for; matrix products, arithmetic and copies ran while one was open for 1% of the time, Pallas kernels for 0%

profile of v1, /device:TPU:0, one launch (start us, length us, event | category | flops | bytes accessed | tf_op | source)
XLA Modules:
  0.0 554.6 jit_solution(6108366979709182208)
XLA Ops:
  7.2 1.0 convert_element_type.29
  8.2 1.3 fusion.19
  10.4 1.5 dynamic-update-slice
  11.9 1.3 copy-done
  13.8 1.2 copy.33
  15.9 1.2 copy.34
  17.8 126.8 %all-reduce.8.cloned.1.call-done = bf16[1065728]{0:T(1024)(128)(2,1)} async-done(((bf16[1065728]{0:T(1024)(128)(2,1)}), bf16[1065728]{0:T(1024)(128)(2,1)}) %all-reduce.8.cloned.1.call-update) | async-done | bytes 2131472
  144.6 0.8 slice.140
  145.4 0.7 copy.43
  146.2 1.0 slice.136
  149.7 0.7 copy.39
  150.6 0.9 copy-done.6
  152.5 0.7 copy.36
  153.9 1.4 copy.35
  156.0 0.8 pad_maximum_fusion.wdo_ref
  157.9 89.8 %layer.1 = (f32[2304,256]{1,0:T(8,128)}, f32[576,128]{1,0:T(8,128)}, f32[2304,256]{1,0:T(8,128)}, f32[576,128]{1,0:T(8,128)}, f32[8328,128]{1,0:T(8,128)}) custom-call(s32[1,2]{1,0:T(1,128)} %ext_ref.1, bf16[2304,256]{1,0:T(8,128)(2,1)} %bitcast.85, bf16[576,128]{1,0:T(8,128)(2,1)} %bitcast.104, bf16[2304,256]{1,0:T(8,128)(2,1)} %bitcast.86, ...), custom_call_target="tpu_custom_call" | custom-call | tf_op jit(solution)/shard_map/layer/pallas_call | solution.py:359
  247.7 3.8 slice_bitcast_fusion
  251.5 189.0 %all-reduce.9 = bf16[1065728]{0:T(1024)(128)(2,1)S(1)} all-reduce(f32[1065728]{0:T(1024)} %slice_bitcast_fusion), channel_id=2, replica_groups=mesh['fsdp'=16,'rep'=2] {'fsdp'}, use_global_device_ids=true, to_apply=%region_0.0.clone | all-reduce | flops 1065728 | bytes 6394368
  440.6 0.8 dynamic-slice.4
  442.1 17.9 %all-reduce.6.cloned.1.call-done = bf16[66608]{0:T(1024)(128)(2,1)} async-done(((bf16[66608]{0:T(1024)(128)(2,1)}), bf16[66608]{0:T(1024)(128)(2,1)}) %all-reduce.6.cloned.1.call-update) | async-done | bytes 133232 | tf_op jit(solution)/shard_map/psum | solution.py:453
  460.0 1.6 fusion.2
  461.5 40.6 %psum.23 = f32[768]{0:T(1024)S(1)} all-reduce(f32[768]{0:T(1024)S(1)} %slice_bitcast_fusion.10), channel_id=1, replica_groups=mesh['fsdp'=16,'rep'=2] {'fsdp','rep'}, use_global_device_ids=true, to_apply=%region_4.0 | all-reduce | flops 768 | bytes 6144 | tf_op jit(solution)/shard_map/psum | solution.py:451
  502.1 41.1 %psum.22 = f32[]{:T(128)} all-reduce(f32[]{:T(128)} %fusion.2), channel_id=1, replica_groups=mesh['fsdp'=16,'rep'=2] {'fsdp'}, use_global_device_ids=true, to_apply=%region_3.0 | all-reduce | flops 1 | bytes 8 | tf_op jit(solution)/shard_map/psum | solution.py:454
  544.6 2.1 multiply_add_fusion
  (60 shorter events, 9.1 us)
Async XLA Ops:
  7.2 137.4 %all-reduce.8.cloned.1.call-start = ((), (), s32[]{:S(2)}) async-start(), calls=%async_computation.1 | async-start | bytes 4263936
  10.2 3.1 copy-start.2
  11.9 1.3 copy-start
  13.2 446.7 %all-reduce.6.cloned.1.call-start = ((), (), s32[]{:S(2)}) async-start(), calls=%async_computation | async-start | bytes 270336 | tf_op jit(solution)/shard_map/psum | solution.py:453
  13.8 1.7 copy-start.3
  145.4 4.2 copy-start.7
  145.4 4.0 slice-start
  150.6 0.9 copy-start.6
  151.8 1.5 slice-start.1
  153.9 1.5 copy-start.8
  153.9 1.5 copy-start.9
  153.9 2.2 copy-start.5
  153.9 3.0 copy-start.1
  251.5 293.1 %copy-start.4 = (f32[66608]{0:T(1024)S(1)}, f32[66608]{0:T(1024)}, u32[]{:S(2)}) copy-start(f32[66608]{0:T(1024)} %param.14) | copy-start | bytes 799300
  251.5 293.1 %copy-start.10 = (f32[66608]{0:T(1024)S(1)}, f32[66608]{0:T(1024)}, u32[]{:S(2)}) copy-start(f32[66608]{0:T(1024)} %param.17) | copy-start | bytes 799300
  251.5 293.1 %copy-start.11 = (f32[66608]{0:T(1024)S(1)}, f32[66608]{0:T(1024)}, u32[]{:S(2)}) copy-start(f32[66608]{0:T(1024)} %param.15) | copy-start | bytes 799300
  251.5 293.1 %copy-start.12 = (f32[66608]{0:T(1024)S(1)}, f32[66608]{0:T(1024)}, u32[]{:S(2)}) copy-start(f32[66608]{0:T(1024)} %param.16) | copy-start | bytes 799300
Sparse Core Ops, SparseCore 0:
  14.2 130.2 all-reduce.7
  441.5 18.4 all-reduce.5

commit v2 on v1

--- a/solution.py
+++ b/solution.py
@@ -28,6 +28,10 @@
 
 def dot_rows(a, b):
     return lax.dot_general(a, b, (((0,), (0,)), ((), ())), preferred_element_type=F32)
+
+
+def dot_lanes(a, b):
+    return lax.dot_general(a, b, (((1,), (1,)), ((), ())), preferred_element_type=F32)
 
 
 def run_sum(x, width):
@@ -75,14 +79,17 @@
 
 
 def layer_kernel(
-    ext_ref, inp_ref, inc_ref, upf_ref, upc_ref,
-    wf_ref, wdo_ref, wde_ref, wdt_ref, wc01_ref, wc2_ref, wu_ref, wut_ref,
-    gf_ref, bf_ref, gc_ref, bc_ref,
-    outf_ref, outc_ref, gif_ref, gic_ref, grad_ref,
-    s_ref, do_ref, de_ref, c_ref, x_ref, xc_ref, lift_ref, mf_ref, mc_ref, scf_ref, scc_ref,
+    plan,
+    ext_ref, inp_ref, upf_ref, inc_ref, upc_ref,
+    wf_ref, wdo_ref, wde_ref, wdn_ref, wc01_ref, wc2_ref, wu_ref, vec_ref,
+    outf_ref, outc_ref, gif_ref, gic_ref, blocks_ref,
+    grad_ref, s_ref, do_ref, de_ref, c_ref, x_ref, xc_ref, lift_ref, mf_ref, mc_ref, scf_ref, scc_ref,
     gl_ref, glo_ref, back_ref, gp_ref, g_ref, row_ref, stage_ref, sem_ref,
 ):
     hh, ww = ext_ref[0, 0], ext_ref[0, 1]
+    gain_f = jnp.concatenate([vec_ref[0:1, :], vec_ref[1:2, :]], axis=1)
+    bias_f = jnp.concatenate([vec_ref[2:3, :], vec_ref[3:4, :]], axis=1)
+    gain_c, bias_c = vec_ref[4:5, :], vec_ref[5:6, :]
     pos = lax.broadcasted_iota(jnp.int32, (48, 128), 0)
     col = jnp.where(pos < 24, 2 * pos, 2 * pos - 47)
     colm = jnp.where(col < ww, 1.0, 0.0).astype(F32)
@@ -107,8 +114,8 @@
     xc_ref[...] = jnp.zeros((576, 128), F32)
     scf_ref[...] = jnp.zeros((8, 256), F32)
     scc_ref[...] = jnp.zeros((8, 128), F32)
-    scf_ref[1:2, :] = 0.5 * bf_ref[...]
-    scc_ref[1:2, :] = 0.5 * bc_ref[...]
+    scf_ref[1:2, :] = 0.5 * bias_f
+    scc_ref[1:2, :] = 0.5 * bias_c
 
     def coarse_branch():
         h = xc_ref[...] * scc_ref[0:1, :] + scc_ref[1:2, :]
@@ -200,8 +207,8 @@
 
         none = jnp.zeros((8, 256), F32)
         sums_f = lax.fori_loop(0, 48, stats, (none, none), unroll=4)
-        finish(*sums_f, C1 // GROUPS, nf, gf_ref[...], bf_ref[...], scf_ref)
-        finish(*sums_c, C2 // GROUPS, nc, gc_ref[...], bc_ref[...], scc_ref)
+        finish(*sums_f, C1 // GROUPS, nf, gain_f, bias_f, scf_ref)
+        finish(*sums_c, C2 // GROUPS, nc, gain_c, bias_c, scc_ref)
         return 0
 
     lax.fori_loop(0, ITERS, iterate, 0)
@@ -255,7 +262,7 @@
         grad_ref[pl.ds(ROW_DOWN + 3 + dx, 256, stride=9), :] = down_even[at]
         grad_ref[pl.ds(ROW_DOWN + 6 + dx, 256, stride=9), :] = down_odd[at, 0:128]
 
-    back_c = (seed_c + dot(gl_ref[...], wut_ref[...])) * mc_ref[...]
+    back_c = (seed_c + dot_lanes(gl_ref[...], wu_ref[...])) * mc_ref[...]
     gic_ref[...] = back_c
 
     def pre_grad(gi, x, scale, shift, mean, inv):
@@ -271,13 +278,13 @@
     gp_c, normed_c = pre_grad(
         back_c, xc_ref[...], scc_ref[0:1, :], scc_ref[1:2, :], scc_ref[2:3, :], scc_ref[3:4, :]
     )
-    gain_c = jnp.sum(gp_c * normed_c, axis=0, keepdims=True)
-    bias_c = jnp.sum(gp_c, axis=0, keepdims=True)
-    grad_ref[ROW_VEC + 4 : ROW_VEC + 5, :] = gain_c
-    grad_ref[ROW_VEC + 5 : ROW_VEC + 6, :] = bias_c
-    grad_ref[ROW_VEC + 6 : ROW_VEC + 8, :] = jnp.zeros((2, 128), F32)
-    mean_h, mean_hn = back_means(bias_c, gain_c, gc_ref[...], C2 // GROUPS, nc)
-    gconv_c = (gp_c * gc_ref[...] - mean_h - normed_c * mean_hn) * scc_ref[3:4, :] * mc_ref[...]
+    sum_gain = jnp.sum(gp_c * normed_c, axis=0, keepdims=True)
+    sum_bias = jnp.sum(gp_c, axis=0, keepdims=True)
+    grad_ref[ROW_VEC + 4 : ROW_VEC + 5, :] = sum_gain
+    grad_ref[ROW_VEC + 5 : ROW_VEC + 6, :] = sum_bias
+    grad_ref[FLAT_ROWS:, :] = jnp.zeros((plan.tall - FLAT_ROWS, 128), F32)
+    mean_h, mean_hn = back_means(sum_bias, sum_gain, gain_c, C2 // GROUPS, nc)
+    gconv_c = (gp_c * gain_c - mean_h - normed_c * mean_hn) * scc_ref[3:4, :] * mc_ref[...]
     around = jnp.concatenate(
         [
             jnp.concatenate([gconv_c[24:], none], axis=0),
@@ -293,11 +300,11 @@
                 128 * dx : 128 * dx + 128, 128 * dy : 128 * dy + 128
             ]
 
-    back_ref[0] = dot(glo_ref[:, 0:128], wdt_ref[0:128, :])
+    back_ref[0] = dot_lanes(glo_ref[:, 0:128], wdn_ref[:, 0:128])
     g00, g10, g01, g11 = (glo_ref[:, 128 * i : 128 * i + 128] for i in range(4))
-    back_ref[1] = dot(jnp.concatenate([g00, g01], axis=1), wdt_ref[128:384, :])
-    back_ref[2] = dot(jnp.concatenate([g00, g10], axis=1), wdt_ref[384:640, :])
-    back_ref[3] = dot(jnp.concatenate([g00, g01, g10, g11], axis=1), wdt_ref[640:1152, :])
+    back_ref[1] = dot_lanes(jnp.concatenate([g00, g01], axis=1), wdn_ref[:, 128:384])
+    back_ref[2] = dot_lanes(jnp.concatenate([g00, g10], axis=1), wdn_ref[:, 384:640])
+    back_ref[3] = dot_lanes(jnp.concatenate([g00, g01, g10, g11], axis=1), wdn_ref[:, 640:1152])
 
     def fine_back(i, carry):
         sums = list(carry)
@@ -318,17 +325,17 @@
         return tuple(sums)
 
     none8 = jnp.zeros((8, 256), F32)
-    gain_f, bias_f = lax.fori_loop(0, 24, fine_back, (none8, none8))
+    sum_gain, sum_bias = lax.fori_loop(0, 24, fine_back, (none8, none8))
     sends[2].start()
     sends[3].start()
-    gain_f = jnp.sum(gain_f, axis=0, keepdims=True)
-    bias_f = jnp.sum(bias_f, axis=0, keepdims=True)
+    sum_gain = jnp.sum(sum_gain, axis=0, keepdims=True)
+    sum_bias = jnp.sum(sum_bias, axis=0, keepdims=True)
     mean_h, mean_hn = [], []
     for p in range(2):
         at = slice(128 * p, 128 * p + 128)
-        grad_ref[ROW_VEC + p : ROW_VEC + p + 1, :] = gain_f[:, at]
-        grad_ref[ROW_VEC + 2 + p : ROW_VEC + 3 + p, :] = bias_f[:, at]
-        a, b = back_means(bias_f[:, at], gain_f[:, at], gf_ref[:, at], C1 // GROUPS, nf)
+        grad_ref[ROW_VEC + p : ROW_VEC + p + 1, :] = sum_gain[:, at]
+        grad_ref[ROW_VEC + 2 + p : ROW_VEC + 3 + p, :] = sum_bias[:, at]
+        a, b = back_means(sum_bias[:, at], sum_gain[:, at], gain_f[:, at], C1 // GROUPS, nf)
         mean_h.append(a)
         mean_hn.append(b)
     row_ref[0:1, :] = jnp.concatenate(mean_h, axis=1)
@@ -339,7 +346,7 @@
     def fine_conv_grad(r, _):
         at = rows_of(r, 48, 48)
         normed = (x_ref[at, :] - scf_ref[2:3, :]) * scf_ref[3:4, :]
-        g = (gp_ref[at, :] * gf_ref[...] - row_ref[0:1, :] - normed * row_ref[1:2, :]) * scf_ref[3:4, :]
+        g = (gp_ref[at, :] * gain_f - row_ref[0:1, :] - normed * row_ref[1:2, :]) * scf_ref[3:4, :]
         g_ref[pl.ds(pl.multiple_of(r * 48 + 48, 48), 48), :] = (g * twice(mf_ref[at, :])).astype(BF)
         return 0
 
@@ -350,24 +357,27 @@
             grad = dot_rows(states, g_ref[48 * (2 - dy) : 48 * (2 - dy) + 2304, :])
             for j in range(2):
                 grad_ref[pl.ds(2 * (3 * dy + dx) + j, 256, stride=18), :] = grad[:, 128 * j : 128 * j + 128]
+    for n, first in enumerate(plan.first):
+        blocks_ref[n] = grad_ref[first : first + plan.rows, :].astype(BF)
     for send in sends:
         send.wait()
 
 
-def layer_call(*args):
+def layer_call(plan, *args):
     whole = pl.BlockSpec(memory_space=pltpu.VMEM)
     return pl.pallas_call(
-        layer_kernel,
+        functools.partial(layer_kernel, plan),
         out_shape=[
             jax.ShapeDtypeStruct((PIX, 256), F32),
             jax.ShapeDtypeStruct((CPIX, 128), F32),
             jax.ShapeDtypeStruct((PIX, 256), F32),
             jax.ShapeDtypeStruct((CPIX, 128), F32),
-            jax.ShapeDtypeStruct((8328, 128), F32),
+            jax.ShapeDtypeStruct((plan.n, plan.rows, 128), BF),
         ],
-        in_specs=[pl.BlockSpec(memory_space=pltpu.SMEM)] + [whole] * 16,
+        in_specs=[pl.BlockSpec(memory_space=pltpu.SMEM)] + [whole] * 12,
         out_specs=[pl.BlockSpec(memory_space=pl.ANY), whole, pl.BlockSpec(memory_space=pl.ANY), whole, whole],
         scratch_shapes=[
+            pltpu.VMEM((plan.tall, 128), F32),
             pltpu.VMEM((2400, 768), BF),
             pltpu.VMEM((576, 768), BF),
             pltpu.VMEM((576, 768), BF),
@@ -393,65 +403,409 @@
     )(*args)
 
 
-def by_parity(x):
-    _, h, w, c = x.shape
-    return x.reshape(h, w // 2, 2, c).transpose(0, 2, 1, 3).reshape(h * w, c)
-
-
-def unpack(params):
-    layouts = ((C1, 9, C1), (C1, 9, C2), (C2, 9, C2), (C2, C1), (1, C1), (1, C1), (1, C2), (1, C2))
-    pieces = []
-    offset = 0
-    for layout in layouts:
-        length = 1
-        for size in layout:
-            length *= size
-        pieces.append(params[offset : offset + length].reshape(layout))
-        offset = offset + length
-    return pieces
-
-
-def weight_forms(params):
-    kf, kd, kc, ku, gf, bf, gc, bc = unpack(params)
-    wf = kf.transpose(1, 0, 2).reshape(9 * C1, C1)
-    kd = kd.transpose(1, 0, 2)
-    turned = kd.transpose(0, 2, 1)
-    wdt = jnp.concatenate([turned[t] for t in (4, 5, 3, 7, 1, 8, 6, 2, 0)], axis=0)
-    kd = kd.reshape(3, 3 * C1, C2)
-    kc = kc.transpose(1, 0, 2).reshape(3, 3 * C2, C2)
-    return (
-        wf,
-        jnp.concatenate([kd[0], kd[2]], axis=1),
-        kd[1],
-        wdt,
-        jnp.concatenate([kc[0], kc[1]], axis=1),
-        kc[2],
-        ku,
-        ku.T,
-        gf.astype(F32),
-        bf.astype(F32),
-        gc.astype(F32),
-        bc.astype(F32),
-    )
+class Plan:
+    def __init__(self, shards, length):
+        self.dims = {16: (4, 2, 2), 128: (4, 8, 4)}.get(shards, (shards, 1, 1))
+        self.n, self.length = shards, length
+        self.first = [s * length // 128 for s in range(shards)]
+        self.rows = -(-(length + 127) // 128)
+        self.rows = -(-self.rows // 32) * 32
+        self.part = self.rows // 2
+        self.cut = -(-self.part // 32) * 16
+        self.tall = -(-(self.first[-1] + self.rows) // 16) * 16
+
+    def here(self):
+        d0, d1, d2 = self.dims
+        me = lax.axis_index("fsdp")
+        return me, lax.axis_index("rep"), me // (d1 * d2), me // d2 % d1, me % d2
+
+    def block(self, a, b, c):
+        d0, d1, d2 = self.dims
+        return (a * d1 + b) * d2 + c
+
+
+def greet(plan, me, core, a, b, c):
+    d0, d1, d2 = plan.dims
+    barrier = pltpu.get_barrier_semaphore()
+    others = [plan.block((a + k) % d0, b, c) for k in range(1, d0)]
+    others += [plan.block(a, (b + k) % d1, c) for k in range(1, d1)]
+    others += [plan.block(a, b, (c + k) % d2) for k in range(1, d2)]
+    for other in others:
+        pl.semaphore_signal(barrier, inc=1, device_id={"fsdp": other, "rep": core}, device_id_type=pl.DeviceIdType.MESH)
+    pl.semaphore_signal(barrier, inc=1, device_id={"fsdp": me, "rep": 1 - core}, device_id_type=pl.DeviceIdType.MESH)
+    pl.semaphore_wait(barrier, len(others) + 1)
+
+
+def gather_kernel(plan, master_ref, inp_ref, upf_ref,
+                  inpo_ref, upfo_ref, wf_ref, wdo_ref, wde_ref, wdn_ref, wc01_ref, wc2_ref, wu_ref, vec_ref,
+                  g_ref, w_ref, tmp_ref, send_sem, recv_sem, sib_send, sib_recv, far_send):
+    d0, d1, d2 = plan.dims
+    me, core, a, b, c = plan.here()
+    part, cut = plan.part, plan.cut
+    off = (me * plan.length) % 128
+    x = master_ref[...]
+    x = pltpu.roll(x, off, 1)
+    row = lax.broadcasted_iota(jnp.int32, x.shape, 0)
+    lane = lax.broadcasted_iota(jnp.int32, x.shape, 1)
+    above = jnp.where(row == 0, 0.0, pltpu.roll(x, 1, 0))
+    g_ref[me] = jnp.where(lane < off, above, x).astype(BF)
+    greet(plan, me, core, a, b, c)
+
+    def span(half, which):
+        start = which * part + (cut if half == 1 else 0)
+        return pl.ds(pl.multiple_of(start, 16), part if half == 2 else (part - cut if half == 1 else cut))
+
+    def copy(block, half, fsdp, rep, send, recv, which=core):
+        at = g_ref.at[block, span(half, which)]
+        return pltpu.make_async_remote_copy(src_ref=at, dst_ref=at, send_sem=send, recv_sem=recv,
+            device_id={"fsdp": fsdp, "rep": rep}, device_id_type=pl.DeviceIdType.MESH)
+
+    def far(k):
+        return copy(me, 2, plan.block((a + d0 - k) % d0, b, c), core, far_send.at[k], recv_sem.at[me, 0])
+
+    def along1(block, half, k):
+        return copy(block, half, plan.block(a, (b + k) % d1, c), core, send_sem.at[block, half, k - 1], recv_sem.at[block, half])
+
+    def along2(block, half, k):
+        return copy(block, half, plan.block(a, b, (c + k) % d2), core, send_sem.at[block, half, d1 - 1 + k - 1], recv_sem.at[block, half])
+
+    def beside(block, half):
+        return copy(block, half, me, 1 - core, sib_send.at[block, half], sib_recv.at[block, half])
+
+    def arrive(block, half, send_to):
+        copy(block, half, me, core, far_send.at[0], recv_sem.at[block, half % 2]).wait_recv()
+
+    sent = []
+    def go(d):
+        d.start()
+        sent.append(d)
+
+    for k in range(1, d0):
+        go(far(k))
+
+    def own_column(k):
+        block = plan.block((a + k) % d0, b, c)
+        if k:
+            copy(block, 2, me, core, far_send.at[0], recv_sem.at[block, 0]).wait_recv()
+        for half in (0, 1):
+            for i in range(1, d2):
+                go(along2(block, half, i))
+            for i in range(1, d1):
+                go(along1(block, half, i))
+        if k:
+            for half in (0, 1):
+                go(beside(block, half))
+
+    def near(k):
+        a2 = (a + k) % d0
+        for i in range(1, d2):
+            block = plan.block(a2, b, (c + i) % d2)
+            arrive(block, 0, None)
+            for j in range(1, d1):
+                go(along1(block, 0, j))
+            go(beside(block, 0))
+        for i in range(1, d1):
+            block = plan.block(a2, (b + i) % d1, c)
+            arrive(block, 1, None)
+            for j in range(1, d2):
+                go(along2(block, 1, j))
+            go(beside(block, 1))
+        for i in range(1, d2):
+            block = plan.block(a2, b, (c + i) % d2)
+            arrive(block, 1, None)
+            go(beside(block, 1))
+        for i in range(1, d1):
+            block = plan.block(a2, (b + i) % d1, c)
+            arrive(block, 0, None)
+            go(beside(block, 0))
+
+    def diagonal(k):
+        a2 = (a + k) % d0
+        for i in range(1, d1):
+            for j in range(1, d2):
+                block = plan.block(a2, (b + i) % d1, (c + j) % d2)
+                for half in (0, 1):
+                    arrive(block, half, None)
+                    go(beside(block, half))
+
+    def parity(src, dst):
+        def one(r, _):
+            at = pl.ds(pl.multiple_of(r * 48, 48), 48)
+            v = src[at, :].astype(F32)
+            for p in range(2):
+                tmp_ref[p, at, :] = v[:, 128 * p:128 * p + 128]
+            even = [tmp_ref[p, pl.ds(r * 48, 24, stride=2), :] for p in range(2)]
+            odd = [tmp_ref[p, pl.ds(r * 48 + 1, 24, stride=2), :] for p in range(2)]
+            both = jnp.concatenate([jnp.concatenate(even, axis=1), jnp.concatenate(odd, axis=1)], axis=0)
+            dst[at, :] = both.astype(BF)
+            return 0
+        lax.fori_loop(0, 48, one, 0, unroll=4)
+
+    own_column(0)
+    parity(inp_ref, inpo_ref)
+    parity(upf_ref, upfo_ref)
+    for k in range(1, d0):
+        own_column(k)
+        near(k - 1)
+        if k > 1:
+            diagonal(k - 2)
+    near(d0 - 1)
+    if d0 > 1:
+        diagonal(d0 - 2)
+    diagonal(d0 - 1)
+    for k in range(1, plan.n):
+        block = (me + k) % plan.n
+        for half in (0, 1):
+            copy(block, half, me, core, far_send.at[0], sib_recv.at[block, half], which=1 - core).wait_recv()
+    for d in sent:
+        d.wait_send()
+
+    for s in range(plan.n):
+        v = g_ref[s].astype(F32)
+        at = plan.first[s]
+        if s:
+            low = w_ref[at:at + 1, :] + v[0:1]
+            w_ref[at:at + plan.rows, :] = v
+            w_ref[at:at + 1, :] = low
+        else:
+            w_ref[0:plan.rows, :] = v
+    for t in range(9):
+        for h in range(2):
+            wf_ref[256 * t:256 * t + 256, 128 * h:128 * h + 128] = w_ref[pl.ds(2 * t + h, 256, stride=18), :].astype(BF)
+        d = w_ref[pl.ds(ROW_DOWN + t, 256, stride=9), :].astype(BF)
+        dy, dx = t // 3, t % 3
+        if dy == 1:
+            wde_ref[256 * dx:256 * dx + 256, :] = d
+        else:
+            wdo_ref[256 * dx:256 * dx + 256, 64 * dy:64 * dy + 128] = d
+        p = (4, 5, 3, 7, 1, 8, 6, 2, 0).index(t)
+        wdn_ref[:, 128 * p:128 * p + 128] = d
+        e = w_ref[pl.ds(ROW_COARSE + t, 128, stride=9), :].astype(BF)
+        if dy < 2:
+            wc01_ref[128 * dx:128 * dx + 128, 128 * dy:128 * dy + 128] = e
+        else:
+            wc2_ref[128 * dx:128 * dx + 128, :] = e
+    for h in range(2):
+        wu_ref[:, 128 * h:128 * h + 128] = w_ref[pl.ds(ROW_UP + h, 128, stride=2), :].astype(BF)
+    vec_ref[...] = w_ref[ROW_VEC:ROW_VEC + 8, :]
+
+
+def gather_call(plan, master, inp, upf):
+    V = pl.BlockSpec(memory_space=pltpu.VMEM)
+    sh = lambda *s: jax.ShapeDtypeStruct(s, BF)
+    d0, d1, d2 = plan.dims
+    D = pltpu.SemaphoreType.DMA
+    return pl.pallas_call(functools.partial(gather_kernel, plan),
+        out_shape=[sh(PIX, 256), sh(PIX, 256), sh(2304, 256), sh(768, 256), sh(768, 128), sh(256, 1152), sh(384, 256), sh(384, 128), sh(128, 256),
+                   jax.ShapeDtypeStruct((8, 128), F32)],
+        in_specs=[V] * 3, out_specs=[V] * 10,
+        scratch_shapes=[pltpu.VMEM((plan.n, plan.rows, 128), BF), pltpu.VMEM((plan.tall, 128), F32), pltpu.VMEM((2, PIX, 128), F32),
+            D((plan.n, 2, max(d1 + d2 - 2, 1))), D((plan.n, 2)), D((plan.n, 2)), D((plan.n, 2)), D((d0,))],
+        compiler_params=pltpu.CompilerParams(collective_id=0, has_side_effects=True, vmem_limit_bytes=40 * 2**20),
+        name="gather_weights")(master, inp, upf)
+
+
+def reduce_kernel(plan, p_ref, out_ref, tile_ref,
+                  q_ref, ua_ref, ub_ref, va_ref, vb_ref, z_ref, sa_ref, total_ref, n1_ref, n2_ref,
+                  q_send, q_recv, s1_send, s1_recv, s2_send, s2_recv, s3_send, s3_recv, t_send, t_recv, n1_send, n1_recv, n2_send, n2_recv):
+    d0, d1, d2 = plan.dims
+    me, core, a, b, c = plan.here()
+    part, cut = plan.part, plan.cut
+    MESH = pl.DeviceIdType.MESH
+    barrier = pltpu.get_barrier_semaphore()
+    others = [({"fsdp": plan.block((a + k) % d0, b, c), "rep": core}) for k in range(1, d0)]
+    plane = []
+    for i in range(d1):
+        for j in range(d2):
+            for o in range(2):
+                if i or j or o:
+                    plane.append((i, j, o, {"fsdp": plan.block(a, (b + i) % d1, (c + j) % d2), "rep": (core + o) % 2}))
+    others += [p[3] for p in plane]
+    for other in others:
+        pl.semaphore_signal(barrier, inc=1, device_id=other, device_id_type=MESH)
+    pl.semaphore_wait(barrier, len(others))
+
+    sent = []
+    def go(src, dst, send, recv, to):
+        d = pltpu.make_async_remote_copy(src_ref=src, dst_ref=dst, send_sem=send, recv_sem=recv, device_id=to, device_id_type=MESH)
+        d.start()
+        sent.append(d)
+
+    def got(ref, recv):
+        pltpu.make_async_copy(ref, ref, recv).wait()
+
+    mine = pl.multiple_of(core * part, 16)
+    theirs = pl.multiple_of((1 - core) * part, 16)
+    halves = ((0, cut), (cut, part - cut))
+    order = [(k + 1) % d0 for k in range(d0)]
+    spots = []
+    for k in order:
+        for i in list(range(1, d1)) + [0]:
+            for j in list(range(1, d2)) + [0]:
+                spots.append((k, i, j))
+    for k, i, j in spots:
+        s = plan.block((a + k) % d0, (b + i) % d1, (c + j) % d2)
+        go(p_ref.at[s, pl.ds(theirs, part)], q_ref.at[s], q_send.at[s], q_recv.at[s], {"fsdp": me, "rep": 1 - core})
+
+    def pair(s, half):
+        start, size = halves[half]
+        x = p_ref[s, pl.ds(pl.multiple_of(mine + start, 16), size), :].astype(F32)
+        return x + q_ref[s, start:start + size, :].astype(F32)
+
+    def step1(k):
+        a2 = (a + k) % d0
+        for i in range(1, d1):
+            for j in list(range(1, d2)) + [0]:
+                s = plan.block(a2, (b + i) % d1, (c + j) % d2)
+                got(q_ref.at[s], q_recv.at[s])
+                sa_ref[s, 0:cut, :] = pair(s, 0).astype(BF)
+                go(sa_ref.at[s, 0:cut], ua_ref.at[a2, (c + j) % d2, i - 1], s1_send.at[s, 0], s1_recv.at[0, a2, (c + j) % d2, i - 1],
+                   {"fsdp": plan.block(a, (b + i) % d1, c), "rep": core})
+                if j:
+                    step1b(s, a2, i, j)
+        for j in range(1, d2):
+            s = plan.block(a2, b, (c + j) % d2)
+            got(q_ref.at[s], q_recv.at[s])
+            step1b(s, a2, 0, j)
+
+    def step1b(s, a2, i, j):
+        sa_ref[s, cut:part, :] = pair(s, 1).astype(BF)
+        go(sa_ref.at[s, cut:part], ub_ref.at[a2, (b + i) % d1, j - 1], s1_send.at[s, 1], s1_recv.at[1, a2, (b + i) % d1, j - 1],
+           {"fsdp": plan.block(a, b, (c + j) % d2), "rep": core})
+
+    def from1(half, a2, other):
+        ref = ua_ref if half == 0 else ub_ref
+        total = None
+        for i in range((d1 if half == 0 else d2) - 1):
+            got(ref.at[a2, other, i], s1_recv.at[half, a2, other, i])
+            v = ref[a2, other, i].astype(F32)
+            total = v if total is None else total + v
+        return total
+
+    def plus(x, y):
+        return x if y is None else x + y
+
+    def step2(k):
+        a2 = (a + k) % d0
+        for j in range(1, d2):
+            c2 = (c + j) % d2
+            s = plan.block(a2, b, c2)
+            sa_ref[s, 0:cut, :] = plus(pair(s, 0), from1(0, a2, c2)).astype(BF)
+            go(sa_ref.at[s, 0:cut], va_ref.at[a2, j - 1], s2_send.at[0, a2, j - 1], s2_recv.at[0, a2, j - 1],
+               {"fsdp": plan.block(a, b, c2), "rep": core})
+        for i in range(1, d1):
+            b2 = (b + i) % d1
+            s = plan.block(a2, b2, c)
+            sa_ref[s, cut:part, :] = plus(pair(s, 1), from1(1, a2, b2)).astype(BF)
+            go(sa_ref.at[s, cut:part], vb_ref.at[a2, i - 1], s2_send.at[1, a2, i - 1], s2_recv.at[1, a2, i - 1],
+               {"fsdp": plan.block(a, b2, c), "rep": core})
+
+    def column(k):
+        a2 = (a + k) % d0
+        s = plan.block(a2, b, c)
+        got(q_ref.at[s], q_recv.at[s])
+        x = plus(pair(s, 0), from1(0, a2, c))
+        for j in range(1, d2):
+            got(va_ref.at[a2, j - 1], s2_recv.at[0, a2, j - 1])
+            x = x + va_ref[a2, j - 1].astype(F32)
+        y = plus(pair(s, 1), from1(1, a2, b))
+        for i in range(1, d1):
+            got(vb_ref.at[a2, i - 1], s2_recv.at[1, a2, i - 1])
+            y = y + vb_ref[a2, i - 1].astype(F32)
+        return s, x, y
+
+    def step3(k):
+        s, x, y = column(k)
+        sa_ref[s, 0:cut, :] = x.astype(BF)
+        sa_ref[s, cut:part, :] = y.astype(BF)
+        go(sa_ref.at[s], z_ref.at[k - 1], s3_send.at[k - 1], s3_recv.at[k - 1], {"fsdp": plan.block((a + k) % d0, b, c), "rep": core})
+
+    for n in range(d0 + 2):
+        if n < d0:
+            step1(order[n])
+        if 0 <= n - 1 < d0:
+            step2(order[n - 1])
+        if 0 <= n - 2 < d0 - 1:
+            step3(order[n - 2])
+    _, x, y = column(0)
+    total = jnp.concatenate([x, y], axis=0)
+    for k in range(1, d0):
+        got(z_ref.at[k - 1], s3_recv.at[k - 1])
+        total = total + z_ref[k - 1].astype(F32)
+    total_ref[pl.ds(mine, part), :] = total
+    go(total_ref.at[pl.ds(mine, part)], total_ref.at[pl.ds(mine, part)], t_send.at[0], t_recv.at[0], {"fsdp": me, "rep": 1 - core})
+
+    off = (me * plan.length) % 128
+    row = lax.broadcasted_iota(jnp.int32, (part, 128), 0) + mine
+    at = row * 128 + lax.broadcasted_iota(jnp.int32, (part, 128), 1)
+    own = jnp.where((at >= off) & (at < off + plan.length), total, 0.0)
+    last = me == plan.n - 1
+    for i in range(6):
+        spot = ROW_VEC - plan.first[-1] + i
+        holds = last & (core == spot // part)
+        n1_ref[a, i:i + 1, :] = jnp.where(holds, total[spot % part:spot % part + 1], 0.0)
+    n1_ref[a, 6:7, :] = jnp.sum(own * own, axis=0, keepdims=True)
+    n1_ref[a, 7:8, :] = jnp.zeros((1, 128), F32)
+    for k in range(1, d0):
+        go(n1_ref.at[a], n1_ref.at[a], n1_send.at[k], n1_recv.at[a], {"fsdp": plan.block((a + k) % d0, b, c), "rep": core})
+    for k in range(1, d0):
+        got(n1_ref.at[(a + k) % d0], n1_recv.at[(a + k) % d0])
+    tile = n1_ref[0]
+    for k in range(1, d0):
+        tile = tile + n1_ref[k]
+    slot = (b * d2 + c) * 2 + core
+    n2_ref[slot] = tile
+    for n, (i, j, o, to) in enumerate(plane):
+        go(n2_ref.at[slot], n2_ref.at[slot], n2_send.at[n], n2_recv.at[slot], to)
+    got(total_ref.at[pl.ds(theirs, part)], t_recv.at[0])
+    x = pltpu.roll(total_ref[...], (128 - off) % 128, 1)
+    below = pltpu.roll(x, plan.rows - 1, 0)
+    lane = lax.broadcasted_iota(jnp.int32, x.shape, 1)
+    out_ref[...] = jnp.where(lane + off >= 128, below, x)
+    for n, (i, j, o, to) in enumerate(plane):
+        other = (((b + i) % d1) * d2 + (c + j) % d2) * 2 + (core + o) % 2
+        got(n2_ref.at[other], n2_recv.at[other])
+    tile = n2_ref[0]
+    for n in range(1, 2 * d1 * d2):
+        tile = tile + n2_ref[n]
+    tile_ref[...] = tile
+    for d in sent:
+        d.wait_send()
+
+
+def reduce_call(plan, grads):
+    V = pl.BlockSpec(memory_space=pltpu.VMEM)
+    d0, d1, d2 = plan.dims
+    D = pltpu.SemaphoreType.DMA
+    b = lambda *s: pltpu.VMEM(s, BF)
+    e1, e2 = max(d1 - 1, 1), max(d2 - 1, 1)
+    return pl.pallas_call(functools.partial(reduce_kernel, plan),
+        out_shape=[jax.ShapeDtypeStruct((plan.rows, 128), F32), jax.ShapeDtypeStruct((8, 128), F32)],
+        in_specs=[V], out_specs=[V] * 2,
+        scratch_shapes=[b(plan.n, plan.part, 128), b(d0, d2, e1, plan.cut, 128), b(d0, d1, e2, plan.part - plan.cut, 128),
+            b(d0, e2, plan.cut, 128), b(d0, e1, plan.part - plan.cut, 128), b(max(d0 - 1, 1), plan.part, 128), b(plan.n, plan.part, 128),
+            pltpu.VMEM((plan.rows, 128), F32), pltpu.VMEM((d0, 8, 128), F32), pltpu.VMEM((2 * d1 * d2, 8, 128), F32),
+            D((plan.n,)), D((plan.n,)), D((plan.n, 2)), D((2, d0, max(d1, d2), max(e1, e2))), D((2, d0, max(e1, e2))), D((2, d0, max(e1, e2))),
+            D((d0,)), D((d0,)), D((1,)), D((1,)), D((d0,)), D((d0,)), D((2 * d1 * d2,)), D((2 * d1 * d2,))],
+        compiler_params=pltpu.CompilerParams(collective_id=1, has_side_effects=True, vmem_limit_bytes=40 * 2**20),
+        name="reduce_gradients")(grads)
 
 
 def per_device(
     input_fine, input_coarse, upstream_fine, upstream_coarse, extents, master, first_moment, second_moment, average
 ):
-    resident = lax.all_gather(master.astype(BF), "fsdp", axis=0, tiled=True)
-    out_fine, out_coarse, gi_fine, gi_coarse, grad = layer_call(
-        extents,
-        by_parity(input_fine),
-        input_coarse.reshape(CPIX, C2),
-        by_parity(upstream_fine),
-        upstream_coarse.reshape(CPIX, C2),
-        *weight_forms(resident),
+    plan = Plan(lax.axis_size("fsdp"), master.shape[0])
+    padded = jnp.pad(master, (0, plan.rows * 128 - plan.length)).reshape(plan.rows, 128)
+    inp, upf, *weights = gather_call(
+        plan, padded, input_fine.reshape(PIX, C1), upstream_fine.reshape(PIX, C1)
     )
-    flat_grad = grad[:FLAT_ROWS].reshape(-1)
-    small_total = lax.psum(flat_grad[-2 * (C1 + C2) :], ("fsdp", "rep"))
-    shard_grad = lax.psum_scatter(flat_grad, "fsdp", scatter_dimension=0, tiled=True)
-    shard_grad = lax.psum(shard_grad.astype(BF), "rep").astype(F32)
-    total_square = lax.psum(jnp.sum(shard_grad * shard_grad), "fsdp")
+    out_fine, out_coarse, gi_fine, gi_coarse, blocks = layer_call(
+        plan, extents, inp, upf, input_coarse.reshape(CPIX, C2), upstream_coarse.reshape(CPIX, C2), *weights
+    )
+    shard_grad, tile = reduce_call(plan, blocks)
+    shard_grad = shard_grad.reshape(-1)[: plan.length]
+    total_square = jnp.sum(tile[6])
+    small_total = tile[:6].reshape(-1)
     grad_norm = jnp.sqrt(total_square)
     factor = jnp.minimum(1.0, clip_norm / (grad_norm + 1e-06))
     clipped = shard_grad * factor

time: 555 us -> 159 us (0.29)
  blocking collectives: 271 us -> 0 us
  waiting for transfers between devices: 145 us -> 0 us
  Pallas kernels: 89.8 us -> 140 us
  between operations: 17.5 us -> 2.58 us
  local copies, waits for them, and re-layouts: 24 us -> 13.1 us
    unnamed x1 -> x0, blocking collectives: 189 us -> none
    unnamed x3 -> x0, waiting for transfers between devices: 127 us -> none
    psum x2 -> x0, blocking collectives: 81.7 us -> none  [the longest x1 41.1 us: per_device(): total_square = lax.psum(jnp.sum(shard_grad * shard_grad), 'fsdp')]
    pallas_call x1 -> x3, Pallas kernels: 89.8 us -> 140 us  [the longest x1 89.3 us: layer_call(): pl.pallas_call(functools.partial(layer_kernel, plan), out_shape=[jax.Shap...]
    psum x1 -> x0, waiting for transfers between devices: 17.9 us -> none  [per_device(): shard_grad = lax.psum(shard_grad.astype(BF), 'rep').astype(F32)]
    reshape x9 -> x1, local copies, waits for them, and re-layouts: 8.91 us -> 0.97 us  [per_device(): jnp.pad(master, (0, plan.rows * 128 - plan.length)).reshape(plan.rows, 128)]
    slice x17 -> x0, local copies, waits for them, and re-layouts: 7.18 us -> none  [the longest x8 2.58 us: unpack(): pieces.append(params[offset:offset + length].reshape(layout))]
    unnamed x38 -> x34, local copies, waits for them, and re-layouts: 6.46 us -> 12.1 us
  transfers between devices with their start and end apart: 2 -> 0, of which waited for: 2 -> 0; matrix products, arithmetic and copies ran while one was open for 1% -> 0% of each run, Pallas kernels for 0% -> 0%
where the time goes in v2:
time: 159 us; the launch traced here: 158 us
  Pallas kernels  140 us (88%)
  local copies, waits for them, and re-layouts  13.1 us (8%)
  between operations  2.58 us (2%)
  other arithmetic  2.34 us (1%)
    pallas_call x1, Pallas kernels, layer_call(): pl.pallas_call(functools.partial(layer_kernel, plan), out_shape=[jax.Shap...  89.3 us
    pallas_call x1, Pallas kernels, reduce_call(): pl.pallas_call(functools.partial(reduce_kernel, plan), out_shape=[jax.Sha...  27.6 us
    pallas_call x1, Pallas kernels, gather_call(): pl.pallas_call(functools.partial(gather_kernel, plan), out_shape=[sh(PIX,...  23.5 us
    unnamed x34, local copies, waits for them, and re-layouts  12.1 us

profile of v2, /device:TPU:0, one launch (start us, length us, event | category | flops | bytes accessed | tf_op | source)
XLA Modules:
  0.0 158.4 jit_solution(8562352695409779689)
XLA Ops:
  0.6 1.0 pad_bitcast_fusion.master_ref
  1.6 0.0 copy-start.1
  1.6 1.3 copy-done.1
  2.9 1.3 copy-done.2
  4.2 23.5 %gather_weights.1 = (bf16[2304,256]{1,0:T(8,128)(2,1)S(1)}, bf16[2304,256]{1,0:T(8,128)(2,1)S(1)}, bf16[2304,256]{1,0:T(8,128)(2,1)S(1)}, bf16[768,256]{1,0:T(8,...) custom-call(f32[544,128]{1,0:T(8,128)S(1)} %pad_bitcast_fusion.maste, ...), custom_call_target="tpu_custom_call" | custom-call | tf_op jit(solution)/shard_map/gather_weights/pallas_call | solution.py:598
  27.6 0.0 copy-start.3
  27.7 1.0 copy-done.3
  28.7 1.0 copy-done.4
  29.7 1.1 copy-done.5
  30.8 0.8 copy-done.6
  31.6 0.7 copy-done.7
  32.4 0.7 copy-done.8
  33.0 0.7 copy-done.9
  33.7 0.6 copy-done.10
  34.4 0.6 copy-done.11
  35.0 0.6 copy-done.12
  35.6 89.3 %layer.1 = (f32[2304,256]{1,0:T(8,128)}, f32[576,128]{1,0:T(8,128)}, f32[2304,256]{1,0:T(8,128)}, f32[576,128]{1,0:T(8,128)}, bf16[16,544,128]{2,1,0:T(8,128)(2,1)}) custom-call(s32[1,2]{1,0:T(1,128)} %ext_ref.1, bf16[2304,256]{1,0:T(8,128)(2,1)} %copy-done.3, bf16[2304,256]{1,0:T(8,128)(2,1)} %copy-done.4, bf16[576,128]{1,0:T(8,128)(2,1)} %bitcast.16, ...), custom_call_target="tpu_custom_call" | custom-call | tf_op jit(solution)/shard_map/layer/pallas_call | solution.py:368
  124.9 0.0 copy-start
  124.9 1.6 %copy-done = bf16[16,544,128]{2,1,0:T(8,128)(2,1)S(1)} copy-done((bf16[16,544,128]{2,1,0:T(8,128)(2,1)S(1)}, bf16[16,544,128]{2,1,0:T(8,128)(2,1)}, u32[]{:S(2)}) %copy-start) | copy-done | bytes 2228248
  126.5 27.6 %reduce_gradients.1 = (f32[544,128]{1,0:T(8,128)S(1)}, f32[8,128]{1,0:T(8,128)S(1)}) custom-call(bf16[16,544,128]{2,1,0:T(8,128)(2,1)S(1)} %copy-done), custom_call_target="tpu_custom_call" | custom-call | tf_op jit(solution)/shard_map/reduce_gradients/pallas_call | solution.py:782
  154.2 0.6 slice_reduce_fusion
  155.5 0.6 multiply_bitcast_fusion
  156.1 0.0 copy-done.13
  156.1 1.1 multiply_add_fusion
  (17 shorter events, 0.0 us)
Async XLA Ops:
  1.6 1.3 copy-start.1
  2.9 1.3 copy-start.2
  27.6 1.0 copy-start.3
  28.7 1.0 copy-start.4
  29.7 1.1 copy-start.5
  30.8 0.8 copy-start.6
  31.6 0.7 copy-start.7
  32.4 0.7 copy-start.8
  33.0 0.7 copy-start.9
  33.7 0.6 copy-start.10
  34.3 0.6 copy-start.11
  35.0 0.6 copy-start.12
  35.6 120.5 %copy-start.13 = (f32[66608]{0:T(1024)S(1)}, f32[66608]{0:T(1024)}, u32[]{:S(2)}) copy-start(f32[66608]{0:T(1024)} %param.14) | copy-start | bytes 799300
  35.6 120.5 %copy-start.14 = (f32[66608]{0:T(1024)S(1)}, f32[66608]{0:T(1024)}, u32[]{:S(2)}) copy-start(f32[66608]{0:T(1024)} %param.17) | copy-start | bytes 799300
  35.6 120.5 %copy-start.15 = (f32[66608]{0:T(1024)S(1)}, f32[66608]{0:T(1024)}, u32[]{:S(2)}) copy-start(f32[66608]{0:T(1024)} %param.15) | copy-start | bytes 799300
  35.6 120.5 %copy-start.16 = (f32[66608]{0:T(1024)S(1)}, f32[66608]{0:T(1024)}, u32[]{:S(2)}) copy-start(f32[66608]{0:T(1024)} %param.16) | copy-start | bytes 799300
  124.9 1.6 %copy-start = (bf16[16,544,128]{2,1,0:T(8,128)(2,1)S(1)}, bf16[16,544,128]{2,1,0:T(8,128)(2,1)}, u32[]{:S(2)}) copy-start(bf16[16,544,128]{2,1,0:T(8,128)(2,1)} %get-tuple-element.41.p_ref) | copy-start | bytes 6684676

commit v3 on v2

v3 whole, which is shorter than its diff:
```python
import functools

import jax
import jax.numpy as jnp
from jax import lax
from jax.experimental import pallas as pl
from jax.experimental.pallas import tpu as pltpu
from jax.sharding import PartitionSpec as P

F32, BF = jnp.float32, jnp.bfloat16
C1, C2, GROUPS, ITERS, STEP = 256, 128, 8, 12, 10
HEIGHT, HALF = 48, 24
PIX, CPIX = HEIGHT * HEIGHT, HALF * HALF
FLAT_ROWS = 8326
ROW_DOWN, ROW_COARSE, ROW_UP, ROW_VEC = 4608, 6912, 8064, 8320

clip_norm = 1.0
learn_rate = 0.02
beta_one = 0.9
beta_two = 0.999
adam_eps = 1e-08
decay_rate = 0.1


def dot(a, b):
    return jnp.dot(a, b, preferred_element_type=F32)


def dot_rows(a, b):
    return lax.dot_general(a, b, (((0,), (0,)), ((), ())), preferred_element_type=F32)


def dot_lanes(a, b):
    return lax.dot_general(a, b, (((1,), (1,)), ((), ())), preferred_element_type=F32)


def run_sum(x, width):
    lane = lax.broadcasted_iota(jnp.int32, x.shape, 1)
    step = 1
    while step < width:
        up = pltpu.roll(x, 128 - step, 1)
        down = pltpu.roll(x, step, 1)
        x = x + jnp.where((lane & step) == 0, up, down)
        step *= 2
    return x


def shift_down(x):
    count = x.shape[0] // 8
    top = lax.broadcasted_iota(jnp.int32, (8, x.shape[1]), 0) == 0
    turned = [pltpu.roll(x[8 * i : 8 * i + 8], 1, 0) for i in range(count)]
    return jnp.concatenate(
        [jnp.where(top, turned[i - 1] if i else 0.0, turned[i]) for i in range(count)], axis=0
    )


def shift_up(x):
    count = x.shape[0] // 8
    end = lax.broadcasted_iota(jnp.int32, (8, x.shape[1]), 0) == 7
    turned = [pltpu.roll(x[8 * i : 8 * i + 8], 7, 0) for i in range(count)]
    return jnp.concatenate(
        [jnp.where(end, turned[i + 1] if i < count - 1 else 0.0, turned[i]) for i in range(count)], axis=0
    )


def in_rows(x, change):
    return jnp.concatenate([change(x[24 * r : 24 * r + 24]) for r in range(24)], axis=0)


def row_down(x):
    return jnp.concatenate([jnp.zeros((24, x.shape[1]), F32), x[:552]], axis=0)


def row_up(x):
    return jnp.concatenate([x[24:], jnp.zeros((24, x.shape[1]), F32)], axis=0)


def tile_sum(x):
    total = x[0:8]
    for i in range(1, x.shape[0] // 8):
        total = total + x[8 * i : 8 * i + 8]
    return total


def twice(m):
    return jnp.concatenate([m, m], axis=1)


def interleave(ref, r, even, odd):
    for p in range(2):
        at = slice(128 * p, 128 * p + 128)
        ref[p, pl.ds(r * 48, 24, stride=2), :] = even[:, at]
        ref[p, pl.ds(r * 48 + 1, 24, stride=2), :] = odd[:, at]


def rows_of(r, count, unit):
    start = r * unit
    return pl.ds(start if isinstance(r, int) else pl.multiple_of(start, unit if unit % 16 == 0 else 8), count)


def layer_kernel(
    plan,
    ext_ref, vec_ref, inp_hbm, inc_hbm, wu_hbm, wdn_hbm, wc6_hbm, wf_hbm, upf_hbm, upc_hbm,
    outf_ref, outc_ref, gif_ref, gic_ref, blocks_ref,
    inp_ref, inc_ref, wu_ref, wdn_ref, wc6_ref, wf_ref, upf_ref, upc_ref,
    grad_ref, block_ref, s_ref, ph_ref, c_ref, x_ref, xc_ref, lift_ref, mf_ref, mc_ref, scf_ref, scc_ref,
    gl_ref, glo_ref, back_ref, gp_ref, g_ref, row_ref, stage_ref, small_ref, in_sem, out_sem, block_sem, small_sem,
):
    loads = [
        pltpu.make_async_copy(src, dst, in_sem.at[n])
        for n, (src, dst) in enumerate(
            (
                (inp_hbm, inp_ref), (inc_hbm, inc_ref), (wu_hbm, wu_ref), (wdn_hbm, wdn_ref),
                (wc6_hbm, wc6_ref), (wf_hbm, wf_ref), (upf_hbm, upf_ref), (upc_hbm, upc_ref),
            )
        )
    ]
    for load in loads:
        load.start()
    hh, ww = ext_ref[0, 0], ext_ref[0, 1]
    gain_f = jnp.concatenate([vec_ref[0:1, :], vec_ref[1:2, :]], axis=1)
    bias_f = jnp.concatenate([vec_ref[2:3, :], vec_ref[3:4, :]], axis=1)
    gain_c, bias_c = vec_ref[4:5, :], vec_ref[5:6, :]
    pos = lax.broadcasted_iota(jnp.int32, (48, 128), 0)
    col = jnp.where(pos < 24, 2 * pos, 2 * pos - 47)
    colm = jnp.where(col < ww, 1.0, 0.0).astype(F32)

    def setup(r, _):
        at = rows_of(r, 48, 48)
        mf_ref[at, :] = jnp.where(r < hh, colm, 0.0)
        x_ref[at, :] = jnp.zeros((48, 256), F32)
        return 0

    lax.fori_loop(0, 48, setup, 0)

    def setup_coarse(r, _):
        mc_ref[rows_of(r, 24, 24), :] = jnp.where(2 * r < hh, colm[0:24], 0.0)
        return 0

    lax.fori_loop(0, 24, setup_coarse, 0)
    nf = (hh * ww).astype(F32) * (C1 // GROUPS)
    nc = (((hh + 1) // 2) * ((ww + 1) // 2)).astype(F32) * (C2 // GROUPS)
    s_ref[0:48, :] = jnp.zeros((48, 768), BF)
    s_ref[49 * 48 : 50 * 48, :] = jnp.zeros((48, 768), BF)
    g_ref[0:48, :] = jnp.zeros((48, 256), BF)
    g_ref[49 * 48 : 50 * 48, :] = jnp.zeros((48, 256), BF)
    grad_ref[FLAT_ROWS:, :] = jnp.zeros((plan.tall - FLAT_ROWS, 128), F32)
    xc_ref[...] = jnp.zeros((576, 128), F32)
    scf_ref[...] = jnp.zeros((8, 256), F32)
    scc_ref[...] = jnp.zeros((8, 128), F32)
    scf_ref[1:2, :] = 0.5 * bias_f
    scc_ref[1:2, :] = 0.5 * bias_c
    for load in loads[:6]:
        load.wait()

    def coarse_branch():
        h = xc_ref[...] * scc_ref[0:1, :] + scc_ref[1:2, :]
        y = h * jnp.tanh(h) + h
        branch = ((y + inc_ref[...].astype(F32)) * mc_ref[...]).astype(BF)
        lift_ref[...] = dot(branch, wu_ref[...])
        return branch

    def fine_rows(g, final):
        scale, shift = scf_ref[0:1, :], scf_ref[1:2, :]
        pieces = ([], [])
        for j in range(4):
            r = 4 * g + j
            at = rows_of(r, 48, 48)
            m = twice(mf_ref[at, :])
            h = x_ref[at, :] * scale + shift
            y = h * jnp.tanh(h) + h
            lift = lift_ref[rows_of(2 * g + j // 2, 24, 24), :]
            lift = jnp.concatenate([lift, lift], axis=0)
            if final:
                low = ((y + inp_ref[at, :].astype(F32)) * m).astype(BF)
                branch = low.astype(F32)
                z = (branch + lift) * m
                interleave(stage_ref.at[0], r, z[0:24], z[24:48])
            else:
                m = m.astype(BF)
                low = (y.astype(BF) + inp_ref[at, :]) * m
                branch = low.astype(F32)
                z = ((low + lift.astype(BF)) * m).astype(F32)
                even, odd = z[0:24], z[24:48]
                to = rows_of(r + 1, 48, 48)
                s_ref[to, 0:256] = jnp.concatenate([shift_down(odd), even], axis=0).astype(BF)
                s_ref[to, 256:512] = z.astype(BF)
                s_ref[to, 512:768] = jnp.concatenate([odd, shift_up(even)], axis=0).astype(BF)
            pieces[j % 2].append(branch)
        at = rows_of(g, 48, 48)
        for i, (above, below) in enumerate(pieces):
            ph_ref[2 * i, at, :] = jnp.concatenate([above[0:24], below[0:24]], axis=0).astype(BF)
            ph_ref[2 * i + 1, at, :] = jnp.concatenate([above[24:48], below[24:48]], axis=0).astype(BF)

    def lowered():
        ee, eo, oe, oo = (ph_ref[i] for i in range(4))
        p = dot(eo, wdn_ref[:, 128:384]) + dot(oo, wdn_ref[:, 640:896])
        q = dot(oe, wdn_ref[:, 384:640])
        t = dot(oo, wdn_ref[:, 896:1152])
        here = p[:, :128] + q[:, :128] + dot(ee, wdn_ref[:, 0:128])
        return here + row_down(q[:, 128:] + t[:, :128]) + in_rows(p[:, 128:] + row_down(t[:, 128:]), shift_down)

    def coarse_step(branch):
        zc = (branch.astype(F32) + lowered()) * mc_ref[...]
        c_ref[:, 0:128] = in_rows(zc, shift_down).astype(BF)
        c_ref[:, 128:256] = zc.astype(BF)
        p = dot(c_ref[...], wc6_ref[...])
        t = [p[:, 128 * i : 128 * i + 128] for i in range(6)]
        xc = row_down(t[0]) + t[1] + row_up(t[2]) + in_rows(row_down(t[3]) + t[4] + row_up(t[5]), shift_up)
        xc_ref[...] = xc
        xm = xc * mc_ref[...]
        return tile_sum(xm), tile_sum(xm * xm)

    def conv_rows(first, last):
        total = None
        for dy in range(3):
            p = dot(s_ref[48 * (first + dy) : 48 * (last + dy), :], wf_ref[768 * dy : 768 * dy + 768, :])
            total = p if total is None else total + p
        x_ref[48 * first : 48 * last, :] = total
        xm = total * twice(mf_ref[48 * first : 48 * last, :])
        return tile_sum(xm), tile_sum(xm * xm)

    def finish(s, q, width, n, gain, bias, to_ref):
        s, q = jnp.sum(s, axis=0, keepdims=True), jnp.sum(q, axis=0, keepdims=True)
        for p in range(s.shape[1] // 128):
            at = slice(128 * p, 128 * p + 128)
            mean = run_sum(s[:, at], width) / n
            var = jnp.maximum(run_sum(q[:, at], width) / n - mean * mean, 0.0)
            inv = lax.rsqrt(var + 1e-5)
            to_ref[0:1, at] = 0.5 * inv * gain[:, at]
            to_ref[1:2, at] = 0.5 * (bias[:, at] - mean * inv * gain[:, at])
            to_ref[2:3, at] = mean
            to_ref[3:4, at] = inv

    def iterate(t, _):
        branch_c = coarse_branch()
        s = q = None
        for g in range(12):
            fine_rows(g, False)
            ds, dq = conv_rows(4 * g - 1 if g else 0, 4 * g + 3 if g < 11 else 48)
            s, q = (ds, dq) if s is None else (s + ds, q + dq)
        sums_c = coarse_step(branch_c)
        finish(s, q, C1 // GROUPS, nf, gain_f, bias_f, scf_ref)
        finish(*sums_c, C2 // GROUPS, nc, gain_c, bias_c, scc_ref)
        return 0

    lax.fori_loop(0, ITERS, iterate, 0)
    branch_c = coarse_branch()

    def fine_last(g, _):
        fine_rows(g, True)
        return 0

    lax.fori_loop(0, 12, fine_last, 0, unroll=2)
    sends = [
        pltpu.make_async_copy(stage_ref.at[i, p], ref.at[:, 128 * p : 128 * p + 128], out_sem.at[i, p])
        for i, ref in enumerate((outf_ref, gif_ref))
        for p in range(2)
    ]
    sends += [
        pltpu.make_async_copy(small_ref.at[i], ref, small_sem.at[i]) for i, ref in enumerate((outc_ref, gic_ref))
    ]
    sends[0].start()
    sends[1].start()
    small_ref[0] = (branch_c.astype(F32) + lowered()) * mc_ref[...]
    sends[4].start()
    for load in loads[6:]:
        load.wait()

    seed_c = upc_ref[...].astype(F32) * mc_ref[...]
    right = in_rows(seed_c, shift_up)
    glo_ref[:, 0:128] = seed_c.astype(BF)
    glo_ref[:, 128:256] = right.astype(BF)
    glo_ref[:, 256:384] = row_up(seed_c).astype(BF)
    glo_ref[:, 384:512] = row_up(right).astype(BF)

    def fold(g, _):
        both = []
        for i in range(2):
            total = None
            for j in range(2):
                at = rows_of(4 * g + 2 * i + j, 48, 48)
                seed = upf_ref[at, :].astype(F32) * twice(mf_ref[at, :])
                part = seed[0:24] + seed[24:48]
                total = part if total is None else total + part
            both.append(total)
        gl_ref[rows_of(g, 48, 48), :] = jnp.concatenate(both, axis=0).astype(BF)
        return 0

    lax.fori_loop(0, 12, fold, 0, unroll=2)
    up_grad = dot_rows(branch_c, gl_ref[...])
    for j in range(2):
        grad_ref[pl.ds(ROW_UP + j, 128, stride=2), :] = up_grad[:, 128 * j : 128 * j + 128]
    g00, g01, g10, g11 = (glo_ref[:, 128 * i : 128 * i + 128] for i in range(4))
    for i, (parts, taps) in enumerate(
        (((g00,), (4,)), ((g00, g01), (5, 3)), ((g00, g10), (7, 1)), ((g00, g01, g10, g11), (8, 6, 2, 0)))
    ):
        down = dot_rows(ph_ref[i], jnp.concatenate(parts, axis=1))
        for n, tap in enumerate(taps):
            grad_ref[pl.ds(ROW_DOWN + tap, 256, stride=9), :] = down[:, 128 * n : 128 * n + 128]

    back_c = (seed_c + dot_lanes(gl_ref[...], wu_ref[...])) * mc_ref[...]
    small_ref[1] = back_c
    sends[5].start()

    def pre_grad(gi, x, scale, shift, mean, inv):
        h = x * scale + shift
        t = jnp.tanh(h)
        sig = 0.5 * t + 0.5
        normed = (x - mean) * inv
        return gi * sig * (1.0 + 2.0 * h * (1.0 - sig)), normed

    def back_means(sum_bias, sum_gain, gain, width, n):
        return run_sum(sum_bias * gain, width) / n, run_sum(sum_gain * gain, width) / n

    gp_c, normed_c = pre_grad(
        back_c, xc_ref[...], scc_ref[0:1, :], scc_ref[1:2, :], scc_ref[2:3, :], scc_ref[3:4, :]
    )
    sum_gain = jnp.sum(gp_c * normed_c, axis=0, keepdims=True)
    sum_bias = jnp.sum(gp_c, axis=0, keepdims=True)
    grad_ref[ROW_VEC + 4 : ROW_VEC + 5, :] = sum_gain
    grad_ref[ROW_VEC + 5 : ROW_VEC + 6, :] = sum_bias
    mean_h, mean_hn = back_means(sum_bias, sum_gain, gain_c, C2 // GROUPS, nc)
    gconv = (gp_c * gain_c - mean_h - normed_c * mean_hn) * scc_ref[3:4, :] * mc_ref[...]
    around = jnp.concatenate([row_up(gconv), gconv, row_down(gconv)], axis=1)
    pair = dot_rows(c_ref[...], around.astype(BF))
    single = dot_rows(c_ref[:, 128:256], in_rows(around, shift_down).astype(BF))
    for dy in range(3):
        at = slice(128 * dy, 128 * dy + 128)
        grad_ref[pl.ds(ROW_COARSE + 3 * dy, 128, stride=9), :] = pair[0:128, at]
        grad_ref[pl.ds(ROW_COARSE + 3 * dy + 1, 128, stride=9), :] = pair[128:256, at]
        grad_ref[pl.ds(ROW_COARSE + 3 * dy + 2, 128, stride=9), :] = single[:, at]

    back_ref[0] = dot_lanes(g00, wdn_ref[:, 0:128])
    back_ref[1] = dot_lanes(jnp.concatenate([g00, g01], axis=1), wdn_ref[:, 128:384])
    back_ref[2] = dot_lanes(jnp.concatenate([g00, g10], axis=1), wdn_ref[:, 384:640])
    back_ref[3] = dot_lanes(glo_ref[...], wdn_ref[:, 640:1152])

    def fine_back(i, carry):
        sums = list(carry)
        for j in range(2):
            r = 2 * i + j
            at = rows_of(r, 48, 48)
            half = rows_of(i, 24, 24)
            m = twice(mf_ref[at, :])
            back = jnp.concatenate([back_ref[2 * j, half, :], back_ref[2 * j + 1, half, :]], axis=0)
            gi = (upf_ref[at, :].astype(F32) + back) * m
            interleave(stage_ref.at[1], r, gi[0:24], gi[24:48])
            gp, normed = pre_grad(
                gi, x_ref[at, :], scf_ref[0:1, :], scf_ref[1:2, :], scf_ref[2:3, :], scf_ref[3:4, :]
            )
            gp_ref[at, :] = gp
            sums[0] = sums[0] + tile_sum(gp * normed)
            sums[1] = sums[1] + tile_sum(gp)
        return tuple(sums)

    none8 = jnp.zeros((8, 256), F32)
    sum_gain, sum_bias = lax.fori_loop(0, 24, fine_back, (none8, none8), unroll=2)
    sends[2].start()
    sends[3].start()
    sum_gain = jnp.sum(sum_gain, axis=0, keepdims=True)
    sum_bias = jnp.sum(sum_bias, axis=0, keepdims=True)
    for p in range(2):
        at = slice(128 * p, 128 * p + 128)
        grad_ref[ROW_VEC + p : ROW_VEC + p + 1, :] = sum_gain[:, at]
        grad_ref[ROW_VEC + 2 + p : ROW_VEC + 3 + p, :] = sum_bias[:, at]
        row_ref[0:1, at], row_ref[1:2, at] = back_means(
            sum_bias[:, at], sum_gain[:, at], gain_f[:, at], C1 // GROUPS, nf
        )

    def fine_conv_grad(r, _):
        at = rows_of(r, 48, 48)
        normed = (x_ref[at, :] - scf_ref[2:3, :]) * scf_ref[3:4, :]
        g = (gp_ref[at, :] * gain_f - row_ref[0:1, :] - normed * row_ref[1:2, :]) * scf_ref[3:4, :]
        g_ref[rows_of(r + 1, 48, 48), :] = (g * twice(mf_ref[at, :])).astype(BF)
        return 0

    lax.fori_loop(0, 48, fine_conv_grad, 0, unroll=2)
    for dx in range(3):
        states = s_ref[48:2352, 256 * dx : 256 * dx + 256]
        for dy in range(3):
            grad = dot_rows(states, g_ref[48 * (2 - dy) : 48 * (2 - dy) + 2304, :])
            for j in range(2):
                grad_ref[pl.ds(2 * (3 * dy + dx) + j, 256, stride=18), :] = grad[:, 128 * j : 128 * j + 128]
    for n, first in enumerate(plan.first):
        block_ref[n] = grad_ref[first : first + plan.rows, :].astype(BF)
        send = pltpu.make_async_copy(block_ref.at[n], blocks_ref.at[n], block_sem.at[n])
        send.start()
        sends.append(send)
    for send in sends:
        send.wait()


def layer_call(plan, *args):
    there = pl.BlockSpec(memory_space=pltpu.HBM)
    low = lambda *shape: pltpu.VMEM(shape, BF)
    wide = lambda *shape: pltpu.VMEM(shape, F32)
    return pl.pallas_call(
        functools.partial(layer_kernel, plan),
        out_shape=[
            jax.ShapeDtypeStruct((PIX, 256), F32),
            jax.ShapeDtypeStruct((CPIX, 128), F32),
            jax.ShapeDtypeStruct((PIX, 256), F32),
            jax.ShapeDtypeStruct((CPIX, 128), F32),
            jax.ShapeDtypeStruct((plan.n, plan.rows, 128), BF),
        ],
        in_specs=[pl.BlockSpec(memory_space=pltpu.SMEM), pl.BlockSpec(memory_space=pltpu.VMEM)] + [there] * 8,
        out_specs=[there] * 5,
        scratch_shapes=[
            low(PIX, 256), low(CPIX, 128), low(128, 256), low(256, 1152), low(256, 768), low(9 * 256, 256),
            low(PIX, 256), low(CPIX, 128),
            wide(plan.tall, 128), low(plan.n, plan.rows, 128),
            low(2400, 768), low(4, CPIX, 256), low(CPIX, 256),
            wide(PIX, 256), wide(CPIX, 128), wide(CPIX, 256), wide(PIX, 128), wide(CPIX, 128),
            wide(8, 256), wide(8, 128),
            low(CPIX, 256), low(CPIX, 512), wide(4, CPIX, 256), wide(PIX, 256), low(2400, 256), wide(8, 256),
            wide(2, 2, PIX, 128), wide(2, CPIX, 128),
            pltpu.SemaphoreType.DMA((8,)),
            pltpu.SemaphoreType.DMA((2, 2)),
            pltpu.SemaphoreType.DMA((plan.n,)),
            pltpu.SemaphoreType.DMA((2,)),
        ],
        compiler_params=pltpu.CompilerParams(vmem_limit_bytes=62 * 2**20),
        name="layer",
    )(*args)


class Plan:
    def __init__(self, shards, length):
        self.dims = {16: (4, 2, 2), 128: (4, 8, 4)}.get(shards, (shards, 1, 1))
        self.n, self.length = shards, length
        self.first = [s * length // 128 for s in range(shards)]
        self.rows = -(-(length + 127) // 128)
        self.rows = -(-self.rows // 32) * 32
        self.part = self.rows // 2
        self.cut = -(-self.part // 32) * 16
        self.tall = -(-(self.first[-1] + self.rows) // 16) * 16

    def here(self):
        d0, d1, d2 = self.dims
        me = lax.axis_index("fsdp")
        return me, lax.axis_index("rep"), me // (d1 * d2), me // d2 % d1, me % d2

    def block(self, a, b, c):
        d0, d1, d2 = self.dims
        return (a * d1 + b) * d2 + c


def flip(a, k):
    bit = 1
    while bit <= k:
        if k & bit:
            a = a + bit - 2 * bit * (a // bit % 2)
        bit *= 2
    return a


def gather_kernel(
    plan,
    master_hbm, inp_hbm, upf_hbm,
    vec_hbm, inpo_hbm, upfo_hbm, wu_hbm, wdn_hbm, wc6_hbm, wf_hbm,
    master_ref, inp_ref, upf_ref, vec_ref, inpo_ref, upfo_ref, wu_ref, wdn_ref, wc6_ref, wf_ref,
    g_ref, w_ref, tmp_ref, in_sem, out_sem, send_sem, recv_sem, sib_send, sib_recv, far_send,
):
    d0, d1, d2 = plan.dims
    me, core, a, b, c = plan.here()
    part, cut = plan.part, plan.cut
    loads = [
        pltpu.make_async_copy(src, dst, in_sem.at[n])
        for n, (src, dst) in enumerate(((master_hbm, master_ref), (inp_hbm, inp_ref), (upf_hbm, upf_ref)))
    ]
    for load in loads:
        load.start()
    barrier = pltpu.get_barrier_semaphore()
    others = [plan.block((a + k) % d0, b, c) for k in range(1, d0)]
    others += [plan.block(a, (b + k) % d1, c) for k in range(1, d1)]
    others += [plan.block(a, b, (c + k) % d2) for k in range(1, d2)]
    others = [{"fsdp": other, "rep": core} for other in others] + [{"fsdp": me, "rep": 1 - core}]
    for other in others:
        pl.semaphore_signal(barrier, inc=1, device_id=other, device_id_type=pl.DeviceIdType.MESH)
    loads[0].wait()
    off = (me * plan.length) % 128
    x = pltpu.roll(master_ref[...], off, 1)
    row = lax.broadcasted_iota(jnp.int32, x.shape, 0)
    lane = lax.broadcasted_iota(jnp.int32, x.shape, 1)
    above = jnp.where(row == 0, 0.0, pltpu.roll(x, 1, 0))
    g_ref[me] = jnp.where(lane < off, above, x).astype(BF)
    pl.semaphore_wait(barrier, len(others))

    def span(half, which):
        start = which * part + (cut if half == 1 else 0)
        return pl.ds(pl.multiple_of(start, 16), (cut, part - cut)[half])

    def copy(block, half, fsdp, rep, send, recv, which):
        at = g_ref.at[block, span(half, which)]
        return pltpu.make_async_remote_copy(
            src_ref=at, dst_ref=at, send_sem=send, recv_sem=recv,
            device_id={"fsdp": fsdp, "rep": rep}, device_id_type=pl.DeviceIdType.MESH,
        )

    def arrive(block, half):
        copy(block, half, me, core, far_send.at[0, 0], recv_sem.at[block, half], core).wait_recv()

    sent = []

    def go(d):
        d.start()
        sent.append(d)

    def along1(block, half):
        for k in range(1, d1):
            go(copy(block, half, plan.block(a, (b + k) % d1, c), core,
                    send_sem.at[block, half, k - 1], recv_sem.at[block, half], core))

    def along2(block, half):
        for k in range(1, d2):
            go(copy(block, half, plan.block(a, b, (c + k) % d2), core,
                    send_sem.at[block, half, d1 + k - 2], recv_sem.at[block, half], core))

    def beside(block, half):
        go(copy(block, half, me, 1 - core, sib_send.at[block, half], sib_recv.at[block, half], core))

    def own_column(k):
        block = plan.block(flip(a, k), b, c)
        if k:
            arrive(block, 0)
        along2(block, 0)
        if k:
            arrive(block, 1)
        along1(block, 1)
        along2(block, 1)
        along1(block, 0)
        if k:
            beside(block, 0)
            beside(block, 1)

    def near(k):
        a2 = flip(a, k)
        ahead = [plan.block(a2, b, (c + i) % d2) for i in range(1, d2)]
        above = [plan.block(a2, (b + i) % d1, c) for i in range(1, d1)]
        for block in ahead:
            arrive(block, 0)
            along1(block, 0)
            beside(block, 0)
        for block in above:
            arrive(block, 1)
            along2(block, 1)
            beside(block, 1)
        for block in ahead:
            arrive(block, 1)
            beside(block, 1)
        for block in above:
            arrive(block, 0)
            beside(block, 0)

    def diagonal(k):
        a2 = flip(a, k)
        for i in range(1, d1):
            for j in range(1, d2):
                block = plan.block(a2, (b + i) % d1, (c + j) % d2)
                for half in (0, 1):
                    arrive(block, half)
                    beside(block, half)

    def parity(src, dst):
        def one(r, _):
            at = rows_of(r, 48, 48)
            v = src[at, :].astype(F32)
            for p in range(2):
                tmp_ref[p, at, :] = v[:, 128 * p : 128 * p + 128]
            even = [tmp_ref[p, pl.ds(r * 48, 24, stride=2), :] for p in range(2)]
            odd = [tmp_ref[p, pl.ds(r * 48 + 1, 24, stride=2), :] for p in range(2)]
            both = [jnp.concatenate(even, axis=1), jnp.concatenate(odd, axis=1)]
            dst[at, :] = jnp.concatenate(both, axis=0).astype(BF)
            return 0

        lax.fori_loop(0, 48, one, 0, unroll=4)

    outs = []

    def put(src, dst):
        copy_out = pltpu.make_async_copy(src, dst, out_sem.at[len(outs)])
        copy_out.start()
        outs.append(copy_out)

    for k in range(1, d0):
        for half in (0, 1):
            go(copy(me, half, plan.block(flip(a, k), b, c), core, far_send.at[k, half], recv_sem.at[me, half], core))
    own_column(0)
    loads[1].wait()
    parity(inp_ref, inpo_ref)
    put(inpo_ref, inpo_hbm)
    loads[2].wait()
    parity(upf_ref, upfo_ref)
    put(upfo_ref, upfo_hbm)
    for k in range(1, d0):
        own_column(k)
    for k in range(d0):
        near(k)
    for k in range(d0):
        diagonal(k)
    for k in range(1, plan.n):
        block = (me + k) % plan.n
        for half in (0, 1):
            copy(block, half, me, core, far_send.at[0, 0], sib_recv.at[block, half], 1 - core).wait_recv()

    for s in range(plan.n):
        v = g_ref[s].astype(F32)
        at = plan.first[s]
        if s:
            low = w_ref[at : at + 1, :] + v[0:1]
            w_ref[at : at + plan.rows, :] = v
            w_ref[at : at + 1, :] = low
        else:
            w_ref[0 : plan.rows, :] = v
    vec_ref[...] = w_ref[ROW_VEC : ROW_VEC + 8, :]
    put(vec_ref, vec_hbm)
    for t in range(9):
        at = slice(256 * t, 256 * t + 256)
        for h in range(2):
            wf_ref[at, 128 * h : 128 * h + 128] = w_ref[pl.ds(2 * t + h, 256, stride=18), :].astype(BF)
        put(wf_ref.at[at], wf_hbm.at[at])
    for h in range(2):
        wu_ref[:, 128 * h : 128 * h + 128] = w_ref[pl.ds(ROW_UP + h, 128, stride=2), :].astype(BF)
    put(wu_ref, wu_hbm)
    for t in range(9):
        p = (4, 5, 3, 7, 1, 8, 6, 2, 0).index(t)
        wdn_ref[:, 128 * p : 128 * p + 128] = w_ref[pl.ds(ROW_DOWN + t, 256, stride=9), :].astype(BF)
    put(wdn_ref, wdn_hbm)
    wc6_ref[0:128, 384:768] = jnp.zeros((128, 384), BF)
    for t in range(9):
        dy, dx = t // 3, t % 3
        at, p = 128 * (dx + 1) // 2 // 128 * 128, dy + 3 * (dx // 2)
        wc6_ref[at : at + 128, 128 * p : 128 * p + 128] = w_ref[pl.ds(ROW_COARSE + t, 128, stride=9), :].astype(BF)
    put(wc6_ref, wc6_hbm)
    for d in sent:
        d.wait_send()
    for d in outs:
        d.wait()


def gather_call(plan, master, inp, upf):
    there = pl.BlockSpec(memory_space=pltpu.HBM)
    low = lambda *shape: jax.ShapeDtypeStruct(shape, BF)
    outs = [
        jax.ShapeDtypeStruct((8, 128), F32), low(PIX, 256), low(PIX, 256), low(128, 256), low(256, 1152),
        low(256, 768), low(9 * 256, 256),
    ]
    d0, d1, d2 = plan.dims
    sems = pltpu.SemaphoreType.DMA
    return pl.pallas_call(
        functools.partial(gather_kernel, plan),
        out_shape=[pltpu.HBM(o.shape, o.dtype) for o in outs],
        in_specs=[there] * 3,
        out_specs=[there] * 7,
        scratch_shapes=[pltpu.VMEM((plan.rows, 128), F32), pltpu.VMEM((PIX, 256), BF), pltpu.VMEM((PIX, 256), BF)]
        + [pltpu.VMEM(o.shape, o.dtype) for o in outs]
        + [
            pltpu.VMEM((plan.n, plan.rows, 128), BF), pltpu.VMEM((plan.tall, 128), F32), pltpu.VMEM((2, PIX, 128), F32),
            sems((3,)), sems((15,)), sems((plan.n, 2, max(d1 + d2 - 2, 1))), sems((plan.n, 2)), sems((plan.n, 2)),
            sems((plan.n, 2)), sems((d0, 2)),
        ],
        compiler_params=pltpu.CompilerParams(collective_id=0, has_side_effects=True, vmem_limit_bytes=32 * 2**20),
        name="gather_weights",
    )(*(pltpu.with_memory_space_constraint(x, pltpu.HBM) for x in (master, inp, upf)))


def reduce_kernel(plan, p_hbm, out_ref, tile_ref,
                  p_ref, q_ref, ua_ref, ub_ref, va_ref, vb_ref, z_ref, sa_ref, total_ref, n1_ref, n2_ref,
                  q_send, q_recv, s1_send, s1_recv, s2_send, s2_recv, s3_send, s3_recv, t_send, t_recv, n1_send, n1_recv, n2_send, n2_recv, own_sem):
    d0, d1, d2 = plan.dims
    me, core, a, b, c = plan.here()
    part, cut = plan.part, plan.cut
    MESH = pl.DeviceIdType.MESH
    mine = pl.multiple_of(core * part, 16)
    theirs = pl.multiple_of((1 - core) * part, 16)
    load = pltpu.make_async_copy(p_hbm.at[:, pl.ds(mine, part)], p_ref, own_sem.at[0])
    load.start()
    barrier = pltpu.get_barrier_semaphore()
    others = [({"fsdp": plan.block((a + k) % d0, b, c), "rep": core}) for k in range(1, d0)]
    plane = []
    for i in range(d1):
        for j in range(d2):
            for o in range(2):
                if i or j or o:
                    plane.append((i, j, o, {"fsdp": plan.block(a, (b + i) % d1, (c + j) % d2), "rep": (core + o) % 2}))
    others += [p[3] for p in plane]
    for other in others:
        pl.semaphore_signal(barrier, inc=1, device_id=other, device_id_type=MESH)
    pl.semaphore_wait(barrier, len(others))

    sent = []
    def go(src, dst, send, recv, to):
        d = pltpu.make_async_remote_copy(src_ref=src, dst_ref=dst, send_sem=send, recv_sem=recv, device_id=to, device_id_type=MESH)
        d.start()
        sent.append(d)

    def got(ref, recv):
        pltpu.make_async_copy(ref, ref, recv).wait()

    halves = ((0, cut), (cut, part - cut))
    order = [(k + 1) % d0 for k in range(d0)]
    spots = []
    for k in order:
        for i in list(range(1, d1)) + [0]:
            for j in list(range(1, d2)) + [0]:
                spots.append((k, i, j))
    for k, i, j in spots:
        s = plan.block((a + k) % d0, (b + i) % d1, (c + j) % d2)
        go(p_hbm.at[s, pl.ds(theirs, part)], q_ref.at[s], q_send.at[s], q_recv.at[s], {"fsdp": me, "rep": 1 - core})

    load.wait()

    def pair(s, half):
        start, size = halves[half]
        x = p_ref[s, start:start + size, :].astype(F32)
        return x + q_ref[s, start:start + size, :].astype(F32)

    def step1(k):
        a2 = (a + k) % d0
        for i in range(1, d1):
            for j in list(range(1, d2)) + [0]:
                s = plan.block(a2, (b + i) % d1, (c + j) % d2)
                got(q_ref.at[s], q_recv.at[s])
                sa_ref[s, 0:cut, :] = pair(s, 0).astype(BF)
                go(sa_ref.at[s, 0:cut], ua_ref.at[a2, (c + j) % d2, i - 1], s1_send.at[s, 0], s1_recv.at[0, a2, (c + j) % d2, i - 1],
                   {"fsdp": plan.block(a, (b + i) % d1, c), "rep": core})
                if j:
                    step1b(s, a2, i, j)
        for j in range(1, d2):
            s = plan.block(a2, b, (c + j) % d2)
            got(q_ref.at[s], q_recv.at[s])
            step1b(s, a2, 0, j)

    def step1b(s, a2, i, j):
        sa_ref[s, cut:part, :] = pair(s, 1).astype(BF)
        go(sa_ref.at[s, cut:part], ub_ref.at[a2, (b + i) % d1, j - 1], s1_send.at[s, 1], s1_recv.at[1, a2, (b + i) % d1, j - 1],
           {"fsdp": plan.block(a, b, (c + j) % d2), "rep": core})

    def from1(half, a2, other):
        ref = ua_ref if half == 0 else ub_ref
        total = None
        for i in range((d1 if half == 0 else d2) - 1):
            got(ref.at[a2, other, i], s1_recv.at[half, a2, other, i])
            v = ref[a2, other, i].astype(F32)
            total = v if total is None else total + v
        return total

    def plus(x, y):
        return x if y is None else x + y

    def step2(k):
        a2 = (a + k) % d0
        for j in range(1, d2):
            c2 = (c + j) % d2
            s = plan.block(a2, b, c2)
            sa_ref[s, 0:cut, :] = plus(pair(s, 0), from1(0, a2, c2)).astype(BF)
            go(sa_ref.at[s, 0:cut], va_ref.at[a2, j - 1], s2_send.at[0, a2, j - 1], s2_recv.at[0, a2, j - 1],
               {"fsdp": plan.block(a, b, c2), "rep": core})
        for i in range(1, d1):
            b2 = (b + i) % d1
            s = plan.block(a2, b2, c)
            sa_ref[s, cut:part, :] = plus(pair(s, 1), from1(1, a2, b2)).astype(BF)
            go(sa_ref.at[s, cut:part], vb_ref.at[a2, i - 1], s2_send.at[1, a2, i - 1], s2_recv.at[1, a2, i - 1],
               {"fsdp": plan.block(a, b2, c), "rep": core})

    def column(k):
        a2 = (a + k) % d0
        s = plan.block(a2, b, c)
        got(q_ref.at[s], q_recv.at[s])
        x = plus(pair(s, 0), from1(0, a2, c))
        for j in range(1, d2):
            got(va_ref.at[a2, j - 1], s2_recv.at[0, a2, j - 1])
            x = x + va_ref[a2, j - 1].astype(F32)
        y = plus(pair(s, 1), from1(1, a2, b))
        for i in range(1, d1):
            got(vb_ref.at[a2, i - 1], s2_recv.at[1, a2, i - 1])
            y = y + vb_ref[a2, i - 1].astype(F32)
        return s, x, y

    def step3(k):
        s, x, y = column(k)
        sa_ref[s, 0:cut, :] = x.astype(BF)
        sa_ref[s, cut:part, :] = y.astype(BF)
        go(sa_ref.at[s], z_ref.at[k - 1], s3_send.at[k - 1], s3_recv.at[k - 1], {"fsdp": plan.block((a + k) % d0, b, c), "rep": core})

    for n in range(d0 + 2):
        if n < d0:
            step1(order[n])
        if 0 <= n - 1 < d0:
            step2(order[n - 1])
        if 0 <= n - 2 < d0 - 1:
            step3(order[n - 2])
    _, x, y = column(0)
    total = jnp.concatenate([x, y], axis=0)
    for k in range(1, d0):
        got(z_ref.at[k - 1], s3_recv.at[k - 1])
        total = total + z_ref[k - 1].astype(F32)
    total_ref[pl.ds(mine, part), :] = total
    go(total_ref.at[pl.ds(mine, part)], total_ref.at[pl.ds(mine, part)], t_send.at[0], t_recv.at[0], {"fsdp": me, "rep": 1 - core})

    off = (me * plan.length) % 128
    row = lax.broadcasted_iota(jnp.int32, (part, 128), 0) + mine
    at = row * 128 + lax.broadcasted_iota(jnp.int32, (part, 128), 1)
    own = jnp.where((at >= off) & (at < off + plan.length), total, 0.0)
    last = me == plan.n - 1
    for i in range(6):
        spot = ROW_VEC - plan.first[-1] + i
        holds = last & (core == spot // part)
        n1_ref[a, i:i + 1, :] = jnp.where(holds, total[spot % part:spot % part + 1], 0.0)
    n1_ref[a, 6:7, :] = jnp.sum(own * own, axis=0, keepdims=True)
    n1_ref[a, 7:8, :] = jnp.zeros((1, 128), F32)
    for k in range(1, d0):
        go(n1_ref.at[a], n1_ref.at[a], n1_send.at[k], n1_recv.at[a], {"fsdp": plan.block((a + k) % d0, b, c), "rep": core})
    for k in range(1, d0):
        got(n1_ref.at[(a + k) % d0], n1_recv.at[(a + k) % d0])
    tile = n1_ref[0]
    for k in range(1, d0):
        tile = tile + n1_ref[k]
    slot = (b * d2 + c) * 2 + core
    n2_ref[slot] = tile
    for n, (i, j, o, to) in enumerate(plane):
        go(n2_ref.at[slot], n2_ref.at[slot], n2_send.at[n], n2_recv.at[slot], to)
    got(total_ref.at[pl.ds(theirs, part)], t_recv.at[0])
    x = pltpu.roll(total_ref[...], (128 - off) % 128, 1)
    below = pltpu.roll(x, plan.rows - 1, 0)
    lane = lax.broadcasted_iota(jnp.int32, x.shape, 1)
    moved = jnp.where(lane + off >= 128, below, x)
    for n, (i, j, o, to) in enumerate(plane):
        other = (((b + i) % d1) * d2 + (c + j) % d2) * 2 + (core + o) % 2
        got(n2_ref.at[other], n2_recv.at[other])
    tile = n2_ref[0]
    for n in range(1, 2 * d1 * d2):
        tile = tile + n2_ref[n]
    grad_norm = jnp.sqrt(jnp.sum(tile[6:7], axis=1, keepdims=True))
    factor = jnp.minimum(1.0, clip_norm / (grad_norm + 1e-06))
    out_ref[...] = moved * factor
    tile_ref[0:6, :] = tile[0:6] * factor
    tile_ref[6:8, :] = jnp.broadcast_to(grad_norm, (2, 128))
    for d in sent:
        d.wait_send()


def reduce_call(plan, grads):
    V = pl.BlockSpec(memory_space=pltpu.VMEM)
    d0, d1, d2 = plan.dims
    D = pltpu.SemaphoreType.DMA
    b = lambda *s: pltpu.VMEM(s, BF)
    e1, e2 = max(d1 - 1, 1), max(d2 - 1, 1)
    return pl.pallas_call(functools.partial(reduce_kernel, plan),
        out_shape=[jax.ShapeDtypeStruct((plan.rows, 128), F32), jax.ShapeDtypeStruct((8, 128), F32)],
        in_specs=[pl.BlockSpec(memory_space=pltpu.HBM)], out_specs=[V] * 2,
        scratch_shapes=[b(plan.n, plan.part, 128), b(plan.n, plan.part, 128), b(d0, d2, e1, plan.cut, 128), b(d0, d1, e2, plan.part - plan.cut, 128),
            b(d0, e2, plan.cut, 128), b(d0, e1, plan.part - plan.cut, 128), b(max(d0 - 1, 1), plan.part, 128), b(plan.n, plan.part, 128),
            pltpu.VMEM((plan.rows, 128), F32), pltpu.VMEM((d0, 8, 128), F32), pltpu.VMEM((2 * d1 * d2, 8, 128), F32),
            D((plan.n,)), D((plan.n,)), D((plan.n, 2)), D((2, d0, max(d1, d2), max(e1, e2))), D((2, d0, max(e1, e2))), D((2, d0, max(e1, e2))),
            D((d0,)), D((d0,)), D((1,)), D((1,)), D((d0,)), D((d0,)), D((2 * d1 * d2,)), D((2 * d1 * d2,)), D((1,))],
        compiler_params=pltpu.CompilerParams(collective_id=1, has_side_effects=True, vmem_limit_bytes=32 * 2**20),
        name="reduce_gradients")(pltpu.with_memory_space_constraint(grads, pltpu.HBM))


def per_device(
    input_fine, input_coarse, upstream_fine, upstream_coarse, extents, master, first_moment, second_moment, average
):
    plan = Plan(lax.axis_size("fsdp"), master.shape[0])
    padded = jnp.pad(master, (0, plan.rows * 128 - plan.length)).reshape(plan.rows, 128)
    vec, inp, upf, wu, wdn, wc6, wf = gather_call(
        plan, padded, input_fine.reshape(PIX, C1), upstream_fine.reshape(PIX, C1)
    )
    out_fine, out_coarse, gi_fine, gi_coarse, blocks = layer_call(
        plan, extents, vec, inp, input_coarse.reshape(CPIX, C2), wu, wdn, wc6, wf, upf,
        upstream_coarse.reshape(CPIX, C2),
    )
    clipped, tile = reduce_call(plan, blocks)
    clipped = clipped.reshape(-1)[: plan.length]
    grad_norm = tile[6, 0]
    norm_grads = tile[:6].reshape(-1)
    new_first = beta_one * first_moment + (1.0 - beta_one) * clipped
    new_second = beta_two * second_moment + (1.0 - beta_two) * clipped * clipped
    corrected_first = new_first / (1.0 - beta_one**STEP)
    corrected_second = new_second / (1.0 - beta_two**STEP)
    new_master = master - learn_rate * (
        corrected_first / (jnp.sqrt(corrected_second) + adam_eps) + decay_rate * master
    )
    ema_rate = min(0.999, (1.0 + STEP) / (10.0 + STEP))
    new_average = ema_rate * average + (1.0 - ema_rate) * new_master
    return (
        out_fine.reshape(input_fine.shape),
        out_coarse.reshape(input_coarse.shape),
        gi_fine.reshape(input_fine.shape),
        gi_coarse.reshape(input_coarse.shape),
        grad_norm,
        new_master,
        new_first,
        new_second,
        new_average,
        norm_grads,
    )


def solution(mesh):
    images = P(("fsdp", "rep"), None, None, None)
    flat = P("fsdp")
    in_specs = (images,) * 4 + (P(("fsdp", "rep"), None),) + (flat,) * 4
    out_specs = (images,) * 4 + (P(),) + (flat,) * 4 + (P(),)
    return jax.shard_map(per_device, mesh=mesh, in_specs=in_specs, out_specs=out_specs, check_vma=False)
```

time: 159 us -> 121 us (0.76)
  Pallas kernels: 140 us -> 116 us
  local copies, waits for them, and re-layouts: 13.1 us -> 2.81 us
  between operations: 2.58 us -> 0.7 us
    pallas_call x1, Pallas kernels: 89.3 us -> 67 us  [layer_call(): pl.pallas_call(functools.partial(layer_kernel, plan), out_shape=[jax.Shap...]
    unnamed x34 -> x8, local copies, waits for them, and re-layouts: 12.1 us -> 0.03 us
where the time goes in v3:
time: 121 us
  Pallas kernels  116 us (96%)
  local copies, waits for them, and re-layouts  2.81 us (2%)
    pallas_call x1, Pallas kernels, layer_call(): pl.pallas_call(functools.partial(layer_kernel, plan), out_shape=[jax.Shap...  67 us
    pallas_call x1, Pallas kernels, reduce_call(): pl.pallas_call(functools.partial(reduce_kernel, plan), out_shape=[jax.Sha...  26.8 us
    pallas_call x1, Pallas kernels, gather_call(): pl.pallas_call(functools.partial(gather_kernel, plan), out_shape=[pltpu.H...  22.2 us

profile of v3, /device:TPU:0, one launch (start us, length us, event | category | flops | bytes accessed | tf_op | source)
XLA Modules:
  0.0 120.6 jit_solution(13300842206523689045)
XLA Ops:
  0.6 1.7 %pad_bitcast_fusion.master_hbm = f32[544,128]{1,0:T(8,128)} fusion(f32[66608]{0:T(1024)} %param.14), kind=kLoop, calls=%fused_computation.1 | loop fusion | bytes 544960 | tf_op jit(solution)/shard_map/reshape | solution.py:866
  2.3 22.2 %gather_weights.1 = (f32[8,128]{1,0:T(8,128)}, bf16[2304,256]{1,0:T(8,128)(2,1)}, bf16[2304,256]{1,0:T(8,128)(2,1)}, bf16[128,256]{1,0:T(8,128)(2,1)}, bf16[256,...) custom-call(f32[544,128]{1,0:T(8,128)} %pad_bitcast_fusion.master_hbm, ...), custom_call_target="tpu_custom_call" | custom-call | tf_op jit(solution)/shard_map/gather_weights/pallas_call | solution.py:651
  24.6 67.0 %layer.1 = (f32[2304,256]{1,0:T(8,128)}, f32[576,128]{1,0:T(8,128)}, f32[2304,256]{1,0:T(8,128)}, f32[576,128]{1,0:T(8,128)}, bf16[16,544,128]{2,1,0:T(8,128)(2,1)}) custom-call(s32[1,2]{1,0:T(1,128)} %ext_ref.1, f32[8,128]{1,0:T(8,128)} %get-tuple-element.24.vec_ref, bf16[2304,256]{1,0:T(8,128)(2,1)} %get-tuple-element.25.inp_hbm, ...), custom_call_target="tpu_custom_call" | custom-call | tf_op jit(solution)/shard_map/layer/pallas_call | solution.py:398
  91.5 0.0 copy-start
  91.5 0.0 copy-start.1
  91.5 0.0 copy-start.2
  91.6 0.0 copy-start.3
  91.6 26.8 %reduce_gradients.1 = (f32[544,128]{1,0:T(8,128)S(1)}, f32[8,128]{1,0:T(8,128)S(1)}) custom-call(bf16[16,544,128]{2,1,0:T(8,128)(2,1)} %get-tuple-element.35.p_hbm), custom_call_target="tpu_custom_call" | custom-call | tf_op jit(solution)/shard_map/reduce_gradients/pallas_call | solution.py:850
  118.4 0.5 slice.9
  118.9 0.6 slice_bitcast_fusion
  119.5 0.0 copy-done
  119.5 0.0 copy-done.1
  119.5 0.0 copy-done.2
  119.5 0.0 copy-done.3
  119.5 1.1 multiply_add_fusion
Async XLA Ops:
  91.5 28.0 %copy-start = (f32[66608]{0:T(1024)S(1)}, f32[66608]{0:T(1024)}, u32[]{:S(2)}) copy-start(f32[66608]{0:T(1024)} %param.14) | copy-start | bytes 799300
  91.5 28.0 %copy-start.1 = (f32[66608]{0:T(1024)S(1)}, f32[66608]{0:T(1024)}, u32[]{:S(2)}) copy-start(f32[66608]{0:T(1024)} %param.17) | copy-start | bytes 799300
  91.5 28.0 %copy-start.2 = (f32[66608]{0:T(1024)S(1)}, f32[66608]{0:T(1024)}, u32[]{:S(2)}) copy-start(f32[66608]{0:T(1024)} %param.15) | copy-start | bytes 799300
  91.6 27.9 %copy-start.3 = (f32[66608]{0:T(1024)S(1)}, f32[66608]{0:T(1024)}, u32[]{:S(2)}) copy-start(f32[66608]{0:T(1024)} %param.16) | copy-start | bytes 799300

commit v4 on v3

--- a/solution.py
+++ b/solution.py
@@ -63,16 +63,31 @@
     )
 
 
+def rows_out(x):
+    parts = [x[24 * i : 24 * i + 24] for i in range(24)]
+    return parts[0::2] + parts[1::2]
+
+
+def pair_order(rows):
+    return jnp.concatenate([rows[i // 2 + 12 * (i % 2)] for i in range(24)], axis=0)
+
+
+def image_order(x):
+    return jnp.concatenate(rows_out(x), axis=0)
+
+
 def in_rows(x, change):
     return jnp.concatenate([change(x[24 * r : 24 * r + 24]) for r in range(24)], axis=0)
 
 
 def row_down(x):
-    return jnp.concatenate([jnp.zeros((24, x.shape[1]), F32), x[:552]], axis=0)
+    rows = rows_out(x)
+    return pair_order([jnp.zeros_like(rows[0])] + rows[:-1])
 
 
 def row_up(x):
-    return jnp.concatenate([x[24:], jnp.zeros((24, x.shape[1]), F32)], axis=0)
+    rows = rows_out(x)
+    return pair_order(rows[1:] + [jnp.zeros_like(rows[0])])
 
 
 def tile_sum(x):
@@ -98,19 +113,23 @@
     return pl.ds(start if isinstance(r, int) else pl.multiple_of(start, unit if unit % 16 == 0 else 8), count)
 
 
+STEPS = "E0 E1 E2 C0 E3 E4 E5 C1 E6 E7 E8 C2 E9 E10 E11 C3 L C4 Z K C5 S F B"
+
+
 def layer_kernel(
     plan,
     ext_ref, vec_ref, inp_hbm, inc_hbm, wu_hbm, wdn_hbm, wc6_hbm, wf_hbm, upf_hbm, upc_hbm,
     outf_ref, outc_ref, gif_ref, gic_ref, blocks_ref,
-    inp_ref, inc_ref, wu_ref, wdn_ref, wc6_ref, wf_ref, upf_ref, upc_ref,
-    grad_ref, block_ref, s_ref, ph_ref, c_ref, x_ref, xc_ref, lift_ref, mf_ref, mc_ref, scf_ref, scc_ref,
-    gl_ref, glo_ref, back_ref, gp_ref, g_ref, row_ref, stage_ref, small_ref, in_sem, out_sem, block_sem, small_sem,
+    inp_ref, inc_in, wu_ref, wdn_ref, wc6_ref, wf_ref, upf_ref, upc_ref,
+    grad_ref, block_ref, u_ref, ph_ref, c_ref, x_ref, xc_ref, inc_ref, branch_ref, lift_ref, mf_ref, mb_ref, mc_ref,
+    scf_ref, scc_ref, gl_ref, glo_ref, back_ref, gp_ref, g_ref, row_ref, stage_ref, small_ref,
+    in_sem, out_sem, block_sem, small_sem,
 ):
     loads = [
         pltpu.make_async_copy(src, dst, in_sem.at[n])
         for n, (src, dst) in enumerate(
             (
-                (inp_hbm, inp_ref), (inc_hbm, inc_ref), (wu_hbm, wu_ref), (wdn_hbm, wdn_ref),
+                (inc_hbm, inc_in), (inp_hbm, inp_ref), (wu_hbm, wu_ref), (wdn_hbm, wdn_ref),
                 (wc6_hbm, wc6_ref), (wf_hbm, wf_ref), (upf_hbm, upf_ref), (upc_hbm, upc_ref),
             )
         )
@@ -121,104 +140,136 @@
     gain_f = jnp.concatenate([vec_ref[0:1, :], vec_ref[1:2, :]], axis=1)
     bias_f = jnp.concatenate([vec_ref[2:3, :], vec_ref[3:4, :]], axis=1)
     gain_c, bias_c = vec_ref[4:5, :], vec_ref[5:6, :]
-    pos = lax.broadcasted_iota(jnp.int32, (48, 128), 0)
-    col = jnp.where(pos < 24, 2 * pos, 2 * pos - 47)
-    colm = jnp.where(col < ww, 1.0, 0.0).astype(F32)
+    pos = lax.broadcasted_iota(jnp.int32, (24, 128), 0)
+    even = jnp.where(2 * pos < ww, 1.0, 0.0).astype(F32)
+    odd = jnp.where(2 * pos + 1 < ww, 1.0, 0.0).astype(F32)
 
     def setup(r, _):
-        at = rows_of(r, 48, 48)
-        mf_ref[at, :] = jnp.where(r < hh, colm, 0.0)
-        x_ref[at, :] = jnp.zeros((48, 256), F32)
+        at = rows_of(r, 96, 96)
+        low, high = r < hh, r + 24 < hh
+        m = [jnp.where(here, v, 0.0) for v in (even, odd) for here in (low, high)]
+        m = jnp.concatenate(m, axis=0)
+        mf_ref[at, :] = m
+        mb_ref[at, :] = m.astype(BF)
+        x_ref[at, :] = jnp.zeros((96, 256), F32)
         return 0
 
-    lax.fori_loop(0, 48, setup, 0)
+    lax.fori_loop(0, 24, setup, 0)
 
     def setup_coarse(r, _):
-        mc_ref[rows_of(r, 24, 24), :] = jnp.where(2 * r < hh, colm[0:24], 0.0)
+        m = [jnp.where(2 * r < hh, even, 0.0), jnp.where(2 * r + 24 < hh, even, 0.0)]
+        mc_ref[rows_of(r, 48, 48), :] = jnp.concatenate(m, axis=0)
         return 0
 
-    lax.fori_loop(0, 24, setup_coarse, 0)
+    lax.fori_loop(0, 12, setup_coarse, 0)
     nf = (hh * ww).astype(F32) * (C1 // GROUPS)
     nc = (((hh + 1) // 2) * ((ww + 1) // 2)).astype(F32) * (C2 // GROUPS)
-    s_ref[0:48, :] = jnp.zeros((48, 768), BF)
-    s_ref[49 * 48 : 50 * 48, :] = jnp.zeros((48, 768), BF)
-    g_ref[0:48, :] = jnp.zeros((48, 256), BF)
-    g_ref[49 * 48 : 50 * 48, :] = jnp.zeros((48, 256), BF)
+    g_ref[:, 0:96, :] = jnp.zeros((4, 96, 256), BF)
+    g_ref[:, 26 * 48 : 28 * 48, :] = jnp.zeros((4, 96, 256), BF)
     grad_ref[FLAT_ROWS:, :] = jnp.zeros((plan.tall - FLAT_ROWS, 128), F32)
     xc_ref[...] = jnp.zeros((576, 128), F32)
     scf_ref[...] = jnp.zeros((8, 256), F32)
     scc_ref[...] = jnp.zeros((8, 128), F32)
     scf_ref[1:2, :] = 0.5 * bias_f
     scc_ref[1:2, :] = 0.5 * bias_c
-    for load in loads[:6]:
+    loads[0].wait()
+    v = inc_in[...].astype(F32)
+    inc_ref[...] = pair_order([v[24 * r : 24 * r + 24] for r in range(24)])
+    for load in loads[1:6]:
         load.wait()
 
     def coarse_branch():
         h = xc_ref[...] * scc_ref[0:1, :] + scc_ref[1:2, :]
         y = h * jnp.tanh(h) + h
-        branch = ((y + inc_ref[...].astype(F32)) * mc_ref[...]).astype(BF)
+        branch = ((y + inc_ref[...]) * mc_ref[...]).astype(BF)
+        branch_ref[...] = branch
         lift_ref[...] = dot(branch, wu_ref[...])
-        return branch
-
-    def fine_rows(g, final):
+
+    def unit(r, final):
         scale, shift = scf_ref[0:1, :], scf_ref[1:2, :]
-        pieces = ([], [])
-        for j in range(4):
-            r = 4 * g + j
-            at = rows_of(r, 48, 48)
-            m = twice(mf_ref[at, :])
+        half = rows_of(r // 2, 48, 48)
+        lift = lift_ref[half, :]
+        lift_low = lift.astype(BF)
+        z = []
+        for p in range(2):
+            at = rows_of(2 * r + p, 48, 48)
             h = x_ref[at, :] * scale + shift
             y = h * jnp.tanh(h) + h
-            lift = lift_ref[rows_of(2 * g + j // 2, 24, 24), :]
-            lift = jnp.concatenate([lift, lift], axis=0)
             if final:
+                m = twice(mf_ref[at, :])
                 low = ((y + inp_ref[at, :].astype(F32)) * m).astype(BF)
-                branch = low.astype(F32)
-                z = (branch + lift) * m
-                interleave(stage_ref.at[0], r, z[0:24], z[24:48])
+                z.append((low.astype(F32) + lift) * m)
             else:
-                m = m.astype(BF)
+                m = twice(mb_ref[at, :])
                 low = (y.astype(BF) + inp_ref[at, :]) * m
-                branch = low.astype(F32)
-                z = ((low + lift.astype(BF)) * m).astype(F32)
-                even, odd = z[0:24], z[24:48]
-                to = rows_of(r + 1, 48, 48)
-                s_ref[to, 0:256] = jnp.concatenate([shift_down(odd), even], axis=0).astype(BF)
-                s_ref[to, 256:512] = z.astype(BF)
-                s_ref[to, 512:768] = jnp.concatenate([odd, shift_up(even)], axis=0).astype(BF)
-            pieces[j % 2].append(branch)
-        at = rows_of(g, 48, 48)
-        for i, (above, below) in enumerate(pieces):
-            ph_ref[2 * i, at, :] = jnp.concatenate([above[0:24], below[0:24]], axis=0).astype(BF)
-            ph_ref[2 * i + 1, at, :] = jnp.concatenate([above[24:48], below[24:48]], axis=0).astype(BF)
-
-    def lowered():
+                z.append((low + lift_low) * m)
+            ph_ref[2 * (r % 2) + p, half, :] = low
+        even, odd = z
+        if final:
+            for i in range(2):
+                at = slice(24 * i, 24 * i + 24)
+                interleave(stage_ref.at[0], r + 24 * i, even[at], odd[at])
+            return
+        wide = odd.astype(F32)
+        left = jnp.concatenate([shift_down(wide[0:24]), shift_down(wide[24:48])], axis=0).astype(BF)
+        wide = even.astype(F32)
+        right = jnp.concatenate([shift_up(wide[0:24]), shift_up(wide[24:48])], axis=0).astype(BF)
+        for i, u in enumerate((left - odd, even + odd, odd - even, even - right)):
+            u_ref[i, rows_of(r + 1, 48, 48), :] = u
+            if r == 0:
+                w = u.astype(F32)
+                u_ref[i, 25 * 48 : 26 * 48, :] = jnp.concatenate([w[24:48], jnp.zeros_like(w[0:24])], axis=0).astype(BF)
+            if r == 23:
+                w = u.astype(F32)
+                u_ref[i, 0:48, :] = jnp.concatenate([jnp.zeros_like(w[0:24]), w[0:24]], axis=0).astype(BF)
+
+    def lowered_parts():
         ee, eo, oe, oo = (ph_ref[i] for i in range(4))
         p = dot(eo, wdn_ref[:, 128:384]) + dot(oo, wdn_ref[:, 640:896])
         q = dot(oe, wdn_ref[:, 384:640])
         t = dot(oo, wdn_ref[:, 896:1152])
-        here = p[:, :128] + q[:, :128] + dot(ee, wdn_ref[:, 0:128])
+        return p, q, t, dot(ee, wdn_ref[:, 0:128])
+
+    def lowered(parts):
+        p, q, t, e = parts
+        here = p[:, :128] + q[:, :128] + e
         return here + row_down(q[:, 128:] + t[:, :128]) + in_rows(p[:, 128:] + row_down(t[:, 128:]), shift_down)
 
-    def coarse_step(branch):
-        zc = (branch.astype(F32) + lowered()) * mc_ref[...]
+    def coarse_state(parts):
+        zc = (branch_ref[...].astype(F32) + lowered(parts)) * mc_ref[...]
         c_ref[:, 0:128] = in_rows(zc, shift_down).astype(BF)
         c_ref[:, 128:256] = zc.astype(BF)
-        p = dot(c_ref[...], wc6_ref[...])
+
+    def coarse_sums(p):
         t = [p[:, 128 * i : 128 * i + 128] for i in range(6)]
         xc = row_down(t[0]) + t[1] + row_up(t[2]) + in_rows(row_down(t[3]) + t[4] + row_up(t[5]), shift_up)
         xc_ref[...] = xc
         xm = xc * mc_ref[...]
         return tile_sum(xm), tile_sum(xm * xm)
 
-    def conv_rows(first, last):
-        total = None
-        for dy in range(3):
-            p = dot(s_ref[48 * (first + dy) : 48 * (last + dy), :], wf_ref[768 * dy : 768 * dy + 768, :])
-            total = p if total is None else total + p
-        x_ref[48 * first : 48 * last, :] = total
-        xm = total * twice(mf_ref[48 * first : 48 * last, :])
-        return tile_sum(xm), tile_sum(xm * xm)
+    def conv_units(units):
+        products = []
+        for i in range(4):
+            total = None
+            for dy in range(3):
+                rows = [u_ref[i, 48 * (first + dy) : 48 * (last + dy), :] for first, last in units]
+                rows = rows[0] if len(rows) == 1 else jnp.concatenate(rows, axis=0)
+                at = 768 * i + 256 * dy
+                p = dot(rows, wf_ref[at : at + 256, :])
+                total = p if total is None else total + p
+            products.append(total)
+        m0, m1, m2, m3 = products
+        even, odd = m0 + m1 + m2, m1 - m2 - m3
+        s = q = None
+        for n, r in enumerate(r for first, last in units for r in range(first, last)):
+            for p, y in enumerate((even, odd)):
+                y = y[48 * n : 48 * n + 48]
+                at = slice(96 * r + 48 * p, 96 * r + 48 * p + 48)
+                x_ref[at, :] = y
+                ym = y * twice(mf_ref[at, :])
+                ds, dq = tile_sum(ym), tile_sum(ym * ym)
+                s, q = (ds, dq) if s is None else (s + ds, q + dq)
+        return s, q
 
     def finish(s, q, width, n, gain, bias, to_ref):
         s, q = jnp.sum(s, axis=0, keepdims=True), jnp.sum(q, axis=0, keepdims=True)
@@ -233,25 +284,40 @@
             to_ref[3:4, at] = inv
 
     def iterate(t, _):
-        branch_c = coarse_branch()
-        s = q = None
-        for g in range(12):
-            fine_rows(g, False)
-            ds, dq = conv_rows(4 * g - 1 if g else 0, 4 * g + 3 if g < 11 else 48)
-            s, q = (ds, dq) if s is None else (s + ds, q + dq)
-        sums_c = coarse_step(branch_c)
+        s = q = parts = conv_c = sums_c = None
+        for step in STEPS.split():
+            n = int(step[1:] or 0)
+            if step[0] == "E":
+                unit(2 * n, False)
+                unit(2 * n + 1, False)
+            elif step[0] == "C":
+                units = ((4 * n + 1, 4 * n + 5),) if n < 5 else ((21, 24), (0, 1))
+                ds, dq = conv_units(units)
+                s, q = (ds, dq) if s is None else (s + ds, q + dq)
+            elif step == "L":
+                parts = lowered_parts()
+            elif step == "Z":
+                coarse_state(parts)
+            elif step == "K":
+                conv_c = dot(c_ref[...], wc6_ref[...])
+            elif step == "S":
+                sums_c = coarse_sums(conv_c)
+            elif step == "F":
+                finish(*sums_c, C2 // GROUPS, nc, gain_c, bias_c, scc_ref)
+            elif step == "B":
+                coarse_branch()
         finish(s, q, C1 // GROUPS, nf, gain_f, bias_f, scf_ref)
-        finish(*sums_c, C2 // GROUPS, nc, gain_c, bias_c, scc_ref)
         return 0
 
+    coarse_branch()
     lax.fori_loop(0, ITERS, iterate, 0)
-    branch_c = coarse_branch()
-
-    def fine_last(g, _):
-        fine_rows(g, True)
+
+    def last_rows(r, _):
+        unit(2 * r, True)
+        unit(2 * r + 1, True)
         return 0
 
-    lax.fori_loop(0, 12, fine_last, 0, unroll=2)
+    lax.fori_loop(0, 12, last_rows, 0)
     sends = [
         pltpu.make_async_copy(stage_ref.at[i, p], ref.at[:, 128 * p : 128 * p + 128], out_sem.at[i, p])
         for i, ref in enumerate((outf_ref, gif_ref))
@@ -262,33 +328,30 @@
     ]
     sends[0].start()
     sends[1].start()
-    small_ref[0] = (branch_c.astype(F32) + lowered()) * mc_ref[...]
+    small_ref[0] = image_order((branch_ref[...].astype(F32) + lowered(lowered_parts())) * mc_ref[...])
     sends[4].start()
     for load in loads[6:]:
         load.wait()
 
-    seed_c = upc_ref[...].astype(F32) * mc_ref[...]
+    v = upc_ref[...].astype(F32)
+    seed_c = pair_order([v[24 * r : 24 * r + 24] for r in range(24)]) * mc_ref[...]
     right = in_rows(seed_c, shift_up)
     glo_ref[:, 0:128] = seed_c.astype(BF)
     glo_ref[:, 128:256] = right.astype(BF)
     glo_ref[:, 256:384] = row_up(seed_c).astype(BF)
     glo_ref[:, 384:512] = row_up(right).astype(BF)
 
-    def fold(g, _):
-        both = []
-        for i in range(2):
-            total = None
-            for j in range(2):
-                at = rows_of(4 * g + 2 * i + j, 48, 48)
-                seed = upf_ref[at, :].astype(F32) * twice(mf_ref[at, :])
-                part = seed[0:24] + seed[24:48]
-                total = part if total is None else total + part
-            both.append(total)
-        gl_ref[rows_of(g, 48, 48), :] = jnp.concatenate(both, axis=0).astype(BF)
+    def fold(j, _):
+        total = None
+        for i in range(4):
+            at = rows_of(4 * j + i, 48, 48)
+            seed = upf_ref[at, :].astype(F32) * twice(mf_ref[at, :])
+            total = seed if total is None else total + seed
+        gl_ref[rows_of(j, 48, 48), :] = total.astype(BF)
         return 0
 
     lax.fori_loop(0, 12, fold, 0, unroll=2)
-    up_grad = dot_rows(branch_c, gl_ref[...])
+    up_grad = dot_rows(branch_ref[...], gl_ref[...])
     for j in range(2):
         grad_ref[pl.ds(ROW_UP + j, 128, stride=2), :] = up_grad[:, 128 * j : 128 * j + 128]
     g00, g01, g10, g11 = (glo_ref[:, 128 * i : 128 * i + 128] for i in range(4))
@@ -300,7 +363,7 @@
             grad_ref[pl.ds(ROW_DOWN + tap, 256, stride=9), :] = down[:, 128 * n : 128 * n + 128]
 
     back_c = (seed_c + dot_lanes(gl_ref[...], wu_ref[...])) * mc_ref[...]
-    small_ref[1] = back_c
+    small_ref[1] = image_order(back_c)
     sends[5].start()
 
     def pre_grad(gi, x, scale, shift, mean, inv):
@@ -336,26 +399,27 @@
     back_ref[2] = dot_lanes(jnp.concatenate([g00, g10], axis=1), wdn_ref[:, 384:640])
     back_ref[3] = dot_lanes(glo_ref[...], wdn_ref[:, 640:1152])
 
-    def fine_back(i, carry):
+    def fine_back(j, carry):
         sums = list(carry)
-        for j in range(2):
-            r = 2 * i + j
-            at = rows_of(r, 48, 48)
-            half = rows_of(i, 24, 24)
-            m = twice(mf_ref[at, :])
-            back = jnp.concatenate([back_ref[2 * j, half, :], back_ref[2 * j + 1, half, :]], axis=0)
-            gi = (upf_ref[at, :].astype(F32) + back) * m
-            interleave(stage_ref.at[1], r, gi[0:24], gi[24:48])
-            gp, normed = pre_grad(
-                gi, x_ref[at, :], scf_ref[0:1, :], scf_ref[1:2, :], scf_ref[2:3, :], scf_ref[3:4, :]
-            )
-            gp_ref[at, :] = gp
-            sums[0] = sums[0] + tile_sum(gp * normed)
-            sums[1] = sums[1] + tile_sum(gp)
+        for i in range(2):
+            gi = []
+            for p in range(2):
+                at = rows_of(4 * j + 2 * i + p, 48, 48)
+                back = back_ref[2 * i + p, rows_of(j, 48, 48), :]
+                gi.append((upf_ref[at, :].astype(F32) + back) * twice(mf_ref[at, :]))
+                gp, normed = pre_grad(
+                    gi[p], x_ref[at, :], scf_ref[0:1, :], scf_ref[1:2, :], scf_ref[2:3, :], scf_ref[3:4, :]
+                )
+                gp_ref[at, :] = gp
+                sums[0] = sums[0] + tile_sum(gp * normed)
+                sums[1] = sums[1] + tile_sum(gp)
+            for n in range(2):
+                half = slice(24 * n, 24 * n + 24)
+                interleave(stage_ref.at[1], 2 * j + i + 24 * n, gi[0][half], gi[1][half])
         return tuple(sums)
 
     none8 = jnp.zeros((8, 256), F32)
-    sum_gain, sum_bias = lax.fori_loop(0, 24, fine_back, (none8, none8), unroll=2)
+    sum_gain, sum_bias = lax.fori_loop(0, 12, fine_back, (none8, none8))
     sends[2].start()
     sends[3].start()
     sum_gain = jnp.sum(sum_gain, axis=0, keepdims=True)
@@ -369,19 +433,29 @@
         )
 
     def fine_conv_grad(r, _):
-        at = rows_of(r, 48, 48)
-        normed = (x_ref[at, :] - scf_ref[2:3, :]) * scf_ref[3:4, :]
-        g = (gp_ref[at, :] * gain_f - row_ref[0:1, :] - normed * row_ref[1:2, :]) * scf_ref[3:4, :]
-        g_ref[rows_of(r + 1, 48, 48), :] = (g * twice(mf_ref[at, :])).astype(BF)
+        g = []
+        for p in range(2):
+            at = rows_of(2 * r + p, 48, 48)
+            normed = (x_ref[at, :] - scf_ref[2:3, :]) * scf_ref[3:4, :]
+            v = (gp_ref[at, :] * gain_f - row_ref[0:1, :] - normed * row_ref[1:2, :]) * scf_ref[3:4, :]
+            g.append(v * twice(mf_ref[at, :]))
+        even, odd = g
+        for i, v in enumerate((even, even + odd, even - odd, -odd)):
+            g_ref[i, rows_of(r + 2, 48, 48), :] = v.astype(BF)
         return 0
 
-    lax.fori_loop(0, 48, fine_conv_grad, 0, unroll=2)
-    for dx in range(3):
-        states = s_ref[48:2352, 256 * dx : 256 * dx + 256]
+    lax.fori_loop(0, 24, fine_conv_grad, 0, unroll=2)
+    products = []
+    for i in range(4):
+        shifted = [g_ref[i, 48 * (2 - dy) : 48 * (2 - dy) + 26 * 48, :] for dy in range(3)]
+        products.append(dot_rows(u_ref[i], jnp.concatenate(shifted, axis=1)))
+    p0, p1, p2, p3 = products
+    both, apart = 0.5 * (p1 + p2), 0.5 * (p1 - p2)
+    for dx, grad in enumerate((p0 + both, apart, both + p3)):
         for dy in range(3):
-            grad = dot_rows(states, g_ref[48 * (2 - dy) : 48 * (2 - dy) + 2304, :])
             for j in range(2):
-                grad_ref[pl.ds(2 * (3 * dy + dx) + j, 256, stride=18), :] = grad[:, 128 * j : 128 * j + 128]
+                at = 256 * dy + 128 * j
+                grad_ref[pl.ds(2 * (3 * dy + dx) + j, 256, stride=18), :] = grad[:, at : at + 128]
     for n, first in enumerate(plan.first):
         block_ref[n] = grad_ref[first : first + plan.rows, :].astype(BF)
         send = pltpu.make_async_copy(block_ref.at[n], blocks_ref.at[n], block_sem.at[n])
@@ -407,13 +481,14 @@
         in_specs=[pl.BlockSpec(memory_space=pltpu.SMEM), pl.BlockSpec(memory_space=pltpu.VMEM)] + [there] * 8,
         out_specs=[there] * 5,
         scratch_shapes=[
-            low(PIX, 256), low(CPIX, 128), low(128, 256), low(256, 1152), low(256, 768), low(9 * 256, 256),
+            low(PIX, 256), low(CPIX, 128), low(128, 256), low(256, 1152), low(256, 768), low(12 * 256, 256),
             low(PIX, 256), low(CPIX, 128),
             wide(plan.tall, 128), low(plan.n, plan.rows, 128),
-            low(2400, 768), low(4, CPIX, 256), low(CPIX, 256),
-            wide(PIX, 256), wide(CPIX, 128), wide(CPIX, 256), wide(PIX, 128), wide(CPIX, 128),
+            low(4, 26 * 48, 256), low(4, CPIX, 256), low(CPIX, 256),
+            wide(PIX, 256), wide(CPIX, 128), wide(CPIX, 128), low(CPIX, 128), wide(CPIX, 256),
+            wide(PIX, 128), low(PIX, 128), wide(CPIX, 128),
             wide(8, 256), wide(8, 128),
-            low(CPIX, 256), low(CPIX, 512), wide(4, CPIX, 256), wide(PIX, 256), low(2400, 256), wide(8, 256),
+            low(CPIX, 256), low(CPIX, 512), wide(4, CPIX, 256), wide(PIX, 256), low(4, 28 * 48, 256), wide(8, 256),
             wide(2, 2, PIX, 128), wide(2, CPIX, 128),
             pltpu.SemaphoreType.DMA((8,)),
             pltpu.SemaphoreType.DMA((2, 2)),
@@ -564,17 +639,20 @@
 
     def parity(src, dst):
         def one(r, _):
-            at = rows_of(r, 48, 48)
-            v = src[at, :].astype(F32)
-            for p in range(2):
-                tmp_ref[p, at, :] = v[:, 128 * p : 128 * p + 128]
-            even = [tmp_ref[p, pl.ds(r * 48, 24, stride=2), :] for p in range(2)]
-            odd = [tmp_ref[p, pl.ds(r * 48 + 1, 24, stride=2), :] for p in range(2)]
-            both = [jnp.concatenate(even, axis=1), jnp.concatenate(odd, axis=1)]
-            dst[at, :] = jnp.concatenate(both, axis=0).astype(BF)
+            parts = []
+            for n in range(2):
+                at = rows_of(r + 24 * n, 48, 48)
+                v = src[at, :].astype(F32)
+                for p in range(2):
+                    tmp_ref[p, at, :] = v[:, 128 * p : 128 * p + 128]
+            for first in range(2):
+                for n in range(2):
+                    at = pl.ds((r + 24 * n) * 48 + first, 24, stride=2)
+                    parts.append(jnp.concatenate([tmp_ref[p, at, :] for p in range(2)], axis=1))
+            dst[rows_of(r, 96, 96), :] = jnp.concatenate(parts, axis=0).astype(BF)
             return 0
 
-        lax.fori_loop(0, 48, one, 0, unroll=4)
+        lax.fori_loop(0, 24, one, 0, unroll=2)
 
     outs = []
 
@@ -615,11 +693,14 @@
             w_ref[0 : plan.rows, :] = v
     vec_ref[...] = w_ref[ROW_VEC : ROW_VEC + 8, :]
     put(vec_ref, vec_hbm)
-    for t in range(9):
-        at = slice(256 * t, 256 * t + 256)
+    for dy in range(3):
         for h in range(2):
-            wf_ref[at, 128 * h : 128 * h + 128] = w_ref[pl.ds(2 * t + h, 256, stride=18), :].astype(BF)
-        put(wf_ref.at[at], wf_hbm.at[at])
+            g0, g1, g2 = (w_ref[pl.ds(2 * (3 * dy + dx) + h, 256, stride=18), :] for dx in range(3))
+            outer = g0 + g2
+            for i, v in enumerate((g0, 0.5 * (outer + g1), 0.5 * (outer - g1), g2)):
+                at = 768 * i + 256 * dy
+                wf_ref[at : at + 256, 128 * h : 128 * h + 128] = v.astype(BF)
+    put(wf_ref, wf_hbm)
     for h in range(2):
         wu_ref[:, 128 * h : 128 * h + 128] = w_ref[pl.ds(ROW_UP + h, 128, stride=2), :].astype(BF)
     put(wu_ref, wu_hbm)
@@ -644,7 +725,7 @@
     low = lambda *shape: jax.ShapeDtypeStruct(shape, BF)
     outs = [
         jax.ShapeDtypeStruct((8, 128), F32), low(PIX, 256), low(PIX, 256), low(128, 256), low(256, 1152),
-        low(256, 768), low(9 * 256, 256),
+        low(256, 768), low(12 * 256, 256),
     ]
     d0, d1, d2 = plan.dims
     sems = pltpu.SemaphoreType.DMA

time: 121 us -> 110 us (0.909)
  Pallas kernels: 116 us -> 105 us
    pallas_call x1, Pallas kernels: 67 us -> 55.5 us  [layer_call(): pl.pallas_call(functools.partial(layer_kernel, plan), out_shape=[jax.Shap...]
where the time goes in v4:
time: 110 us
  Pallas kernels  105 us (95%)
  local copies, waits for them, and re-layouts  2.81 us (3%)
  other arithmetic  1.13 us (1%)
    pallas_call x1, Pallas kernels, layer_call(): pl.pallas_call(functools.partial(layer_kernel, plan), out_shape=[jax.Shap...  55.5 us
    pallas_call x1, Pallas kernels, reduce_call(): pl.pallas_call(functools.partial(reduce_kernel, plan), out_shape=[jax.Sha...  26.8 us
    pallas_call x1, Pallas kernels, gather_call(): pl.pallas_call(functools.partial(gather_kernel, plan), out_shape=[pltpu.H...  22.8 us

profile of v4, /device:TPU:0, one launch (start us, length us, event | category | flops | bytes accessed | tf_op | source)
XLA Modules:
  0.0 109.7 jit_solution(7787266502278509395)
XLA Ops:
  0.6 1.7 %pad_bitcast_fusion.master_hbm = f32[544,128]{1,0:T(8,128)} fusion(f32[66608]{0:T(1024)} %param.14), kind=kLoop, calls=%fused_computation.1 | loop fusion | bytes 544960 | tf_op jit(solution)/shard_map/reshape | solution.py:947
  2.3 22.8 %gather_weights.1 = (f32[8,128]{1,0:T(8,128)}, bf16[2304,256]{1,0:T(8,128)(2,1)}, bf16[2304,256]{1,0:T(8,128)(2,1)}, bf16[128,256]{1,0:T(8,128)(2,1)}, bf16[256,...) custom-call(f32[544,128]{1,0:T(8,128)} %pad_bitcast_fusion.master_hbm, ...), custom_call_target="tpu_custom_call" | custom-call | tf_op jit(solution)/shard_map/gather_weights/pallas_call | solution.py:732
  25.1 55.5 %layer.1 = (f32[2304,256]{1,0:T(8,128)}, f32[576,128]{1,0:T(8,128)}, f32[2304,256]{1,0:T(8,128)}, f32[576,128]{1,0:T(8,128)}, bf16[16,544,128]{2,1,0:T(8,128)(2,1)}) custom-call(s32[1,2]{1,0:T(1,128)} %ext_ref.1, f32[8,128]{1,0:T(8,128)} %get-tuple-element.24.vec_ref, bf16[2304,256]{1,0:T(8,128)(2,1)} %get-tuple-element.25.inp_hbm, ...), custom_call_target="tpu_custom_call" | custom-call | tf_op jit(solution)/shard_map/layer/pallas_call | solution.py:472
  80.6 0.0 copy-start
  80.6 0.0 copy-start.1
  80.6 0.0 copy-start.2
  80.6 0.0 copy-start.3
  80.7 26.8 %reduce_gradients.1 = (f32[544,128]{1,0:T(8,128)S(1)}, f32[8,128]{1,0:T(8,128)S(1)}) custom-call(bf16[16,544,128]{2,1,0:T(8,128)(2,1)} %get-tuple-element.35.p_hbm), custom_call_target="tpu_custom_call" | custom-call | tf_op jit(solution)/shard_map/reduce_gradients/pallas_call | solution.py:931
  107.5 0.5 slice.9
  108.0 0.6 slice_bitcast_fusion
  108.6 0.0 copy-done
  108.6 0.0 copy-done.1
  108.6 0.0 copy-done.2
  108.6 0.0 copy-done.3
  108.6 1.1 %multiply_add_fusion = (f32[66608]{0:T(1024)}, f32[66608]{0:T(1024)}, f32[66608]{0:T(1024)}, f32[66608]{0:T(1024)}) fusion(f32[66608]{0:T(1024)S(1)} %copy-done.1, f32[66608]{0:T(1024)S(1)} %copy-done, f32[69632]{0:T(1024)S(1)} %bitcast.14, f32[66608]{0:T(1024)S(1)} %copy-done.2, f32[66608]{0:T(1024)S(1)} %copy-done.3), kind=kLoop, calls=%fused_computation.3 | loop fusion | flops 1198944 | bytes 2397888 | tf_op jit(solution)/shard_map/add | solution.py:967
Async XLA Ops:
  80.6 28.0 %copy-start = (f32[66608]{0:T(1024)S(1)}, f32[66608]{0:T(1024)}, u32[]{:S(2)}) copy-start(f32[66608]{0:T(1024)} %param.14) | copy-start | bytes 799300
  80.6 28.0 %copy-start.1 = (f32[66608]{0:T(1024)S(1)}, f32[66608]{0:T(1024)}, u32[]{:S(2)}) copy-start(f32[66608]{0:T(1024)} %param.17) | copy-start | bytes 799300
  80.6 28.0 %copy-start.2 = (f32[66608]{0:T(1024)S(1)}, f32[66608]{0:T(1024)}, u32[]{:S(2)}) copy-start(f32[66608]{0:T(1024)} %param.15) | copy-start | bytes 799300
  80.6 27.9 %copy-start.3 = (f32[66608]{0:T(1024)S(1)}, f32[66608]{0:T(1024)}, u32[]{:S(2)}) copy-start(f32[66608]{0:T(1024)} %param.16) | copy-start | bytes 799300

commit v5 on v4

--- a/solution.py
+++ b/solution.py
@@ -113,17 +113,17 @@
     return pl.ds(start if isinstance(r, int) else pl.multiple_of(start, unit if unit % 16 == 0 else 8), count)
 
 
-STEPS = "E0 E1 E2 C0 E3 E4 E5 C1 E6 E7 E8 C2 E9 E10 E11 C3 L C4 Z K C5 S F B"
+STEPS = "E0 E1 E2 E3 C1-7 E4 E5 E6 C7-13 E7 E8 E9 E10 E11 C13-17 L C17-21 Z K C21-24,0-1 S F B"
 
 
 def layer_kernel(
     plan,
     ext_ref, vec_ref, inp_hbm, inc_hbm, wu_hbm, wdn_hbm, wc6_hbm, wf_hbm, upf_hbm, upc_hbm,
-    outf_ref, outc_ref, gif_ref, gic_ref, blocks_ref,
+    outf_ref, outc_ref, gif_ref, gic_ref, uo_ref, go_ref, join_ref, blocks_ref,
     inp_ref, inc_in, wu_ref, wdn_ref, wc6_ref, wf_ref, upf_ref, upc_ref,
     grad_ref, block_ref, u_ref, ph_ref, c_ref, x_ref, xc_ref, inc_ref, branch_ref, lift_ref, mf_ref, mb_ref, mc_ref,
     scf_ref, scc_ref, gl_ref, glo_ref, back_ref, gp_ref, g_ref, row_ref, stage_ref, small_ref,
-    in_sem, out_sem, block_sem, small_sem,
+    in_sem, out_sem, hand_sem, small_sem,
 ):
     loads = [
         pltpu.make_async_copy(src, dst, in_sem.at[n])
@@ -164,8 +164,8 @@
     lax.fori_loop(0, 12, setup_coarse, 0)
     nf = (hh * ww).astype(F32) * (C1 // GROUPS)
     nc = (((hh + 1) // 2) * ((ww + 1) // 2)).astype(F32) * (C2 // GROUPS)
-    g_ref[:, 0:96, :] = jnp.zeros((4, 96, 256), BF)
-    g_ref[:, 26 * 48 : 28 * 48, :] = jnp.zeros((4, 96, 256), BF)
+    g_ref[:, 0:96, :] = jnp.zeros((2, 96, 256), BF)
+    g_ref[:, 26 * 48 : 28 * 48, :] = jnp.zeros((2, 96, 256), BF)
     grad_ref[FLAT_ROWS:, :] = jnp.zeros((plan.tall - FLAT_ROWS, 128), F32)
     xc_ref[...] = jnp.zeros((576, 128), F32)
     scf_ref[...] = jnp.zeros((8, 256), F32)
@@ -223,8 +223,8 @@
                 w = u.astype(F32)
                 u_ref[i, 0:48, :] = jnp.concatenate([jnp.zeros_like(w[0:24]), w[0:24]], axis=0).astype(BF)
 
-    def lowered_parts():
-        ee, eo, oe, oo = (ph_ref[i] for i in range(4))
+    def lowered_parts(first=0, last=CPIX):
+        ee, eo, oe, oo = (ph_ref[i, first:last, :] for i in range(4))
         p = dot(eo, wdn_ref[:, 128:384]) + dot(oo, wdn_ref[:, 640:896])
         q = dot(oe, wdn_ref[:, 384:640])
         t = dot(oo, wdn_ref[:, 896:1152])
@@ -286,16 +286,18 @@
     def iterate(t, _):
         s = q = parts = conv_c = sums_c = None
         for step in STEPS.split():
-            n = int(step[1:] or 0)
             if step[0] == "E":
-                unit(2 * n, False)
-                unit(2 * n + 1, False)
+                unit(2 * int(step[1:]), False)
+                unit(2 * int(step[1:]) + 1, False)
             elif step[0] == "C":
-                units = ((4 * n + 1, 4 * n + 5),) if n < 5 else ((21, 24), (0, 1))
-                ds, dq = conv_units(units)
+                ds, dq = conv_units([tuple(map(int, piece.split("-"))) for piece in step[1:].split(",")])
                 s, q = (ds, dq) if s is None else (s + ds, q + dq)
             elif step == "L":
                 parts = lowered_parts()
+            elif step == "L0":
+                parts = lowered_parts(0, 288)
+            elif step == "L1":
+                parts = [jnp.concatenate(both, axis=0) for both in zip(parts, lowered_parts(288, 576))]
             elif step == "Z":
                 coarse_state(parts)
             elif step == "K":
@@ -328,6 +330,13 @@
     ]
     sends[0].start()
     sends[1].start()
+
+    def hand(src, dst):
+        send = pltpu.make_async_copy(src, dst, hand_sem.at[len(sends) - 6])
+        send.start()
+        sends.append(send)
+
+    hand(u_ref, uo_ref)
     small_ref[0] = image_order((branch_ref[...].astype(F32) + lowered(lowered_parts())) * mc_ref[...])
     sends[4].start()
     for load in loads[6:]:
@@ -439,28 +448,19 @@
             normed = (x_ref[at, :] - scf_ref[2:3, :]) * scf_ref[3:4, :]
             v = (gp_ref[at, :] * gain_f - row_ref[0:1, :] - normed * row_ref[1:2, :]) * scf_ref[3:4, :]
             g.append(v * twice(mf_ref[at, :]))
-        even, odd = g
-        for i, v in enumerate((even, even + odd, even - odd, -odd)):
-            g_ref[i, rows_of(r + 2, 48, 48), :] = v.astype(BF)
+        for p in range(2):
+            g_ref[p, rows_of(r + 2, 48, 48), :] = g[p].astype(BF)
         return 0
 
-    lax.fori_loop(0, 24, fine_conv_grad, 0, unroll=2)
-    products = []
-    for i in range(4):
-        shifted = [g_ref[i, 48 * (2 - dy) : 48 * (2 - dy) + 26 * 48, :] for dy in range(3)]
-        products.append(dot_rows(u_ref[i], jnp.concatenate(shifted, axis=1)))
-    p0, p1, p2, p3 = products
-    both, apart = 0.5 * (p1 + p2), 0.5 * (p1 - p2)
-    for dx, grad in enumerate((p0 + both, apart, both + p3)):
-        for dy in range(3):
-            for j in range(2):
-                at = 256 * dy + 128 * j
-                grad_ref[pl.ds(2 * (3 * dy + dx) + j, 256, stride=18), :] = grad[:, at : at + 128]
-    for n, first in enumerate(plan.first):
+    for n in range(2):
+        lax.fori_loop(12 * n, 12 * n + 12, fine_conv_grad, 0, unroll=2)
+        at = pl.ds(14 * 48 * n, 14 * 48)
+        hand(g_ref.at[:, at], go_ref.at[:, at])
+    hand(grad_ref.at[pl.ds(ROW_DOWN, plan.rows)], join_ref)
+    for n, s in enumerate(plan.early):
+        first = plan.first[s]
         block_ref[n] = grad_ref[first : first + plan.rows, :].astype(BF)
-        send = pltpu.make_async_copy(block_ref.at[n], blocks_ref.at[n], block_sem.at[n])
-        send.start()
-        sends.append(send)
+        hand(block_ref.at[n], blocks_ref.at[n])
     for send in sends:
         send.wait()
 
@@ -476,23 +476,23 @@
             jax.ShapeDtypeStruct((CPIX, 128), F32),
             jax.ShapeDtypeStruct((PIX, 256), F32),
             jax.ShapeDtypeStruct((CPIX, 128), F32),
-            jax.ShapeDtypeStruct((plan.n, plan.rows, 128), BF),
+            *(pltpu.HBM(shape, dtype) for shape, dtype in plan.handed),
         ],
         in_specs=[pl.BlockSpec(memory_space=pltpu.SMEM), pl.BlockSpec(memory_space=pltpu.VMEM)] + [there] * 8,
-        out_specs=[there] * 5,
+        out_specs=[there] * 8,
         scratch_shapes=[
             low(PIX, 256), low(CPIX, 128), low(128, 256), low(256, 1152), low(256, 768), low(12 * 256, 256),
             low(PIX, 256), low(CPIX, 128),
-            wide(plan.tall, 128), low(plan.n, plan.rows, 128),
+            wide(plan.tall, 128), low(len(plan.early), plan.rows, 128),
             low(4, 26 * 48, 256), low(4, CPIX, 256), low(CPIX, 256),
             wide(PIX, 256), wide(CPIX, 128), wide(CPIX, 128), low(CPIX, 128), wide(CPIX, 256),
             wide(PIX, 128), low(PIX, 128), wide(CPIX, 128),
             wide(8, 256), wide(8, 128),
-            low(CPIX, 256), low(CPIX, 512), wide(4, CPIX, 256), wide(PIX, 256), low(4, 28 * 48, 256), wide(8, 256),
+            low(CPIX, 256), low(CPIX, 512), wide(4, CPIX, 256), wide(PIX, 256), low(2, 28 * 48, 256), wide(8, 256),
             wide(2, 2, PIX, 128), wide(2, CPIX, 128),
             pltpu.SemaphoreType.DMA((8,)),
             pltpu.SemaphoreType.DMA((2, 2)),
-            pltpu.SemaphoreType.DMA((plan.n,)),
+            pltpu.SemaphoreType.DMA((plan.n + 4,)),
             pltpu.SemaphoreType.DMA((2,)),
         ],
         compiler_params=pltpu.CompilerParams(vmem_limit_bytes=62 * 2**20),
@@ -510,6 +510,11 @@
         self.part = self.rows // 2
         self.cut = -(-self.part // 32) * 16
         self.tall = -(-(self.first[-1] + self.rows) // 16) * 16
+        self.early = [s for s in range(shards) if self.first[s] >= ROW_DOWN]
+        self.handed = (
+            ((4, 26 * 48, 256), BF), ((2, 28 * 48, 256), BF), ((self.rows, 128), F32),
+            ((len(self.early), self.rows, 128), BF),
+        )
 
     def here(self):
         d0, d1, d2 = self.dims
@@ -530,11 +535,23 @@
     return a
 
 
+def to_rows(plan, ref):
+    full = plan.length // 128
+    left = plan.length - 128 * full
+    parts = [ref[pl.ds(0, 128 * full)].reshape(full, 128)]
+    if left:
+        tail = ref[pl.ds(128 * full, left)].reshape(1, left)
+        parts.append(jnp.concatenate([tail, jnp.zeros((1, 128 - left), F32)], axis=1))
+    have = full + (left > 0)
+    parts.append(jnp.zeros((plan.rows - have, 128), F32))
+    return jnp.concatenate(parts, axis=0)
+
+
 def gather_kernel(
     plan,
-    master_hbm, inp_hbm, upf_hbm,
+    master_ref, inp_hbm, upf_hbm,
     vec_hbm, inpo_hbm, upfo_hbm, wu_hbm, wdn_hbm, wc6_hbm, wf_hbm,
-    master_ref, inp_ref, upf_ref, vec_ref, inpo_ref, upfo_ref, wu_ref, wdn_ref, wc6_ref, wf_ref,
+    inp_ref, upf_ref, vec_ref, inpo_ref, upfo_ref, wu_ref, wdn_ref, wc6_ref, wf_ref,
     g_ref, w_ref, tmp_ref, in_sem, out_sem, send_sem, recv_sem, sib_send, sib_recv, far_send,
 ):
     d0, d1, d2 = plan.dims
@@ -542,7 +559,7 @@
     part, cut = plan.part, plan.cut
     loads = [
         pltpu.make_async_copy(src, dst, in_sem.at[n])
-        for n, (src, dst) in enumerate(((master_hbm, master_ref), (inp_hbm, inp_ref), (upf_hbm, upf_ref)))
+        for n, (src, dst) in enumerate(((inp_hbm, inp_ref), (upf_hbm, upf_ref)))
     ]
     for load in loads:
         load.start()
@@ -553,9 +570,8 @@
     others = [{"fsdp": other, "rep": core} for other in others] + [{"fsdp": me, "rep": 1 - core}]
     for other in others:
         pl.semaphore_signal(barrier, inc=1, device_id=other, device_id_type=pl.DeviceIdType.MESH)
-    loads[0].wait()
     off = (me * plan.length) % 128
-    x = pltpu.roll(master_ref[...], off, 1)
+    x = pltpu.roll(to_rows(plan, master_ref), off, 1)
     row = lax.broadcasted_iota(jnp.int32, x.shape, 0)
     lane = lax.broadcasted_iota(jnp.int32, x.shape, 1)
     above = jnp.where(row == 0, 0.0, pltpu.roll(x, 1, 0))
@@ -665,10 +681,10 @@
         for half in (0, 1):
             go(copy(me, half, plan.block(flip(a, k), b, c), core, far_send.at[k, half], recv_sem.at[me, half], core))
     own_column(0)
-    loads[1].wait()
+    loads[0].wait()
     parity(inp_ref, inpo_ref)
     put(inpo_ref, inpo_hbm)
-    loads[2].wait()
+    loads[1].wait()
     parity(upf_ref, upfo_ref)
     put(upfo_ref, upfo_hbm)
     for k in range(1, d0):
@@ -732,33 +748,35 @@
     return pl.pallas_call(
         functools.partial(gather_kernel, plan),
         out_shape=[pltpu.HBM(o.shape, o.dtype) for o in outs],
-        in_specs=[there] * 3,
+        in_specs=[pl.BlockSpec(memory_space=pltpu.VMEM), there, there],
         out_specs=[there] * 7,
-        scratch_shapes=[pltpu.VMEM((plan.rows, 128), F32), pltpu.VMEM((PIX, 256), BF), pltpu.VMEM((PIX, 256), BF)]
+        scratch_shapes=[pltpu.VMEM((PIX, 256), BF), pltpu.VMEM((PIX, 256), BF)]
         + [pltpu.VMEM(o.shape, o.dtype) for o in outs]
         + [
             pltpu.VMEM((plan.n, plan.rows, 128), BF), pltpu.VMEM((plan.tall, 128), F32), pltpu.VMEM((2, PIX, 128), F32),
-            sems((3,)), sems((15,)), sems((plan.n, 2, max(d1 + d2 - 2, 1))), sems((plan.n, 2)), sems((plan.n, 2)),
+            sems((2,)), sems((15,)), sems((plan.n, 2, max(d1 + d2 - 2, 1))), sems((plan.n, 2)), sems((plan.n, 2)),
             sems((plan.n, 2)), sems((d0, 2)),
         ],
         compiler_params=pltpu.CompilerParams(collective_id=0, has_side_effects=True, vmem_limit_bytes=32 * 2**20),
         name="gather_weights",
-    )(*(pltpu.with_memory_space_constraint(x, pltpu.HBM) for x in (master, inp, upf)))
-
-
-def reduce_kernel(plan, p_hbm, out_ref, tile_ref,
-                  p_ref, q_ref, ua_ref, ub_ref, va_ref, vb_ref, z_ref, sa_ref, total_ref, n1_ref, n2_ref,
-                  q_send, q_recv, s1_send, s1_recv, s2_send, s2_recv, s3_send, s3_recv, t_send, t_recv, n1_send, n1_recv, n2_send, n2_recv, own_sem):
+    )(master, *(pltpu.with_memory_space_constraint(x, pltpu.HBM) for x in (inp, upf)))
+
+
+def reduce_kernel(
+    plan,
+    u_hbm, g_hbm, join_hbm, blocks_hbm,
+    out_ref, tile_ref,
+    u_ref, g_ref, sums_ref, grad_ref, p_ref, q_ref, ua_ref, ub_ref, va_ref, vb_ref, z_ref, sa_ref, total_ref,
+    n1_ref, n2_ref,
+    in_sem, q_send, q_recv, s1_send, s1_recv, s2_send, s2_recv, s3_send, s3_recv, t_send, t_recv,
+    n1_send, n1_recv, n2_send, n2_recv,
+):
     d0, d1, d2 = plan.dims
     me, core, a, b, c = plan.here()
     part, cut = plan.part, plan.cut
     MESH = pl.DeviceIdType.MESH
-    mine = pl.multiple_of(core * part, 16)
-    theirs = pl.multiple_of((1 - core) * part, 16)
-    load = pltpu.make_async_copy(p_hbm.at[:, pl.ds(mine, part)], p_ref, own_sem.at[0])
-    load.start()
     barrier = pltpu.get_barrier_semaphore()
-    others = [({"fsdp": plan.block((a + k) % d0, b, c), "rep": core}) for k in range(1, d0)]
+    others = [{"fsdp": plan.block((a + k) % d0, b, c), "rep": core} for k in range(1, d0)]
     plane = []
     for i in range(d1):
         for j in range(d2):
@@ -768,34 +786,66 @@
     others += [p[3] for p in plane]
     for other in others:
         pl.semaphore_signal(barrier, inc=1, device_id=other, device_id_type=MESH)
+    loads = [pltpu.make_async_copy(g_hbm, g_ref, in_sem.at[0])]
+    loads += [pltpu.make_async_copy(u_hbm.at[i], u_ref.at[i], in_sem.at[1 + i]) for i in range(4)]
+    loads.append(pltpu.make_async_copy(join_hbm, grad_ref.at[pl.ds(ROW_DOWN, plan.rows)], in_sem.at[5]))
+    count = len(plan.early)
+    loads.append(pltpu.make_async_copy(blocks_hbm, p_ref.at[pl.ds(plan.n - count, count)], in_sem.at[6]))
+    for load in loads:
+        load.start()
+
+    loads[0].wait()
+    even, odd = g_ref[0], g_ref[1]
+    sums_ref[0] = even + odd
+    sums_ref[1] = even - odd
+    products = []
+    for i, ref in enumerate((g_ref.at[0], sums_ref.at[0], sums_ref.at[1], g_ref.at[1])):
+        shifted = [ref[48 * (2 - dy) : 48 * (2 - dy) + 26 * 48, :] for dy in range(3)]
+        loads[1 + i].wait()
+        products.append(dot_rows(u_ref[i], jnp.concatenate(shifted, axis=1)))
+    p0, p1, p2, p3 = products
+    both, apart = 0.5 * (p1 + p2), 0.5 * (p1 - p2)
+    for dx, grad in enumerate((p0 + both, apart, both - p3)):
+        for dy in range(3):
+            for j in range(2):
+                at = 256 * dy + 128 * j
+                grad_ref[pl.ds(2 * (3 * dy + dx) + j, 256, stride=18), :] = grad[:, at : at + 128]
+    loads[5].wait()
+    for s in range(plan.n - count):
+        first = plan.first[s]
+        p_ref[s] = grad_ref[first : first + plan.rows, :].astype(BF)
+    loads[6].wait()
     pl.semaphore_wait(barrier, len(others))
 
     sent = []
+
     def go(src, dst, send, recv, to):
-        d = pltpu.make_async_remote_copy(src_ref=src, dst_ref=dst, send_sem=send, recv_sem=recv, device_id=to, device_id_type=MESH)
+        d = pltpu.make_async_remote_copy(
+            src_ref=src, dst_ref=dst, send_sem=send, recv_sem=recv, device_id=to, device_id_type=MESH
+        )
         d.start()
         sent.append(d)
 
     def got(ref, recv):
         pltpu.make_async_copy(ref, ref, recv).wait()
 
+    mine = pl.multiple_of(core * part, 16)
+    theirs = pl.multiple_of((1 - core) * part, 16)
     halves = ((0, cut), (cut, part - cut))
     order = [(k + 1) % d0 for k in range(d0)]
-    spots = []
     for k in order:
         for i in list(range(1, d1)) + [0]:
             for j in list(range(1, d2)) + [0]:
-                spots.append((k, i, j))
-    for k, i, j in spots:
-        s = plan.block((a + k) % d0, (b + i) % d1, (c + j) % d2)
-        go(p_hbm.at[s, pl.ds(theirs, part)], q_ref.at[s], q_send.at[s], q_recv.at[s], {"fsdp": me, "rep": 1 - core})
-
-    load.wait()
+                s = plan.block((a + k) % d0, (b + i) % d1, (c + j) % d2)
+                go(
+                    p_ref.at[s, pl.ds(theirs, part)], q_ref.at[s], q_send.at[s], q_recv.at[s],
+                    {"fsdp": me, "rep": 1 - core},
+                )
 
     def pair(s, half):
         start, size = halves[half]
-        x = p_ref[s, start:start + size, :].astype(F32)
-        return x + q_ref[s, start:start + size, :].astype(F32)
+        x = p_ref[s, pl.ds(pl.multiple_of(mine + start, 16), size), :].astype(F32)
+        return x + q_ref[s, start : start + size, :].astype(F32)
 
     def step1(k):
         a2 = (a + k) % d0
@@ -906,65 +956,115 @@
     x = pltpu.roll(total_ref[...], (128 - off) % 128, 1)
     below = pltpu.roll(x, plan.rows - 1, 0)
     lane = lax.broadcasted_iota(jnp.int32, x.shape, 1)
-    moved = jnp.where(lane + off >= 128, below, x)
+    out_ref[...] = jnp.where(lane + off >= 128, below, x)
     for n, (i, j, o, to) in enumerate(plane):
         other = (((b + i) % d1) * d2 + (c + j) % d2) * 2 + (core + o) % 2
         got(n2_ref.at[other], n2_recv.at[other])
     tile = n2_ref[0]
     for n in range(1, 2 * d1 * d2):
         tile = tile + n2_ref[n]
-    grad_norm = jnp.sqrt(jnp.sum(tile[6:7], axis=1, keepdims=True))
-    factor = jnp.minimum(1.0, clip_norm / (grad_norm + 1e-06))
-    out_ref[...] = moved * factor
-    tile_ref[0:6, :] = tile[0:6] * factor
-    tile_ref[6:8, :] = jnp.broadcast_to(grad_norm, (2, 128))
+    tile_ref[...] = tile
     for d in sent:
         d.wait_send()
 
 
-def reduce_call(plan, grads):
-    V = pl.BlockSpec(memory_space=pltpu.VMEM)
+def reduce_call(plan, *handed):
+    whole = pl.BlockSpec(memory_space=pltpu.VMEM)
     d0, d1, d2 = plan.dims
-    D = pltpu.SemaphoreType.DMA
-    b = lambda *s: pltpu.VMEM(s, BF)
+    sems = pltpu.SemaphoreType.DMA
+    low = lambda *shape: pltpu.VMEM(shape, BF)
+    wide = lambda *shape: pltpu.VMEM(shape, F32)
     e1, e2 = max(d1 - 1, 1), max(d2 - 1, 1)
-    return pl.pallas_call(functools.partial(reduce_kernel, plan),
+    rest = plan.part - plan.cut
+    return pl.pallas_call(
+        functools.partial(reduce_kernel, plan),
         out_shape=[jax.ShapeDtypeStruct((plan.rows, 128), F32), jax.ShapeDtypeStruct((8, 128), F32)],
-        in_specs=[pl.BlockSpec(memory_space=pltpu.HBM)], out_specs=[V] * 2,
-        scratch_shapes=[b(plan.n, plan.part, 128), b(plan.n, plan.part, 128), b(d0, d2, e1, plan.cut, 128), b(d0, d1, e2, plan.part - plan.cut, 128),
-            b(d0, e2, plan.cut, 128), b(d0, e1, plan.part - plan.cut, 128), b(max(d0 - 1, 1), plan.part, 128), b(plan.n, plan.part, 128),
-            pltpu.VMEM((plan.rows, 128), F32), pltpu.VMEM((d0, 8, 128), F32), pltpu.VMEM((2 * d1 * d2, 8, 128), F32),
-            D((plan.n,)), D((plan.n,)), D((plan.n, 2)), D((2, d0, max(d1, d2), max(e1, e2))), D((2, d0, max(e1, e2))), D((2, d0, max(e1, e2))),
-            D((d0,)), D((d0,)), D((1,)), D((1,)), D((d0,)), D((d0,)), D((2 * d1 * d2,)), D((2 * d1 * d2,)), D((1,))],
-        compiler_params=pltpu.CompilerParams(collective_id=1, has_side_effects=True, vmem_limit_bytes=32 * 2**20),
-        name="reduce_gradients")(pltpu.with_memory_space_constraint(grads, pltpu.HBM))
+        in_specs=[pl.BlockSpec(memory_space=pltpu.HBM)] * 4,
+        out_specs=[whole] * 2,
+        scratch_shapes=[
+            low(4, 26 * 48, 256), low(2, 28 * 48, 256), low(2, 28 * 48, 256), wide(ROW_DOWN + plan.rows, 128),
+            low(plan.n, plan.rows, 128), low(plan.n, plan.part, 128),
+            low(d0, d2, e1, plan.cut, 128), low(d0, d1, e2, rest, 128),
+            low(d0, e2, plan.cut, 128), low(d0, e1, rest, 128), low(max(d0 - 1, 1), plan.part, 128),
+            low(plan.n, plan.part, 128),
+            wide(plan.rows, 128), wide(d0, 8, 128), wide(2 * d1 * d2, 8, 128),
+            sems((7,)), sems((plan.n,)), sems((plan.n,)), sems((plan.n, 2)),
+            sems((2, d0, max(d1, d2), max(e1, e2))), sems((2, d0, max(e1, e2))), sems((2, d0, max(e1, e2))),
+            sems((d0,)), sems((d0,)), sems((1,)), sems((1,)),
+            sems((d0,)), sems((d0,)), sems((2 * d1 * d2,)), sems((2 * d1 * d2,)),
+        ],
+        compiler_params=pltpu.CompilerParams(collective_id=1, has_side_effects=True, vmem_limit_bytes=40 * 2**20),
+        name="reduce_gradients",
+    )(*(pltpu.with_memory_space_constraint(x, pltpu.HBM) for x in handed))
+
+
+def update_kernel(
+    plan,
+    grad_ref, tile_ref, master_ref, first_ref, second_ref, average_ref,
+    norm_ref, new_master_ref, new_first_ref, new_second_ref, new_average_ref, small_ref,
+):
+    grad_norm = jnp.sqrt(jnp.sum(tile_ref[6:7, :], axis=1, keepdims=True))
+    factor = jnp.minimum(1.0, clip_norm / (grad_norm + 1e-06))
+    norm_ref[...] = grad_norm
+    for i in range(6):
+        small_ref[pl.ds(128 * i, 128)] = (tile_ref[i : i + 1, :] * factor).reshape(128)
+    full = plan.length // 128
+    left = plan.length - 128 * full
+    ema_rate = min(0.999, (1.0 + STEP) / (10.0 + STEP))
+
+    def update(row, rows, lanes):
+        at = pl.ds(128 * row, 128 * (rows - 1) + lanes)
+        shape = (rows, lanes)
+        clipped = grad_ref[row : row + rows, 0:lanes] * factor
+        new_first = beta_one * first_ref[at].reshape(shape) + (1.0 - beta_one) * clipped
+        new_second = beta_two * second_ref[at].reshape(shape) + (1.0 - beta_two) * clipped * clipped
+        corrected_first = new_first / (1.0 - beta_one**STEP)
+        corrected_second = new_second / (1.0 - beta_two**STEP)
+        master = master_ref[at].reshape(shape)
+        new_master = master - learn_rate * (
+            corrected_first / (jnp.sqrt(corrected_second) + adam_eps) + decay_rate * master
+        )
+        new_average = ema_rate * average_ref[at].reshape(shape) + (1.0 - ema_rate) * new_master
+        size = 128 * (rows - 1) + lanes
+        new_master_ref[at] = new_master.reshape(size)
+        new_first_ref[at] = new_first.reshape(size)
+        new_second_ref[at] = new_second.reshape(size)
+        new_average_ref[at] = new_average.reshape(size)
+
+    update(0, full, 128)
+    if left:
+        update(full, 1, left)
+
+
+def update_call(plan, *args):
+    whole = pl.BlockSpec(memory_space=pltpu.VMEM)
+    flat = jax.ShapeDtypeStruct((plan.length,), F32)
+    return pl.pallas_call(
+        functools.partial(update_kernel, plan),
+        out_shape=[jax.ShapeDtypeStruct((1, 1), F32), flat, flat, flat, flat, jax.ShapeDtypeStruct((768,), F32)],
+        in_specs=[whole] * 6,
+        out_specs=[whole] * 6,
+        compiler_params=pltpu.CompilerParams(vmem_limit_bytes=16 * 2**20),
+        name="update",
+    )(*args)
 
 
 def per_device(
     input_fine, input_coarse, upstream_fine, upstream_coarse, extents, master, first_moment, second_moment, average
 ):
     plan = Plan(lax.axis_size("fsdp"), master.shape[0])
-    padded = jnp.pad(master, (0, plan.rows * 128 - plan.length)).reshape(plan.rows, 128)
     vec, inp, upf, wu, wdn, wc6, wf = gather_call(
-        plan, padded, input_fine.reshape(PIX, C1), upstream_fine.reshape(PIX, C1)
+        plan, master, input_fine.reshape(PIX, C1), upstream_fine.reshape(PIX, C1)
     )
-    out_fine, out_coarse, gi_fine, gi_coarse, blocks = layer_call(
+    out_fine, out_coarse, gi_fine, gi_coarse, *handed = layer_call(
         plan, extents, vec, inp, input_coarse.reshape(CPIX, C2), wu, wdn, wc6, wf, upf,
         upstream_coarse.reshape(CPIX, C2),
     )
-    clipped, tile = reduce_call(plan, blocks)
-    clipped = clipped.reshape(-1)[: plan.length]
-    grad_norm = tile[6, 0]
-    norm_grads = tile[:6].reshape(-1)
-    new_first = beta_one * first_moment + (1.0 - beta_one) * clipped
-    new_second = beta_two * second_moment + (1.0 - beta_two) * clipped * clipped
-    corrected_first = new_first / (1.0 - beta_one**STEP)
-    corrected_second = new_second / (1.0 - beta_two**STEP)
-    new_master = master - learn_rate * (
-        corrected_first / (jnp.sqrt(corrected_second) + adam_eps) + decay_rate * master
+    grad, tile = reduce_call(plan, *handed)
+    grad_norm, new_master, new_first, new_second, new_average, norm_grads = update_call(
+        plan, grad, tile, master, first_moment, second_moment, average
     )
-    ema_rate = min(0.999, (1.0 + STEP) / (10.0 + STEP))
-    new_average = ema_rate * average + (1.0 - ema_rate) * new_master
+    grad_norm = grad_norm.reshape(())
     return (
         out_fine.reshape(input_fine.shape),
         out_coarse.reshape(input_coarse.shape),

time: 110 us -> 109 us (level)
  Pallas kernels: 105 us -> 107 us
  local copies, waits for them, and re-layouts: 2.81 us -> 0.97 us
  other arithmetic: 1.13 us -> 0 us
    pallas_call x1, Pallas kernels: 26.8 us -> 29.5 us  [reduce_call(): pl.pallas_call(functools.partial(reduce_kernel, plan), out_shape=[jax.Sha...]
    pallas_call x1, Pallas kernels: 55.5 us -> 52.8 us  [layer_call(): pl.pallas_call(functools.partial(layer_kernel, plan), out_shape=[jax.Shap...]
    reshape x2 -> x0, local copies, waits for them, and re-layouts: 2.27 us -> none  [the longest x1 1.68 us: per_device(): jnp.pad(master, (0, plan.rows * 128 - plan.length)).reshape(plan.rows, 128)]
    pallas_call x0 -> x1, Pallas kernels: none -> 1.46 us  [update_call(): pl.pallas_call(functools.partial(update_kernel, plan), out_shape=[jax.Sha...]
    add x1 -> x0, other arithmetic: 1.13 us -> none  [per_device(): new_average = ema_rate * average + (1.0 - ema_rate) * new_master]
where the time goes in v5:
time: 109 us
  Pallas kernels  107 us (98%)
    pallas_call x1, Pallas kernels, layer_call(): pl.pallas_call(functools.partial(layer_kernel, plan), out_shape=[jax.Shap...  52.8 us
    pallas_call x1, Pallas kernels, reduce_call(): pl.pallas_call(functools.partial(reduce_kernel, plan), out_shape=[jax.Sha...  29.5 us
    pallas_call x1, Pallas kernels, gather_call(): pl.pallas_call(functools.partial(gather_kernel, plan), out_shape=[pltpu.H...  23.7 us

profile of v5, /device:TPU:0, one launch (start us, length us, event | category | flops | bytes accessed | tf_op | source)
XLA Modules:
  0.0 109.2 jit_solution(1601498621060375194)
XLA Ops:
  0.6 0.0 copy-start
  0.7 0.9 copy-done
  1.6 23.7 %gather_weights.1 = (f32[8,128]{1,0:T(8,128)}, bf16[2304,256]{1,0:T(8,128)(2,1)}, bf16[2304,256]{1,0:T(8,128)(2,1)}, bf16[128,256]{1,0:T(8,128)(2,1)}, bf16[256,...) custom-call(f32[66608]{0:T(1024)S(1)} %copy-done, bf16[2304,256]{1,0:T(8,128)(2,1)} %bitcast.9, ...), custom_call_target="tpu_custom_call" | custom-call | tf_op jit(solution)/shard_map/gather_weights/pallas_call | solution.py:748
  25.3 52.8 %layer.1 = (f32[2304,256]{1,0:T(8,128)}, f32[576,128]{1,0:T(8,128)}, f32[2304,256]{1,0:T(8,128)}, f32[576,128]{1,0:T(8,128)}, bf16[4,1248,256]{2,1,0:T(8,128)(2,...) custom-call(s32[1,2]{1,0:T(1,128)} %ext_ref.1, ...), custom_call_target="tpu_custom_call" | custom-call | tf_op jit(solution)/shard_map/layer/pallas_call | solution.py:472
  78.1 0.0 copy-start.1
  78.1 0.0 copy-start.2
  78.1 0.0 copy-start.3
  78.1 0.0 copy-start.4
  78.1 29.5 %reduce_gradients.1 = (f32[544,128]{1,0:T(8,128)S(1)}, f32[8,128]{1,0:T(8,128)S(1)}) custom-call(bf16[4,1248,256]{2,1,0:T(8,128)(2,1)} %get-tuple-element.44.u_hbm, bf16[2,1344,256]{2,1,0:T(8,128)(2,1)} %get-tuple-element.45.g_hbm, f32[544,128]{1,0:T(8,128)} %get-tuple-element.46.join_hbm, bf16[7,544,128]{2,1,0:T(8,128)(2,1)} %get-tuple-element.47.blocks_hbm), custom_call_target="tpu_custom_call" | custom-call | tf_op jit(solution)/shard_map/reduce_gradients/pallas_call | solution.py:979
  107.7 0.0 copy-done.1
  107.7 0.0 copy-done.2
  107.7 0.0 copy-done.3
  107.7 0.0 copy-done.4
  107.7 1.5 %update.1 = (f32[1,1]{1,0:T(1,128)}, f32[66608]{0:T(1024)}, f32[66608]{0:T(1024)}, f32[66608]{0:T(1024)}, f32[66608]{0:T(1024)}, /*index=5*/f32[768]{0:T(1024)}) custom-call(f32[544,128]{1,0:T(8,128)S(1)} %get-tuple-element.48.grad_ref, f32[8,128]{1,0:T(8,128)S(1)} %get-tuple-element.49.tile_ref, f32[66608]{0:T(1024)S(1)} %copy-done.1, f32[66608]{0:T(1024)S(1)} %copy-done.2, ...), custom_call_target="tpu_custom_call" | custom-call | tf_op jit(solution)/shard_map/update/pallas_call | solution.py:1042
Async XLA Ops:
  0.6 1.0 copy-start
  78.1 29.6 %copy-start.1 = (f32[66608]{0:T(1024)S(1)}, f32[66608]{0:T(1024)}, u32[]{:S(2)}) copy-start(f32[66608]{0:T(1024)} %master_ref.3) | copy-start | bytes 799300
  78.1 29.6 %copy-start.2 = (f32[66608]{0:T(1024)S(1)}, f32[66608]{0:T(1024)}, u32[]{:S(2)}) copy-start(f32[66608]{0:T(1024)} %first_ref.1) | copy-start | bytes 799300
  78.1 29.6 %copy-start.3 = (f32[66608]{0:T(1024)S(1)}, f32[66608]{0:T(1024)}, u32[]{:S(2)}) copy-start(f32[66608]{0:T(1024)} %second_ref.1) | copy-start | bytes 799300
  78.1 29.6 %copy-start.4 = (f32[66608]{0:T(1024)S(1)}, f32[66608]{0:T(1024)}, u32[]{:S(2)}) copy-start(f32[66608]{0:T(1024)} %average_ref.1) | copy-start | bytes 799300

commit v6 on v5

--- a/solution.py
+++ b/solution.py
@@ -118,20 +118,16 @@
 
 def layer_kernel(
     plan,
-    ext_ref, vec_ref, inp_hbm, inc_hbm, wu_hbm, wdn_hbm, wc6_hbm, wf_hbm, upf_hbm, upc_hbm,
-    outf_ref, outc_ref, gif_ref, gic_ref, uo_ref, go_ref, join_ref, blocks_ref,
-    inp_ref, inc_in, wu_ref, wdn_ref, wc6_ref, wf_ref, upf_ref, upc_ref,
-    grad_ref, block_ref, u_ref, ph_ref, c_ref, x_ref, xc_ref, inc_ref, branch_ref, lift_ref, mf_ref, mb_ref, mc_ref,
-    scf_ref, scc_ref, gl_ref, glo_ref, back_ref, gp_ref, g_ref, row_ref, stage_ref, small_ref,
-    in_sem, out_sem, hand_sem, small_sem,
+    ext_ref, vec_ref, inp_in, wu_in, wdn_in, wc6_in, wf_in, upf_ref, inc_hbm, upc_hbm,
+    outf_ref, outc_ref, gif_ref, gic_ref, u_ref, g_ref, join_ref, blocks_ref,
+    inp_ref, wu_ref, wdn_ref, wc6_ref, wf_ref, inc_in, upc_ref, grad_ref, ph_ref, c_ref, x_ref, xc_ref, inc_ref, branch_ref, lift_ref, mf_ref, mb_ref, mc_ref,
+    scf_ref, scc_ref, gl_ref, glo_ref, back_ref, gp_ref, row_ref, stage_ref, small_ref,
+    in_sem, out_sem, small_sem,
 ):
     loads = [
         pltpu.make_async_copy(src, dst, in_sem.at[n])
         for n, (src, dst) in enumerate(
-            (
-                (inc_hbm, inc_in), (inp_hbm, inp_ref), (wu_hbm, wu_ref), (wdn_hbm, wdn_ref),
-                (wc6_hbm, wc6_ref), (wf_hbm, wf_ref), (upf_hbm, upf_ref), (upc_hbm, upc_ref),
-            )
+            ((inc_hbm, inc_in), (upc_hbm, upc_ref))
         )
     ]
     for load in loads:
@@ -172,11 +168,13 @@
     scc_ref[...] = jnp.zeros((8, 128), F32)
     scf_ref[1:2, :] = 0.5 * bias_f
     scc_ref[1:2, :] = 0.5 * bias_c
+    for src, dst in (
+        (inp_in, inp_ref), (wu_in, wu_ref), (wdn_in, wdn_ref), (wc6_in, wc6_ref), (wf_in, wf_ref)
+    ):
+        dst[...] = src[...]
     loads[0].wait()
     v = inc_in[...].astype(F32)
     inc_ref[...] = pair_order([v[24 * r : 24 * r + 24] for r in range(24)])
-    for load in loads[1:6]:
-        load.wait()
 
     def coarse_branch():
         h = xc_ref[...] * scc_ref[0:1, :] + scc_ref[1:2, :]
@@ -330,17 +328,9 @@
     ]
     sends[0].start()
     sends[1].start()
-
-    def hand(src, dst):
-        send = pltpu.make_async_copy(src, dst, hand_sem.at[len(sends) - 6])
-        send.start()
-        sends.append(send)
-
-    hand(u_ref, uo_ref)
     small_ref[0] = image_order((branch_ref[...].astype(F32) + lowered(lowered_parts())) * mc_ref[...])
     sends[4].start()
-    for load in loads[6:]:
-        load.wait()
+    loads[1].wait()
 
     v = upc_ref[...].astype(F32)
     seed_c = pair_order([v[24 * r : 24 * r + 24] for r in range(24)]) * mc_ref[...]
@@ -452,21 +442,18 @@
             g_ref[p, rows_of(r + 2, 48, 48), :] = g[p].astype(BF)
         return 0
 
-    for n in range(2):
-        lax.fori_loop(12 * n, 12 * n + 12, fine_conv_grad, 0, unroll=2)
-        at = pl.ds(14 * 48 * n, 14 * 48)
-        hand(g_ref.at[:, at], go_ref.at[:, at])
-    hand(grad_ref.at[pl.ds(ROW_DOWN, plan.rows)], join_ref)
+    lax.fori_loop(0, 24, fine_conv_grad, 0, unroll=2)
+    join_ref[...] = grad_ref[ROW_DOWN : ROW_DOWN + plan.rows, :]
     for n, s in enumerate(plan.early):
         first = plan.first[s]
-        block_ref[n] = grad_ref[first : first + plan.rows, :].astype(BF)
-        hand(block_ref.at[n], blocks_ref.at[n])
+        blocks_ref[n] = grad_ref[first : first + plan.rows, :].astype(BF)
     for send in sends:
         send.wait()
 
 
 def layer_call(plan, *args):
     there = pl.BlockSpec(memory_space=pltpu.HBM)
+    whole = pl.BlockSpec(memory_space=pltpu.VMEM)
     low = lambda *shape: pltpu.VMEM(shape, BF)
     wide = lambda *shape: pltpu.VMEM(shape, F32)
     return pl.pallas_call(
@@ -476,26 +463,24 @@
             jax.ShapeDtypeStruct((CPIX, 128), F32),
             jax.ShapeDtypeStruct((PIX, 256), F32),
             jax.ShapeDtypeStruct((CPIX, 128), F32),
-            *(pltpu.HBM(shape, dtype) for shape, dtype in plan.handed),
+            *(jax.ShapeDtypeStruct(shape, dtype) for shape, dtype in plan.handed),
         ],
-        in_specs=[pl.BlockSpec(memory_space=pltpu.SMEM), pl.BlockSpec(memory_space=pltpu.VMEM)] + [there] * 8,
-        out_specs=[there] * 8,
+        in_specs=[pl.BlockSpec(memory_space=pltpu.SMEM)] + [whole] * 7 + [there] * 2,
+        out_specs=[there] * 4 + [whole] * 4,
         scratch_shapes=[
-            low(PIX, 256), low(CPIX, 128), low(128, 256), low(256, 1152), low(256, 768), low(12 * 256, 256),
-            low(PIX, 256), low(CPIX, 128),
-            wide(plan.tall, 128), low(len(plan.early), plan.rows, 128),
-            low(4, 26 * 48, 256), low(4, CPIX, 256), low(CPIX, 256),
+            low(PIX, 256), low(128, 256), low(256, 1152), low(256, 768), low(12 * 256, 256),
+            low(CPIX, 128), low(CPIX, 128),
+            wide(plan.tall, 128), low(4, CPIX, 256), low(CPIX, 256),
             wide(PIX, 256), wide(CPIX, 128), wide(CPIX, 128), low(CPIX, 128), wide(CPIX, 256),
             wide(PIX, 128), low(PIX, 128), wide(CPIX, 128),
             wide(8, 256), wide(8, 128),
-            low(CPIX, 256), low(CPIX, 512), wide(4, CPIX, 256), wide(PIX, 256), low(2, 28 * 48, 256), wide(8, 256),
+            low(CPIX, 256), low(CPIX, 512), wide(4, CPIX, 256), wide(PIX, 256), wide(8, 256),
             wide(2, 2, PIX, 128), wide(2, CPIX, 128),
-            pltpu.SemaphoreType.DMA((8,)),
+            pltpu.SemaphoreType.DMA((2,)),
             pltpu.SemaphoreType.DMA((2, 2)),
-            pltpu.SemaphoreType.DMA((plan.n + 4,)),
             pltpu.SemaphoreType.DMA((2,)),
         ],
-        compiler_params=pltpu.CompilerParams(vmem_limit_bytes=62 * 2**20),
+        compiler_params=pltpu.CompilerParams(vmem_limit_bytes=38 * 2**20),
         name="layer",
     )(*args)
 
@@ -550,9 +535,8 @@
 def gather_kernel(
     plan,
     master_ref, inp_hbm, upf_hbm,
-    vec_hbm, inpo_hbm, upfo_hbm, wu_hbm, wdn_hbm, wc6_hbm, wf_hbm,
-    inp_ref, upf_ref, vec_ref, inpo_ref, upfo_ref, wu_ref, wdn_ref, wc6_ref, wf_ref,
-    g_ref, w_ref, tmp_ref, in_sem, out_sem, send_sem, recv_sem, sib_send, sib_recv, far_send,
+    vec_ref, inpo_ref, upfo_ref, wu_ref, wdn_ref, wc6_ref, wf_ref,
+    inp_ref, upf_ref, g_ref, w_ref, tmp_ref, in_sem, send_sem, recv_sem, sib_send, sib_recv, far_send,
 ):
     d0, d1, d2 = plan.dims
     me, core, a, b, c = plan.here()
@@ -670,23 +654,14 @@
 
         lax.fori_loop(0, 24, one, 0, unroll=2)
 
-    outs = []
-
-    def put(src, dst):
-        copy_out = pltpu.make_async_copy(src, dst, out_sem.at[len(outs)])
-        copy_out.start()
-        outs.append(copy_out)
-
     for k in range(1, d0):
         for half in (0, 1):
             go(copy(me, half, plan.block(flip(a, k), b, c), core, far_send.at[k, half], recv_sem.at[me, half], core))
     own_column(0)
     loads[0].wait()
     parity(inp_ref, inpo_ref)
-    put(inpo_ref, inpo_hbm)
     loads[1].wait()
     parity(upf_ref, upfo_ref)
-    put(upfo_ref, upfo_hbm)
     for k in range(1, d0):
         own_column(k)
     for k in range(d0):
@@ -708,7 +683,6 @@
         else:
             w_ref[0 : plan.rows, :] = v
     vec_ref[...] = w_ref[ROW_VEC : ROW_VEC + 8, :]
-    put(vec_ref, vec_hbm)
     for dy in range(3):
         for h in range(2):
             g0, g1, g2 = (w_ref[pl.ds(2 * (3 * dy + dx) + h, 256, stride=18), :] for dx in range(3))
@@ -716,28 +690,23 @@
             for i, v in enumerate((g0, 0.5 * (outer + g1), 0.5 * (outer - g1), g2)):
                 at = 768 * i + 256 * dy
                 wf_ref[at : at + 256, 128 * h : 128 * h + 128] = v.astype(BF)
-    put(wf_ref, wf_hbm)
     for h in range(2):
         wu_ref[:, 128 * h : 128 * h + 128] = w_ref[pl.ds(ROW_UP + h, 128, stride=2), :].astype(BF)
-    put(wu_ref, wu_hbm)
     for t in range(9):
         p = (4, 5, 3, 7, 1, 8, 6, 2, 0).index(t)
         wdn_ref[:, 128 * p : 128 * p + 128] = w_ref[pl.ds(ROW_DOWN + t, 256, stride=9), :].astype(BF)
-    put(wdn_ref, wdn_hbm)
     wc6_ref[0:128, 384:768] = jnp.zeros((128, 384), BF)
     for t in range(9):
         dy, dx = t // 3, t % 3
         at, p = 128 * (dx + 1) // 2 // 128 * 128, dy + 3 * (dx // 2)
         wc6_ref[at : at + 128, 128 * p : 128 * p + 128] = w_ref[pl.ds(ROW_COARSE + t, 128, stride=9), :].astype(BF)
-    put(wc6_ref, wc6_hbm)
     for d in sent:
         d.wait_send()
-    for d in outs:
-        d.wait()
 
 
 def gather_call(plan, master, inp, upf):
     there = pl.BlockSpec(memory_space=pltpu.HBM)
+    whole = pl.BlockSpec(memory_space=pltpu.VMEM)
     low = lambda *shape: jax.ShapeDtypeStruct(shape, BF)
     outs = [
         jax.ShapeDtypeStruct((8, 128), F32), low(PIX, 256), low(PIX, 256), low(128, 256), low(256, 1152),
@@ -747,28 +716,27 @@
     sems = pltpu.SemaphoreType.DMA
     return pl.pallas_call(
         functools.partial(gather_kernel, plan),
-        out_shape=[pltpu.HBM(o.shape, o.dtype) for o in outs],
-        in_specs=[pl.BlockSpec(memory_space=pltpu.VMEM), there, there],
-        out_specs=[there] * 7,
-        scratch_shapes=[pltpu.VMEM((PIX, 256), BF), pltpu.VMEM((PIX, 256), BF)]
-        + [pltpu.VMEM(o.shape, o.dtype) for o in outs]
-        + [
+        out_shape=outs,
+        in_specs=[whole, there, there],
+        out_specs=[whole] * 7,
+        scratch_shapes=[
+            pltpu.VMEM((PIX, 256), BF), pltpu.VMEM((PIX, 256), BF),
             pltpu.VMEM((plan.n, plan.rows, 128), BF), pltpu.VMEM((plan.tall, 128), F32), pltpu.VMEM((2, PIX, 128), F32),
-            sems((2,)), sems((15,)), sems((plan.n, 2, max(d1 + d2 - 2, 1))), sems((plan.n, 2)), sems((plan.n, 2)),
+            sems((2,)), sems((plan.n, 2, max(d1 + d2 - 2, 1))), sems((plan.n, 2)), sems((plan.n, 2)),
             sems((plan.n, 2)), sems((d0, 2)),
         ],
-        compiler_params=pltpu.CompilerParams(collective_id=0, has_side_effects=True, vmem_limit_bytes=32 * 2**20),
+        compiler_params=pltpu.CompilerParams(collective_id=0, has_side_effects=True, vmem_limit_bytes=20 * 2**20),
         name="gather_weights",
     )(master, *(pltpu.with_memory_space_constraint(x, pltpu.HBM) for x in (inp, upf)))
 
 
 def reduce_kernel(
     plan,
-    u_hbm, g_hbm, join_hbm, blocks_hbm,
+    u_ref, g_ref, join_ref, blocks_ref,
     out_ref, tile_ref,
-    u_ref, g_ref, sums_ref, grad_ref, p_ref, q_ref, ua_ref, ub_ref, va_ref, vb_ref, z_ref, sa_ref, total_ref,
+    sums_ref, grad_ref, p_ref, q_ref, ua_ref, ub_ref, va_ref, vb_ref, z_ref, sa_ref, total_ref,
     n1_ref, n2_ref,
-    in_sem, q_send, q_recv, s1_send, s1_recv, s2_send, s2_recv, s3_send, s3_recv, t_send, t_recv,
+    q_send, q_recv, s1_send, s1_recv, s2_send, s2_recv, s3_send, s3_recv, t_send, t_recv,
     n1_send, n1_recv, n2_send, n2_recv,
 ):
     d0, d1, d2 = plan.dims
@@ -786,22 +754,12 @@
     others += [p[3] for p in plane]
     for other in others:
         pl.semaphore_signal(barrier, inc=1, device_id=other, device_id_type=MESH)
-    loads = [pltpu.make_async_copy(g_hbm, g_ref, in_sem.at[0])]
-    loads += [pltpu.make_async_copy(u_hbm.at[i], u_ref.at[i], in_sem.at[1 + i]) for i in range(4)]
-    loads.append(pltpu.make_async_copy(join_hbm, grad_ref.at[pl.ds(ROW_DOWN, plan.rows)], in_sem.at[5]))
-    count = len(plan.early)
-    loads.append(pltpu.make_async_copy(blocks_hbm, p_ref.at[pl.ds(plan.n - count, count)], in_sem.at[6]))
-    for load in loads:
-        load.start()
-
-    loads[0].wait()
     even, odd = g_ref[0], g_ref[1]
     sums_ref[0] = even + odd
     sums_ref[1] = even - odd
     products = []
     for i, ref in enumerate((g_ref.at[0], sums_ref.at[0], sums_ref.at[1], g_ref.at[1])):
         shifted = [ref[48 * (2 - dy) : 48 * (2 - dy) + 26 * 48, :] for dy in range(3)]
-        loads[1 + i].wait()
         products.append(dot_rows(u_ref[i], jnp.concatenate(shifted, axis=1)))
     p0, p1, p2, p3 = products
     both, apart = 0.5 * (p1 + p2), 0.5 * (p1 - p2)
@@ -810,11 +768,12 @@
             for j in range(2):
                 at = 256 * dy + 128 * j
                 grad_ref[pl.ds(2 * (3 * dy + dx) + j, 256, stride=18), :] = grad[:, at : at + 128]
-    loads[5].wait()
+    count = len(plan.early)
+    grad_ref[ROW_DOWN:, :] = join_ref[...]
     for s in range(plan.n - count):
         first = plan.first[s]
         p_ref[s] = grad_ref[first : first + plan.rows, :].astype(BF)
-    loads[6].wait()
+    p_ref[plan.n - count :] = blocks_ref[...]
     pl.semaphore_wait(barrier, len(others))
 
     sent = []
@@ -979,23 +938,23 @@
     return pl.pallas_call(
         functools.partial(reduce_kernel, plan),
         out_shape=[jax.ShapeDtypeStruct((plan.rows, 128), F32), jax.ShapeDtypeStruct((8, 128), F32)],
-        in_specs=[pl.BlockSpec(memory_space=pltpu.HBM)] * 4,
+        in_specs=[whole] * 4,
         out_specs=[whole] * 2,
         scratch_shapes=[
-            low(4, 26 * 48, 256), low(2, 28 * 48, 256), low(2, 28 * 48, 256), wide(ROW_DOWN + plan.rows, 128),
+            low(2, 28 * 48, 256), wide(ROW_DOWN + plan.rows, 128),
             low(plan.n, plan.rows, 128), low(plan.n, plan.part, 128),
             low(d0, d2, e1, plan.cut, 128), low(d0, d1, e2, rest, 128),
             low(d0, e2, plan.cut, 128), low(d0, e1, rest, 128), low(max(d0 - 1, 1), plan.part, 128),
             low(plan.n, plan.part, 128),
             wide(plan.rows, 128), wide(d0, 8, 128), wide(2 * d1 * d2, 8, 128),
-            sems((7,)), sems((plan.n,)), sems((plan.n,)), sems((plan.n, 2)),
+            sems((plan.n,)), sems((plan.n,)), sems((plan.n, 2)),
             sems((2, d0, max(d1, d2), max(e1, e2))), sems((2, d0, max(e1, e2))), sems((2, d0, max(e1, e2))),
             sems((d0,)), sems((d0,)), sems((1,)), sems((1,)),
             sems((d0,)), sems((d0,)), sems((2 * d1 * d2,)), sems((2 * d1 * d2,)),
         ],
-        compiler_params=pltpu.CompilerParams(collective_id=1, has_side_effects=True, vmem_limit_bytes=40 * 2**20),
+        compiler_params=pltpu.CompilerParams(collective_id=1, has_side_effects=True, vmem_limit_bytes=20 * 2**20),
         name="reduce_gradients",
-    )(*(pltpu.with_memory_space_constraint(x, pltpu.HBM) for x in handed))
+    )(*handed)
 
 
 def update_kernel(
@@ -1057,8 +1016,8 @@
         plan, master, input_fine.reshape(PIX, C1), upstream_fine.reshape(PIX, C1)
     )
     out_fine, out_coarse, gi_fine, gi_coarse, *handed = layer_call(
-        plan, extents, vec, inp, input_coarse.reshape(CPIX, C2), wu, wdn, wc6, wf, upf,
-        upstream_coarse.reshape(CPIX, C2),
+        plan, extents, vec, inp, wu, wdn, wc6, wf, upf,
+        input_coarse.reshape(CPIX, C2), upstream_coarse.reshape(CPIX, C2),
     )
     grad, tile = reduce_call(plan, *handed)
     grad_norm, new_master, new_first, new_second, new_average, norm_grads = update_call(

time: 109 us -> 104 us (0.954)
  Pallas kernels: 107 us -> 102 us
    pallas_call x1, Pallas kernels: 29.5 us -> 27 us  [reduce_call(): pl.pallas_call(functools.partial(reduce_kernel, plan), out_shape=[jax.Sha...]
    pallas_call x1, Pallas kernels: 23.7 us -> 22.2 us  [gather_call(): pl.pallas_call(functools.partial(gather_kernel, plan), out_shape=outs, in...]
    pallas_call x1, Pallas kernels: 52.8 us -> 51.6 us  [layer_call(): pl.pallas_call(functools.partial(layer_kernel, plan), out_shape=[jax.Shap...]
where the time goes in v6:
time: 104 us
  Pallas kernels  102 us (98%)
    pallas_call x1, Pallas kernels, layer_call(): pl.pallas_call(functools.partial(layer_kernel, plan), out_shape=[jax.Shap...  51.6 us
    pallas_call x1, Pallas kernels, reduce_call(): pl.pallas_call(functools.partial(reduce_kernel, plan), out_shape=[jax.Sha...  27 us
    pallas_call x1, Pallas kernels, gather_call(): pl.pallas_call(functools.partial(gather_kernel, plan), out_shape=outs, in...  22.2 us

profile of v6, /device:TPU:0, one launch (start us, length us, event | category | flops | bytes accessed | tf_op | source)
XLA Modules:
  0.0 104.0 jit_solution(17156370523264769285)
XLA Ops:
  0.6 0.0 copy-start.7
  0.7 0.0 copy-start
  0.7 0.9 copy-done
  1.6 0.0 copy-start.5
  1.6 0.0 copy-start.6
  1.6 22.2 %gather_weights.1 = (f32[8,128]{1,0:T(8,128)S(1)}, bf16[2304,256]{1,0:T(8,128)(2,1)S(1)}, bf16[2304,256]{1,0:T(8,128)(2,1)S(1)}, bf16[128,256]{1,0:T(8,128)(2,1)...) custom-call(f32[66608]{0:T(1024)S(1)} %copy-done, ...), custom_call_target="tpu_custom_call" | custom-call | tf_op jit(solution)/shard_map/gather_weights/pallas_call | solution.py:717
  23.9 0.0 copy-done.7
  23.9 0.0 copy-done.5
  23.9 0.0 copy-done.6
  23.9 51.6 %layer.1 = (f32[2304,256]{1,0:T(8,128)}, f32[576,128]{1,0:T(8,128)}, f32[2304,256]{1,0:T(8,128)}, f32[576,128]{1,0:T(8,128)}, bf16[4,1248,256]{2,1,0:T(8,128)(2,...) custom-call(s32[1,2]{1,0:T(1,128)S(1)} %copy-done.7, ...), custom_call_target="tpu_custom_call" | custom-call | tf_op jit(solution)/shard_map/layer/pallas_call | solution.py:459
  75.5 0.0 copy-start.1
  75.5 0.0 copy-start.2
  75.5 0.0 copy-start.3
  75.5 0.0 copy-start.4
  75.5 27.0 %reduce_gradients.1 = (f32[544,128]{1,0:T(8,128)S(1)}, f32[8,128]{1,0:T(8,128)S(1)}) custom-call(bf16[4,1248,256]{2,1,0:T(8,128)(2,1)S(1)} %get-tuple-element.44.u_ref, bf16[2,1344,256]{2,1,0:T(8,128)(2,1)S(1)} %get-tuple-element.45.g_ref, f32[544,128]{1,0:T(8,128)S(1)} %get-tuple-element.46.join_ref, bf16[7,544,128]{2,1,0:T(8,128)(2,1)S(1)} %get-tuple-element.47.blocks_ref), custom_call_target="tpu_custom_call" | custom-call | tf_op jit(solution)/shard_map/reduce_gradients/pallas_call | solution.py:938
  102.5 0.0 copy-done.1
  102.5 0.0 copy-done.2
  102.5 0.0 copy-done.3
  102.5 0.0 copy-done.4
  102.5 1.4 %update.1 = (f32[1,1]{1,0:T(1,128)}, f32[66608]{0:T(1024)}, f32[66608]{0:T(1024)}, f32[66608]{0:T(1024)}, f32[66608]{0:T(1024)}, /*index=5*/f32[768]{0:T(1024)}) custom-call(f32[544,128]{1,0:T(8,128)S(1)} %get-tuple-element.48.grad_ref, f32[8,128]{1,0:T(8,128)S(1)} %get-tuple-element.49.tile_ref, f32[66608]{0:T(1024)S(1)} %copy-done.1, f32[66608]{0:T(1024)S(1)} %copy-done.2, ...), custom_call_target="tpu_custom_call" | custom-call | tf_op jit(solution)/shard_map/update/pallas_call | solution.py:1001
Async XLA Ops:
  0.6 23.2 %copy-start.7 = (s32[1,2]{1,0:T(1,128)S(1)}, s32[1,2]{1,0:T(1,128)}, u32[]{:S(2)}) copy-start(s32[1,2]{1,0:T(1,128)} %ext_ref.1) | copy-start | bytes 28
  0.7 1.0 copy-start
  1.6 22.3 %copy-start.5 = (bf16[1,24,24,128]{3,2,1,0:T(8,128)(2,1)S(1)}, bf16[1,24,24,128]{3,2,1,0:T(8,128)(2,1)}, u32[]{:S(2)}) copy-start(bf16[1,24,24,128]{3,2,1,0:T(8,128)(2,1)} %param.10) | copy-start | bytes 442372
  1.6 22.3 %copy-start.6 = (bf16[1,24,24,128]{3,2,1,0:T(8,128)(2,1)S(1)}, bf16[1,24,24,128]{3,2,1,0:T(8,128)(2,1)}, u32[]{:S(2)}) copy-start(bf16[1,24,24,128]{3,2,1,0:T(8,128)(2,1)} %param.12) | copy-start | bytes 442372
  75.5 27.0 %copy-start.1 = (f32[66608]{0:T(1024)S(1)}, f32[66608]{0:T(1024)}, u32[]{:S(2)}) copy-start(f32[66608]{0:T(1024)} %master_ref.3) | copy-start | bytes 799300
  75.5 27.0 %copy-start.2 = (f32[66608]{0:T(1024)S(1)}, f32[66608]{0:T(1024)}, u32[]{:S(2)}) copy-start(f32[66608]{0:T(1024)} %first_ref.1) | copy-start | bytes 799300
  75.5 27.0 %copy-start.3 = (f32[66608]{0:T(1024)S(1)}, f32[66608]{0:T(1024)}, u32[]{:S(2)}) copy-start(f32[66608]{0:T(1024)} %second_ref.1) | copy-start | bytes 799300
  75.5 27.0 %copy-start.4 = (f32[66608]{0:T(1024)S(1)}, f32[66608]{0:T(1024)}, u32[]{:S(2)}) copy-start(f32[66608]{0:T(1024)} %average_ref.1) | copy-start | bytes 799300

commit v7 on v6

--- a/solution.py
+++ b/solution.py
@@ -192,7 +192,11 @@
         for p in range(2):
             at = rows_of(2 * r + p, 48, 48)
             h = x_ref[at, :] * scale + shift
-            y = h * jnp.tanh(h) + h
+            if final:
+                y = h * jnp.tanh(h) + h
+            else:
+                h = h.astype(BF)
+                y = h * jnp.tanh(h) + h
             if final:
                 m = twice(mf_ref[at, :])
                 low = ((y + inp_ref[at, :].astype(F32)) * m).astype(BF)
@@ -312,24 +316,29 @@
     coarse_branch()
     lax.fori_loop(0, ITERS, iterate, 0)
 
-    def last_rows(r, _):
-        unit(2 * r, True)
-        unit(2 * r + 1, True)
-        return 0
-
-    lax.fori_loop(0, 12, last_rows, 0)
-    sends = [
-        pltpu.make_async_copy(stage_ref.at[i, p], ref.at[:, 128 * p : 128 * p + 128], out_sem.at[i, p])
-        for i, ref in enumerate((outf_ref, gif_ref))
-        for p in range(2)
-    ]
-    sends += [
-        pltpu.make_async_copy(small_ref.at[i], ref, small_sem.at[i]) for i, ref in enumerate((outc_ref, gic_ref))
-    ]
-    sends[0].start()
-    sends[1].start()
+    sends = []
+
+    def put(i, ref, half):
+        for n in range(2):
+            for p in range(2):
+                at = pl.ds(48 * (12 * half + 24 * n), 576)
+                send = pltpu.make_async_copy(
+                    stage_ref.at[i, p, at], ref.at[at, 128 * p : 128 * p + 128], out_sem.at[i, half, n, p]
+                )
+                send.start()
+                sends.append(send)
+
+    def put_small(i, ref):
+        send = pltpu.make_async_copy(small_ref.at[i], ref, small_sem.at[i])
+        send.start()
+        sends.append(send)
+
+    for r in range(24):
+        unit(r, True)
+    put(0, outf_ref, 0)
+    put(0, outf_ref, 1)
     small_ref[0] = image_order((branch_ref[...].astype(F32) + lowered(lowered_parts())) * mc_ref[...])
-    sends[4].start()
+    put_small(0, outc_ref)
     loads[1].wait()
 
     v = upc_ref[...].astype(F32)
@@ -340,30 +349,18 @@
     glo_ref[:, 256:384] = row_up(seed_c).astype(BF)
     glo_ref[:, 384:512] = row_up(right).astype(BF)
 
-    def fold(j, _):
+    for j in range(12):
         total = None
         for i in range(4):
             at = rows_of(4 * j + i, 48, 48)
             seed = upf_ref[at, :].astype(F32) * twice(mf_ref[at, :])
             total = seed if total is None else total + seed
         gl_ref[rows_of(j, 48, 48), :] = total.astype(BF)
-        return 0
-
-    lax.fori_loop(0, 12, fold, 0, unroll=2)
-    up_grad = dot_rows(branch_ref[...], gl_ref[...])
-    for j in range(2):
-        grad_ref[pl.ds(ROW_UP + j, 128, stride=2), :] = up_grad[:, 128 * j : 128 * j + 128]
     g00, g01, g10, g11 = (glo_ref[:, 128 * i : 128 * i + 128] for i in range(4))
-    for i, (parts, taps) in enumerate(
-        (((g00,), (4,)), ((g00, g01), (5, 3)), ((g00, g10), (7, 1)), ((g00, g01, g10, g11), (8, 6, 2, 0)))
-    ):
-        down = dot_rows(ph_ref[i], jnp.concatenate(parts, axis=1))
-        for n, tap in enumerate(taps):
-            grad_ref[pl.ds(ROW_DOWN + tap, 256, stride=9), :] = down[:, 128 * n : 128 * n + 128]
 
     back_c = (seed_c + dot_lanes(gl_ref[...], wu_ref[...])) * mc_ref[...]
     small_ref[1] = image_order(back_c)
-    sends[5].start()
+    put_small(1, gic_ref)
 
     def pre_grad(gi, x, scale, shift, mean, inv):
         h = x * scale + shift
@@ -398,8 +395,9 @@
     back_ref[2] = dot_lanes(jnp.concatenate([g00, g10], axis=1), wdn_ref[:, 384:640])
     back_ref[3] = dot_lanes(glo_ref[...], wdn_ref[:, 640:1152])
 
-    def fine_back(j, carry):
-        sums = list(carry)
+    none8 = jnp.zeros((8, 256), F32)
+    sums = [none8, none8]
+    for j in range(12):
         for i in range(2):
             gi = []
             for p in range(2):
@@ -415,14 +413,18 @@
             for n in range(2):
                 half = slice(24 * n, 24 * n + 24)
                 interleave(stage_ref.at[1], 2 * j + i + 24 * n, gi[0][half], gi[1][half])
-        return tuple(sums)
-
-    none8 = jnp.zeros((8, 256), F32)
-    sum_gain, sum_bias = lax.fori_loop(0, 12, fine_back, (none8, none8))
-    sends[2].start()
-    sends[3].start()
-    sum_gain = jnp.sum(sum_gain, axis=0, keepdims=True)
-    sum_bias = jnp.sum(sum_bias, axis=0, keepdims=True)
+        if j % 6 == 5:
+            put(1, gif_ref, j // 6)
+    up_grad = dot_rows(branch_ref[...], gl_ref[...])
+    for j in range(2):
+        grad_ref[pl.ds(ROW_UP + j, 128, stride=2), :] = up_grad[:, 128 * j : 128 * j + 128]
+    for i, (parts, taps) in enumerate(
+        (((g00,), (4,)), ((g00, g01), (5, 3)), ((g00, g10), (7, 1)), ((g00, g01, g10, g11), (8, 6, 2, 0)))
+    ):
+        down = dot_rows(ph_ref[i], jnp.concatenate(parts, axis=1))
+        for n, tap in enumerate(taps):
+            grad_ref[pl.ds(ROW_DOWN + tap, 256, stride=9), :] = down[:, 128 * n : 128 * n + 128]
+    sum_gain, sum_bias = (jnp.sum(v, axis=0, keepdims=True) for v in sums)
     for p in range(2):
         at = slice(128 * p, 128 * p + 128)
         grad_ref[ROW_VEC + p : ROW_VEC + p + 1, :] = sum_gain[:, at]
@@ -431,7 +433,7 @@
             sum_bias[:, at], sum_gain[:, at], gain_f[:, at], C1 // GROUPS, nf
         )
 
-    def fine_conv_grad(r, _):
+    for r in range(24):
         g = []
         for p in range(2):
             at = rows_of(2 * r + p, 48, 48)
@@ -440,9 +442,6 @@
             g.append(v * twice(mf_ref[at, :]))
         for p in range(2):
             g_ref[p, rows_of(r + 2, 48, 48), :] = g[p].astype(BF)
-        return 0
-
-    lax.fori_loop(0, 24, fine_conv_grad, 0, unroll=2)
     join_ref[...] = grad_ref[ROW_DOWN : ROW_DOWN + plan.rows, :]
     for n, s in enumerate(plan.early):
         first = plan.first[s]
@@ -477,7 +476,7 @@
             low(CPIX, 256), low(CPIX, 512), wide(4, CPIX, 256), wide(PIX, 256), wide(8, 256),
             wide(2, 2, PIX, 128), wide(2, CPIX, 128),
             pltpu.SemaphoreType.DMA((2,)),
-            pltpu.SemaphoreType.DMA((2, 2)),
+            pltpu.SemaphoreType.DMA((2, 2, 2, 2)),
             pltpu.SemaphoreType.DMA((2,)),
         ],
         compiler_params=pltpu.CompilerParams(vmem_limit_bytes=38 * 2**20),

time: 104 us -> 103 us (level)
    pallas_call x1, Pallas kernels: 51.6 us -> 50.1 us  [layer_call(): pl.pallas_call(functools.partial(layer_kernel, plan), out_shape=[jax.Shap...]
where the time goes in v7:
time: 103 us
  Pallas kernels  101 us (98%)
    pallas_call x1, Pallas kernels, layer_call(): pl.pallas_call(functools.partial(layer_kernel, plan), out_shape=[jax.Shap...  50.1 us
    pallas_call x1, Pallas kernels, reduce_call(): pl.pallas_call(functools.partial(reduce_kernel, plan), out_shape=[jax.Sha...  27 us
    pallas_call x1, Pallas kernels, gather_call(): pl.pallas_call(functools.partial(gather_kernel, plan), out_shape=outs, in...  22.2 us

profile of v7, /device:TPU:0, one launch (start us, length us, event | category | flops | bytes accessed | tf_op | source)
XLA Modules:
  0.0 102.5 jit_solution(1675198382559876725)
XLA Ops:
  0.6 0.0 copy-start.7
  0.7 0.0 copy-start
  0.7 0.9 copy-done
  1.6 0.0 copy-start.5
  1.6 0.0 copy-start.6
  1.6 22.2 %gather_weights.1 = (f32[8,128]{1,0:T(8,128)S(1)}, bf16[2304,256]{1,0:T(8,128)(2,1)S(1)}, bf16[2304,256]{1,0:T(8,128)(2,1)S(1)}, bf16[128,256]{1,0:T(8,128)(2,1)...) custom-call(f32[66608]{0:T(1024)S(1)} %copy-done, ...), custom_call_target="tpu_custom_call" | custom-call | tf_op jit(solution)/shard_map/gather_weights/pallas_call | solution.py:716
  23.9 0.0 copy-done.7
  23.9 0.0 copy-done.5
  23.9 0.0 copy-done.6
  23.9 50.1 %layer.1 = (f32[2304,256]{1,0:T(8,128)}, f32[576,128]{1,0:T(8,128)}, f32[2304,256]{1,0:T(8,128)}, f32[576,128]{1,0:T(8,128)}, bf16[4,1248,256]{2,1,0:T(8,128)(2,...) custom-call(s32[1,2]{1,0:T(1,128)S(1)} %copy-done.7, ...), custom_call_target="tpu_custom_call" | custom-call | tf_op jit(solution)/shard_map/layer/pallas_call | solution.py:458
  74.0 0.0 copy-start.1
  74.0 0.0 copy-start.2
  74.0 0.0 copy-start.3
  74.0 0.0 copy-start.4
  74.1 27.0 %reduce_gradients.1 = (f32[544,128]{1,0:T(8,128)S(1)}, f32[8,128]{1,0:T(8,128)S(1)}) custom-call(bf16[4,1248,256]{2,1,0:T(8,128)(2,1)S(1)} %get-tuple-element.44.u_ref, bf16[2,1344,256]{2,1,0:T(8,128)(2,1)S(1)} %get-tuple-element.45.g_ref, f32[544,128]{1,0:T(8,128)S(1)} %get-tuple-element.46.join_ref, bf16[7,544,128]{2,1,0:T(8,128)(2,1)S(1)} %get-tuple-element.47.blocks_ref), custom_call_target="tpu_custom_call" | custom-call | tf_op jit(solution)/shard_map/reduce_gradients/pallas_call | solution.py:937
  101.0 0.0 copy-done.1
  101.0 0.0 copy-done.2
  101.1 0.0 copy-done.3
  101.1 0.0 copy-done.4
  101.1 1.4 %update.1 = (f32[1,1]{1,0:T(1,128)}, f32[66608]{0:T(1024)}, f32[66608]{0:T(1024)}, f32[66608]{0:T(1024)}, f32[66608]{0:T(1024)}, /*index=5*/f32[768]{0:T(1024)}) custom-call(f32[544,128]{1,0:T(8,128)S(1)} %get-tuple-element.48.grad_ref, f32[8,128]{1,0:T(8,128)S(1)} %get-tuple-element.49.tile_ref, f32[66608]{0:T(1024)S(1)} %copy-done.1, f32[66608]{0:T(1024)S(1)} %copy-done.2, ...), custom_call_target="tpu_custom_call" | custom-call | tf_op jit(solution)/shard_map/update/pallas_call | solution.py:1000
Async XLA Ops:
  0.6 23.2 %copy-start.7 = (s32[1,2]{1,0:T(1,128)S(1)}, s32[1,2]{1,0:T(1,128)}, u32[]{:S(2)}) copy-start(s32[1,2]{1,0:T(1,128)} %ext_ref.1) | copy-start | bytes 28
  0.7 1.0 copy-start
  1.6 22.3 %copy-start.5 = (bf16[1,24,24,128]{3,2,1,0:T(8,128)(2,1)S(1)}, bf16[1,24,24,128]{3,2,1,0:T(8,128)(2,1)}, u32[]{:S(2)}) copy-start(bf16[1,24,24,128]{3,2,1,0:T(8,128)(2,1)} %param.10) | copy-start | bytes 442372
  1.6 22.3 %copy-start.6 = (bf16[1,24,24,128]{3,2,1,0:T(8,128)(2,1)S(1)}, bf16[1,24,24,128]{3,2,1,0:T(8,128)(2,1)}, u32[]{:S(2)}) copy-start(bf16[1,24,24,128]{3,2,1,0:T(8,128)(2,1)} %param.12) | copy-start | bytes 442372
  74.0 27.0 %copy-start.1 = (f32[66608]{0:T(1024)S(1)}, f32[66608]{0:T(1024)}, u32[]{:S(2)}) copy-start(f32[66608]{0:T(1024)} %master_ref.3) | copy-start | bytes 799300
  74.0 27.0 %copy-start.2 = (f32[66608]{0:T(1024)S(1)}, f32[66608]{0:T(1024)}, u32[]{:S(2)}) copy-start(f32[66608]{0:T(1024)} %first_ref.1) | copy-start | bytes 799300
  74.0 27.0 %copy-start.3 = (f32[66608]{0:T(1024)S(1)}, f32[66608]{0:T(1024)}, u32[]{:S(2)}) copy-start(f32[66608]{0:T(1024)} %second_ref.1) | copy-start | bytes 799300
  74.0 27.0 %copy-start.4 = (f32[66608]{0:T(1024)S(1)}, f32[66608]{0:T(1024)}, u32[]{:S(2)}) copy-start(f32[66608]{0:T(1024)} %average_ref.1) | copy-start | bytes 799300

commit v8 on v7

--- a/solution.py
+++ b/solution.py
@@ -118,9 +118,9 @@
 
 def layer_kernel(
     plan,
-    ext_ref, vec_ref, inp_in, wu_in, wdn_in, wc6_in, wf_in, upf_ref, inc_hbm, upc_hbm,
-    outf_ref, outc_ref, gif_ref, gic_ref, u_ref, g_ref, join_ref, blocks_ref,
-    inp_ref, wu_ref, wdn_ref, wc6_ref, wf_ref, inc_in, upc_ref, grad_ref, ph_ref, c_ref, x_ref, xc_ref, inc_ref, branch_ref, lift_ref, mf_ref, mb_ref, mc_ref,
+    ext_ref, vec_ref, inp_in, wu_in, wdn_in, wc6_in, wf_in, upf_in, inc_hbm, upc_hbm,
+    outf_ref, outc_ref, gif_ref, gic_ref, uo_ref, go_ref, join_ref, blocks_ref,
+    g_ref, u_ref, upf_ref, inp_ref, wu_ref, wdn_ref, wc6_ref, wf_ref, inc_in, upc_ref, grad_ref, ph_ref, c_ref, x_ref, xc_ref, inc_ref, branch_ref, lift_ref, mf_ref, mb_ref, mc_ref,
     scf_ref, scc_ref, gl_ref, glo_ref, back_ref, gp_ref, row_ref, stage_ref, small_ref,
     in_sem, out_sem, small_sem,
 ):
@@ -335,6 +335,7 @@
 
     for r in range(24):
         unit(r, True)
+    upf_ref[...] = upf_in[...]
     put(0, outf_ref, 0)
     put(0, outf_ref, 1)
     small_ref[0] = image_order((branch_ref[...].astype(F32) + lowered(lowered_parts())) * mc_ref[...])
@@ -390,6 +391,7 @@
         grad_ref[pl.ds(ROW_COARSE + 3 * dy + 1, 128, stride=9), :] = pair[128:256, at]
         grad_ref[pl.ds(ROW_COARSE + 3 * dy + 2, 128, stride=9), :] = single[:, at]
 
+    uo_ref[...] = u_ref[...]
     back_ref[0] = dot_lanes(g00, wdn_ref[:, 0:128])
     back_ref[1] = dot_lanes(jnp.concatenate([g00, g01], axis=1), wdn_ref[:, 128:384])
     back_ref[2] = dot_lanes(jnp.concatenate([g00, g10], axis=1), wdn_ref[:, 384:640])
@@ -442,6 +444,7 @@
             g.append(v * twice(mf_ref[at, :]))
         for p in range(2):
             g_ref[p, rows_of(r + 2, 48, 48), :] = g[p].astype(BF)
+    go_ref[...] = g_ref[...]
     join_ref[...] = grad_ref[ROW_DOWN : ROW_DOWN + plan.rows, :]
     for n, s in enumerate(plan.early):
         first = plan.first[s]
@@ -467,7 +470,7 @@
         in_specs=[pl.BlockSpec(memory_space=pltpu.SMEM)] + [whole] * 7 + [there] * 2,
         out_specs=[there] * 4 + [whole] * 4,
         scratch_shapes=[
-            low(PIX, 256), low(128, 256), low(256, 1152), low(256, 768), low(12 * 256, 256),
+            low(2, 28 * 48, 256), low(4, 26 * 48, 256), low(PIX, 256), low(PIX, 256), low(128, 256), low(256, 1152), low(256, 768), low(12 * 256, 256),
             low(CPIX, 128), low(CPIX, 128),
             wide(plan.tall, 128), low(4, CPIX, 256), low(CPIX, 256),
             wide(PIX, 256), wide(CPIX, 128), wide(CPIX, 128), low(CPIX, 128), wide(CPIX, 256),

time: 103 us -> 101 us (0.981)
  Pallas kernels: 101 us -> 98.6 us
    pallas_call x1, Pallas kernels: 50.1 us -> 47.9 us  [layer_call(): pl.pallas_call(functools.partial(layer_kernel, plan), out_shape=[jax.Shap...]
where the time goes in v8:
time: 101 us; the launch traced here: 100 us
  Pallas kernels  98.6 us (98%)
    pallas_call x1, Pallas kernels, layer_call(): pl.pallas_call(functools.partial(layer_kernel, plan), out_shape=[jax.Shap...  47.9 us
    pallas_call x1, Pallas kernels, reduce_call(): pl.pallas_call(functools.partial(reduce_kernel, plan), out_shape=[jax.Sha...  27 us
    pallas_call x1, Pallas kernels, gather_call(): pl.pallas_call(functools.partial(gather_kernel, plan), out_shape=outs, in...  22.2 us

profile of v8, /device:TPU:0, one launch (start us, length us, event | category | flops | bytes accessed | tf_op | source)
XLA Modules:
  0.0 100.4 jit_solution(7236480724862959360)
XLA Ops:
  0.6 0.0 copy-start.7
  0.7 0.0 copy-start
  0.7 0.9 copy-done
  1.6 0.0 copy-start.5
  1.6 0.0 copy-start.6
  1.6 22.2 %gather_weights.1 = (f32[8,128]{1,0:T(8,128)S(1)}, bf16[2304,256]{1,0:T(8,128)(2,1)S(1)}, bf16[2304,256]{1,0:T(8,128)(2,1)S(1)}, bf16[128,256]{1,0:T(8,128)(2,1)...) custom-call(f32[66608]{0:T(1024)S(1)} %copy-done, ...), custom_call_target="tpu_custom_call" | custom-call | tf_op jit(solution)/shard_map/gather_weights/pallas_call | solution.py:719
  23.9 0.0 copy-done.7
  23.9 0.0 copy-done.5
  23.9 0.0 copy-done.6
  23.9 47.9 %layer.1 = (f32[2304,256]{1,0:T(8,128)}, f32[576,128]{1,0:T(8,128)}, f32[2304,256]{1,0:T(8,128)}, f32[576,128]{1,0:T(8,128)}, bf16[4,1248,256]{2,1,0:T(8,128)(2,...) custom-call(s32[1,2]{1,0:T(1,128)S(1)} %copy-done.7, ...), custom_call_target="tpu_custom_call" | custom-call | tf_op jit(solution)/shard_map/layer/pallas_call | solution.py:461
  71.8 0.0 copy-start.1
  71.8 0.0 copy-start.2
  71.9 0.0 copy-start.3
  71.9 0.0 copy-start.4
  71.9 27.0 %reduce_gradients.1 = (f32[544,128]{1,0:T(8,128)S(1)}, f32[8,128]{1,0:T(8,128)S(1)}) custom-call(bf16[4,1248,256]{2,1,0:T(8,128)(2,1)S(1)} %get-tuple-element.44.u_ref, bf16[2,1344,256]{2,1,0:T(8,128)(2,1)S(1)} %get-tuple-element.45.g_ref, f32[544,128]{1,0:T(8,128)S(1)} %get-tuple-element.46.join_ref, bf16[7,544,128]{2,1,0:T(8,128)(2,1)S(1)} %get-tuple-element.47.blocks_ref), custom_call_target="tpu_custom_call" | custom-call | tf_op jit(solution)/shard_map/reduce_gradients/pallas_call | solution.py:940
  98.9 0.0 copy-done.1
  98.9 0.0 copy-done.2
  98.9 0.0 copy-done.3
  98.9 0.0 copy-done.4
  98.9 1.4 %update.1 = (f32[1,1]{1,0:T(1,128)}, f32[66608]{0:T(1024)}, f32[66608]{0:T(1024)}, f32[66608]{0:T(1024)}, f32[66608]{0:T(1024)}, /*index=5*/f32[768]{0:T(1024)}) custom-call(f32[544,128]{1,0:T(8,128)S(1)} %get-tuple-element.48.grad_ref, f32[8,128]{1,0:T(8,128)S(1)} %get-tuple-element.49.tile_ref, f32[66608]{0:T(1024)S(1)} %copy-done.1, f32[66608]{0:T(1024)S(1)} %copy-done.2, ...), custom_call_target="tpu_custom_call" | custom-call | tf_op jit(solution)/shard_map/update/pallas_call | solution.py:1003
Async XLA Ops:
  0.6 23.2 %copy-start.7 = (s32[1,2]{1,0:T(1,128)S(1)}, s32[1,2]{1,0:T(1,128)}, u32[]{:S(2)}) copy-start(s32[1,2]{1,0:T(1,128)} %ext_ref.1) | copy-start | bytes 28
  0.7 1.0 copy-start
  1.6 22.3 %copy-start.5 = (bf16[1,24,24,128]{3,2,1,0:T(8,128)(2,1)S(1)}, bf16[1,24,24,128]{3,2,1,0:T(8,128)(2,1)}, u32[]{:S(2)}) copy-start(bf16[1,24,24,128]{3,2,1,0:T(8,128)(2,1)} %param.10) | copy-start | bytes 442372
  1.6 22.3 %copy-start.6 = (bf16[1,24,24,128]{3,2,1,0:T(8,128)(2,1)S(1)}, bf16[1,24,24,128]{3,2,1,0:T(8,128)(2,1)}, u32[]{:S(2)}) copy-start(bf16[1,24,24,128]{3,2,1,0:T(8,128)(2,1)} %param.12) | copy-start | bytes 442372
  71.8 27.0 %copy-start.1 = (f32[66608]{0:T(1024)S(1)}, f32[66608]{0:T(1024)}, u32[]{:S(2)}) copy-start(f32[66608]{0:T(1024)} %master_ref.3) | copy-start | bytes 799300
  71.8 27.0 %copy-start.2 = (f32[66608]{0:T(1024)S(1)}, f32[66608]{0:T(1024)}, u32[]{:S(2)}) copy-start(f32[66608]{0:T(1024)} %first_ref.1) | copy-start | bytes 799300
  71.9 27.0 %copy-start.3 = (f32[66608]{0:T(1024)S(1)}, f32[66608]{0:T(1024)}, u32[]{:S(2)}) copy-start(f32[66608]{0:T(1024)} %second_ref.1) | copy-start | bytes 799300
  71.9 27.0 %copy-start.4 = (f32[66608]{0:T(1024)S(1)}, f32[66608]{0:T(1024)}, u32[]{:S(2)}) copy-start(f32[66608]{0:T(1024)} %average_ref.1) | copy-start | bytes 799300

commit v9 on v8

--- a/solution.py
+++ b/solution.py
@@ -477,7 +477,7 @@
             wide(PIX, 128), low(PIX, 128), wide(CPIX, 128),
             wide(8, 256), wide(8, 128),
             low(CPIX, 256), low(CPIX, 512), wide(4, CPIX, 256), wide(PIX, 256), wide(8, 256),
-            wide(2, 2, PIX, 128), wide(2, CPIX, 128),
+            wide(2, 2, PIX + 8, 128), wide(2, CPIX, 128),
             pltpu.SemaphoreType.DMA((2,)),
             pltpu.SemaphoreType.DMA((2, 2, 2, 2)),
             pltpu.SemaphoreType.DMA((2,)),
@@ -491,6 +491,7 @@
     def __init__(self, shards, length):
         self.dims = {16: (4, 2, 2), 128: (4, 8, 4)}.get(shards, (shards, 1, 1))
         self.n, self.length = shards, length
+        self.tiled = length // 1024 * 1024
         self.first = [s * length // 128 for s in range(shards)]
         self.rows = -(-(length + 127) // 128)
         self.rows = -(-self.rows // 32) * 32
@@ -522,30 +523,36 @@
     return a
 
 
-def to_rows(plan, ref):
-    full = plan.length // 128
-    left = plan.length - 128 * full
-    parts = [ref[pl.ds(0, 128 * full)].reshape(full, 128)]
+def to_rows(plan, ref, tail_ref):
+    full = plan.tiled // 128
+    left = plan.length - plan.tiled
+    parts = [ref[...].reshape(full, 128)]
+    whole = left // 128
+    if whole:
+        parts.append(tail_ref[pl.ds(0, 128 * whole)].reshape(whole, 128))
+    left = left - 128 * whole
     if left:
-        tail = ref[pl.ds(128 * full, left)].reshape(1, left)
+        tail = tail_ref[pl.ds(128 * whole, left)].reshape(1, left)
         parts.append(jnp.concatenate([tail, jnp.zeros((1, 128 - left), F32)], axis=1))
-    have = full + (left > 0)
+    have = full + whole + (left > 0)
     parts.append(jnp.zeros((plan.rows - have, 128), F32))
     return jnp.concatenate(parts, axis=0)
 
 
 def gather_kernel(
     plan,
-    master_ref, inp_hbm, upf_hbm,
+    master_hbm, tail_ref, inp_hbm, upf_hbm,
     vec_ref, inpo_ref, upfo_ref, wu_ref, wdn_ref, wc6_ref, wf_ref,
-    inp_ref, upf_ref, g_ref, w_ref, tmp_ref, in_sem, send_sem, recv_sem, sib_send, sib_recv, far_send,
+    master_ref, inp_ref, upf_ref, g_ref, w_ref, tmp_ref, in_sem, send_sem, recv_sem, sib_send, sib_recv, far_send,
 ):
     d0, d1, d2 = plan.dims
     me, core, a, b, c = plan.here()
     part, cut = plan.part, plan.cut
     loads = [
         pltpu.make_async_copy(src, dst, in_sem.at[n])
-        for n, (src, dst) in enumerate(((inp_hbm, inp_ref), (upf_hbm, upf_ref)))
+        for n, (src, dst) in enumerate(
+            ((master_hbm.at[pl.ds(0, plan.tiled)], master_ref), (inp_hbm, inp_ref), (upf_hbm, upf_ref))
+        )
     ]
     for load in loads:
         load.start()
@@ -557,7 +564,8 @@
     for other in others:
         pl.semaphore_signal(barrier, inc=1, device_id=other, device_id_type=pl.DeviceIdType.MESH)
     off = (me * plan.length) % 128
-    x = pltpu.roll(to_rows(plan, master_ref), off, 1)
+    loads[0].wait()
+    x = pltpu.roll(to_rows(plan, master_ref, tail_ref), off, 1)
     row = lax.broadcasted_iota(jnp.int32, x.shape, 0)
     lane = lax.broadcasted_iota(jnp.int32, x.shape, 1)
     above = jnp.where(row == 0, 0.0, pltpu.roll(x, 1, 0))
@@ -660,9 +668,9 @@
         for half in (0, 1):
             go(copy(me, half, plan.block(flip(a, k), b, c), core, far_send.at[k, half], recv_sem.at[me, half], core))
     own_column(0)
-    loads[0].wait()
+    loads[1].wait()
     parity(inp_ref, inpo_ref)
-    loads[1].wait()
+    loads[2].wait()
     parity(upf_ref, upfo_ref)
     for k in range(1, d0):
         own_column(k)
@@ -719,17 +727,20 @@
     return pl.pallas_call(
         functools.partial(gather_kernel, plan),
         out_shape=outs,
-        in_specs=[whole, there, there],
+        in_specs=[there, whole, there, there],
         out_specs=[whole] * 7,
         scratch_shapes=[
-            pltpu.VMEM((PIX, 256), BF), pltpu.VMEM((PIX, 256), BF),
-            pltpu.VMEM((plan.n, plan.rows, 128), BF), pltpu.VMEM((plan.tall, 128), F32), pltpu.VMEM((2, PIX, 128), F32),
-            sems((2,)), sems((plan.n, 2, max(d1 + d2 - 2, 1))), sems((plan.n, 2)), sems((plan.n, 2)),
+            pltpu.VMEM((plan.tiled,), F32), pltpu.VMEM((PIX, 256), BF), pltpu.VMEM((PIX, 256), BF),
+            pltpu.VMEM((plan.n, plan.rows, 128), BF), pltpu.VMEM((plan.tall, 128), F32), pltpu.VMEM((2, PIX + 8, 128), F32),
+            sems((3,)), sems((plan.n, 2, max(d1 + d2 - 2, 1))), sems((plan.n, 2)), sems((plan.n, 2)),
             sems((plan.n, 2)), sems((d0, 2)),
         ],
         compiler_params=pltpu.CompilerParams(collective_id=0, has_side_effects=True, vmem_limit_bytes=20 * 2**20),
         name="gather_weights",
-    )(master, *(pltpu.with_memory_space_constraint(x, pltpu.HBM) for x in (inp, upf)))
+    )(
+        pltpu.with_memory_space_constraint(master, pltpu.HBM), master[plan.tiled :],
+        *(pltpu.with_memory_space_constraint(x, pltpu.HBM) for x in (inp, upf)),
+    )
 
 
 def reduce_kernel(

time: 101 us -> 99.7 us (0.987)
  no operation moved by 1% of the time
where the time goes in v9:
time: 99.7 us; the launch traced here: 99.5 us
  Pallas kernels  97.9 us (98%)
    pallas_call x1, Pallas kernels, layer_call(): pl.pallas_call(functools.partial(layer_kernel, plan), out_shape=[jax.Shap...  47.9 us
    pallas_call x1, Pallas kernels, reduce_call(): pl.pallas_call(functools.partial(reduce_kernel, plan), out_shape=[jax.Sha...  27.2 us
    pallas_call x1, Pallas kernels, gather_call(): pl.pallas_call(functools.partial(gather_kernel, plan), out_shape=outs, in...  21.3 us

profile of v9, /device:TPU:0, one launch (start us, length us, event | category | flops | bytes accessed | tf_op | source)
XLA Modules:
  0.0 99.5 jit_solution(11436585130623737660)
XLA Ops:
  0.6 0.0 copy-start.6
  0.7 0.0 copy-start.5
  0.7 0.0 copy-start.4
  0.7 0.7 slice.3.tail_ref
  1.4 21.3 %gather_weights.1 = (f32[8,128]{1,0:T(8,128)S(1)}, bf16[2304,256]{1,0:T(8,128)(2,1)S(1)}, bf16[2304,256]{1,0:T(8,128)(2,1)S(1)}, bf16[128,256]{1,0:T(8,128)(2,1)...) custom-call(f32[66608]{0:T(1024)} %master_ref.1, ...), custom_call_target="tpu_custom_call" | custom-call | tf_op jit(solution)/shard_map/gather_weights/pallas_call | solution.py:727
  22.8 0.0 copy-done.6
  22.8 0.0 copy-done.5
  22.8 0.0 copy-done.4
  22.8 47.9 %layer.1 = (f32[2304,256]{1,0:T(8,128)}, f32[576,128]{1,0:T(8,128)}, f32[2304,256]{1,0:T(8,128)}, f32[576,128]{1,0:T(8,128)}, bf16[4,1248,256]{2,1,0:T(8,128)(2,...) custom-call(s32[1,2]{1,0:T(1,128)S(1)} %copy-done.6, ...), custom_call_target="tpu_custom_call" | custom-call | tf_op jit(solution)/shard_map/layer/pallas_call | solution.py:461
  70.7 0.0 copy-start
  70.7 0.0 copy-start.1
  70.8 0.0 copy-start.2
  70.8 0.0 copy-start.3
  70.8 27.2 %reduce_gradients.1 = (f32[544,128]{1,0:T(8,128)S(1)}, f32[8,128]{1,0:T(8,128)S(1)}) custom-call(bf16[4,1248,256]{2,1,0:T(8,128)(2,1)S(1)} %get-tuple-element.44.u_ref, bf16[2,1344,256]{2,1,0:T(8,128)(2,1)S(1)} %get-tuple-element.45.g_ref, f32[544,128]{1,0:T(8,128)S(1)} %get-tuple-element.46.join_ref, bf16[7,544,128]{2,1,0:T(8,128)(2,1)S(1)} %get-tuple-element.47.blocks_ref), custom_call_target="tpu_custom_call" | custom-call | tf_op jit(solution)/shard_map/reduce_gradients/pallas_call | solution.py:951
  98.0 0.0 copy-done
  98.0 0.0 copy-done.1
  98.0 0.0 copy-done.2
  98.0 0.0 copy-done.3
  98.0 1.4 %update.1 = (f32[1,1]{1,0:T(1,128)}, f32[66608]{0:T(1024)}, f32[66608]{0:T(1024)}, f32[66608]{0:T(1024)}, f32[66608]{0:T(1024)}, /*index=5*/f32[768]{0:T(1024)}) custom-call(f32[544,128]{1,0:T(8,128)S(1)} %get-tuple-element.48.grad_ref, f32[8,128]{1,0:T(8,128)S(1)} %get-tuple-element.49.tile_ref, f32[66608]{0:T(1024)S(1)} %copy-done, f32[66608]{0:T(1024)S(1)} %copy-done.1, ...), custom_call_target="tpu_custom_call" | custom-call | tf_op jit(solution)/shard_map/update/pallas_call | solution.py:1014
Async XLA Ops:
  0.6 22.1 %copy-start.6 = (s32[1,2]{1,0:T(1,128)S(1)}, s32[1,2]{1,0:T(1,128)}, u32[]{:S(2)}) copy-start(s32[1,2]{1,0:T(1,128)} %ext_ref.1) | copy-start | bytes 28
  0.7 22.1 %copy-start.5 = (bf16[1,24,24,128]{3,2,1,0:T(8,128)(2,1)S(1)}, bf16[1,24,24,128]{3,2,1,0:T(8,128)(2,1)}, u32[]{:S(2)}) copy-start(bf16[1,24,24,128]{3,2,1,0:T(8,128)(2,1)} %param.12) | copy-start | bytes 442372
  0.7 22.1 %copy-start.4 = (bf16[1,24,24,128]{3,2,1,0:T(8,128)(2,1)S(1)}, bf16[1,24,24,128]{3,2,1,0:T(8,128)(2,1)}, u32[]{:S(2)}) copy-start(bf16[1,24,24,128]{3,2,1,0:T(8,128)(2,1)} %param.10) | copy-start | bytes 442372
  70.7 27.3 %copy-start = (f32[66608]{0:T(1024)S(1)}, f32[66608]{0:T(1024)}, u32[]{:S(2)}) copy-start(f32[66608]{0:T(1024)} %master_ref.1) | copy-start | bytes 799300
  70.7 27.3 %copy-start.1 = (f32[66608]{0:T(1024)S(1)}, f32[66608]{0:T(1024)}, u32[]{:S(2)}) copy-start(f32[66608]{0:T(1024)} %first_ref.1) | copy-start | bytes 799300
  70.8 27.3 %copy-start.2 = (f32[66608]{0:T(1024)S(1)}, f32[66608]{0:T(1024)}, u32[]{:S(2)}) copy-start(f32[66608]{0:T(1024)} %second_ref.1) | copy-start | bytes 799300
  70.8 27.3 %copy-start.3 = (f32[66608]{0:T(1024)S(1)}, f32[66608]{0:T(1024)}, u32[]{:S(2)}) copy-start(f32[66608]{0:T(1024)} %average_ref.1) | copy-start | bytes 799300

commit v10 on v9

--- a/solution.py
+++ b/solution.py
@@ -118,7 +118,7 @@
 
 def layer_kernel(
     plan,
-    ext_ref, vec_ref, inp_in, wu_in, wdn_in, wc6_in, wf_in, upf_in, inc_hbm, upc_hbm,
+    ext_ref, vec_ref, inp_in, w_ref, upf_in, inc_hbm, upc_hbm,
     outf_ref, outc_ref, gif_ref, gic_ref, uo_ref, go_ref, join_ref, blocks_ref,
     g_ref, u_ref, upf_ref, inp_ref, wu_ref, wdn_ref, wc6_ref, wf_ref, inc_in, upc_ref, grad_ref, ph_ref, c_ref, x_ref, xc_ref, inc_ref, branch_ref, lift_ref, mf_ref, mb_ref, mc_ref,
     scf_ref, scc_ref, gl_ref, glo_ref, back_ref, gp_ref, row_ref, stage_ref, small_ref,
@@ -168,10 +168,24 @@
     scc_ref[...] = jnp.zeros((8, 128), F32)
     scf_ref[1:2, :] = 0.5 * bias_f
     scc_ref[1:2, :] = 0.5 * bias_c
-    for src, dst in (
-        (inp_in, inp_ref), (wu_in, wu_ref), (wdn_in, wdn_ref), (wc6_in, wc6_ref), (wf_in, wf_ref)
-    ):
-        dst[...] = src[...]
+    for dy in range(3):
+        for h in range(2):
+            g0, g1, g2 = (w_ref[pl.ds(2 * (3 * dy + dx) + h, 256, stride=18), :] for dx in range(3))
+            outer = g0 + g2
+            for i, v in enumerate((g0, 0.5 * (outer + g1), 0.5 * (outer - g1), g2)):
+                at = 768 * i + 256 * dy
+                wf_ref[at : at + 256, 128 * h : 128 * h + 128] = v.astype(BF)
+    for h in range(2):
+        wu_ref[:, 128 * h : 128 * h + 128] = w_ref[pl.ds(ROW_UP + h, 128, stride=2), :].astype(BF)
+    for t in range(9):
+        p = (4, 5, 3, 7, 1, 8, 6, 2, 0).index(t)
+        wdn_ref[:, 128 * p : 128 * p + 128] = w_ref[pl.ds(ROW_DOWN + t, 256, stride=9), :].astype(BF)
+    wc6_ref[0:128, 384:768] = jnp.zeros((128, 384), BF)
+    for t in range(9):
+        dy, dx = t // 3, t % 3
+        at, p = 128 * (dx + 1) // 2 // 128 * 128, dy + 3 * (dx // 2)
+        wc6_ref[at : at + 128, 128 * p : 128 * p + 128] = w_ref[pl.ds(ROW_COARSE + t, 128, stride=9), :].astype(BF)
+    inp_ref[...] = inp_in[...]
     loads[0].wait()
     v = inc_in[...].astype(F32)
     inc_ref[...] = pair_order([v[24 * r : 24 * r + 24] for r in range(24)])
@@ -467,7 +481,7 @@
             jax.ShapeDtypeStruct((CPIX, 128), F32),
             *(jax.ShapeDtypeStruct(shape, dtype) for shape, dtype in plan.handed),
         ],
-        in_specs=[pl.BlockSpec(memory_space=pltpu.SMEM)] + [whole] * 7 + [there] * 2,
+        in_specs=[pl.BlockSpec(memory_space=pltpu.SMEM)] + [whole] * 4 + [there] * 2,
         out_specs=[there] * 4 + [whole] * 4,
         scratch_shapes=[
             low(2, 28 * 48, 256), low(4, 26 * 48, 256), low(PIX, 256), low(PIX, 256), low(128, 256), low(256, 1152), low(256, 768), low(12 * 256, 256),
@@ -542,8 +556,8 @@
 def gather_kernel(
     plan,
     master_hbm, tail_ref, inp_hbm, upf_hbm,
-    vec_ref, inpo_ref, upfo_ref, wu_ref, wdn_ref, wc6_ref, wf_ref,
-    master_ref, inp_ref, upf_ref, g_ref, w_ref, tmp_ref, in_sem, send_sem, recv_sem, sib_send, sib_recv, far_send,
+    vec_ref, inpo_ref, upfo_ref, w_ref,
+    master_ref, inp_ref, upf_ref, g_ref, tmp_ref, in_sem, send_sem, recv_sem, sib_send, sib_recv, far_send,
 ):
     d0, d1, d2 = plan.dims
     me, core, a, b, c = plan.here()
@@ -693,23 +707,6 @@
         else:
             w_ref[0 : plan.rows, :] = v
     vec_ref[...] = w_ref[ROW_VEC : ROW_VEC + 8, :]
-    for dy in range(3):
-        for h in range(2):
-            g0, g1, g2 = (w_ref[pl.ds(2 * (3 * dy + dx) + h, 256, stride=18), :] for dx in range(3))
-            outer = g0 + g2
-            for i, v in enumerate((g0, 0.5 * (outer + g1), 0.5 * (outer - g1), g2)):
-                at = 768 * i + 256 * dy
-                wf_ref[at : at + 256, 128 * h : 128 * h + 128] = v.astype(BF)
-    for h in range(2):
-        wu_ref[:, 128 * h : 128 * h + 128] = w_ref[pl.ds(ROW_UP + h, 128, stride=2), :].astype(BF)
-    for t in range(9):
-        p = (4, 5, 3, 7, 1, 8, 6, 2, 0).index(t)
-        wdn_ref[:, 128 * p : 128 * p + 128] = w_ref[pl.ds(ROW_DOWN + t, 256, stride=9), :].astype(BF)
-    wc6_ref[0:128, 384:768] = jnp.zeros((128, 384), BF)
-    for t in range(9):
-        dy, dx = t // 3, t % 3
-        at, p = 128 * (dx + 1) // 2 // 128 * 128, dy + 3 * (dx // 2)
-        wc6_ref[at : at + 128, 128 * p : 128 * p + 128] = w_ref[pl.ds(ROW_COARSE + t, 128, stride=9), :].astype(BF)
     for d in sent:
         d.wait_send()
 
@@ -719,8 +716,8 @@
     whole = pl.BlockSpec(memory_space=pltpu.VMEM)
     low = lambda *shape: jax.ShapeDtypeStruct(shape, BF)
     outs = [
-        jax.ShapeDtypeStruct((8, 128), F32), low(PIX, 256), low(PIX, 256), low(128, 256), low(256, 1152),
-        low(256, 768), low(12 * 256, 256),
+        jax.ShapeDtypeStruct((8, 128), F32), low(PIX, 256), low(PIX, 256),
+        jax.ShapeDtypeStruct((plan.tall, 128), F32),
     ]
     d0, d1, d2 = plan.dims
     sems = pltpu.SemaphoreType.DMA
@@ -728,10 +725,10 @@
         functools.partial(gather_kernel, plan),
         out_shape=outs,
         in_specs=[there, whole, there, there],
-        out_specs=[whole] * 7,
+        out_specs=[whole] * 4,
         scratch_shapes=[
             pltpu.VMEM((plan.tiled,), F32), pltpu.VMEM((PIX, 256), BF), pltpu.VMEM((PIX, 256), BF),
-            pltpu.VMEM((plan.n, plan.rows, 128), BF), pltpu.VMEM((plan.tall, 128), F32), pltpu.VMEM((2, PIX + 8, 128), F32),
+            pltpu.VMEM((plan.n, plan.rows, 128), BF), pltpu.VMEM((2, PIX + 8, 128), F32),
             sems((3,)), sems((plan.n, 2, max(d1 + d2 - 2, 1))), sems((plan.n, 2)), sems((plan.n, 2)),
             sems((plan.n, 2)), sems((d0, 2)),
         ],
@@ -867,25 +864,26 @@
             go(sa_ref.at[s, cut:part], vb_ref.at[a2, i - 1], s2_send.at[1, a2, i - 1], s2_recv.at[1, a2, i - 1],
                {"fsdp": plan.block(a, b2, c), "rep": core})
 
-    def column(k):
+    def column(k, half):
         a2 = (a + k) % d0
         s = plan.block(a2, b, c)
-        got(q_ref.at[s], q_recv.at[s])
-        x = plus(pair(s, 0), from1(0, a2, c))
-        for j in range(1, d2):
-            got(va_ref.at[a2, j - 1], s2_recv.at[0, a2, j - 1])
-            x = x + va_ref[a2, j - 1].astype(F32)
-        y = plus(pair(s, 1), from1(1, a2, b))
-        for i in range(1, d1):
-            got(vb_ref.at[a2, i - 1], s2_recv.at[1, a2, i - 1])
-            y = y + vb_ref[a2, i - 1].astype(F32)
-        return s, x, y
+        if half == 0:
+            got(q_ref.at[s], q_recv.at[s])
+        total = plus(pair(s, half), from1(half, a2, (c, b)[half]))
+        ref = (va_ref, vb_ref)[half]
+        for i in range(1, (d2, d1)[half]):
+            got(ref.at[a2, i - 1], s2_recv.at[half, a2, i - 1])
+            total = total + ref[a2, i - 1].astype(F32)
+        return s, total
 
     def step3(k):
-        s, x, y = column(k)
-        sa_ref[s, 0:cut, :] = x.astype(BF)
-        sa_ref[s, cut:part, :] = y.astype(BF)
-        go(sa_ref.at[s], z_ref.at[k - 1], s3_send.at[k - 1], s3_recv.at[k - 1], {"fsdp": plan.block((a + k) % d0, b, c), "rep": core})
+        for half, (start, size) in enumerate(halves):
+            s, total = column(k, half)
+            sa_ref[s, start:start + size, :] = total.astype(BF)
+            go(
+                sa_ref.at[s, start:start + size], z_ref.at[k - 1, start:start + size], s3_send.at[k - 1, half],
+                s3_recv.at[k - 1, half], {"fsdp": s, "rep": core},
+            )
 
     for n in range(d0 + 2):
         if n < d0:
@@ -894,11 +892,14 @@
             step2(order[n - 1])
         if 0 <= n - 2 < d0 - 1:
             step3(order[n - 2])
-    _, x, y = column(0)
-    total = jnp.concatenate([x, y], axis=0)
-    for k in range(1, d0):
-        got(z_ref.at[k - 1], s3_recv.at[k - 1])
-        total = total + z_ref[k - 1].astype(F32)
+    sums = []
+    for half, (start, size) in enumerate(halves):
+        _, total = column(0, half)
+        for k in range(1, d0):
+            got(z_ref.at[k - 1, start:start + size], s3_recv.at[k - 1, half])
+            total = total + z_ref[k - 1, start:start + size, :].astype(F32)
+        sums.append(total)
+    total = jnp.concatenate(sums, axis=0)
     total_ref[pl.ds(mine, part), :] = total
     go(total_ref.at[pl.ds(mine, part)], total_ref.at[pl.ds(mine, part)], t_send.at[0], t_recv.at[0], {"fsdp": me, "rep": 1 - core})
 
@@ -962,7 +963,7 @@
             wide(plan.rows, 128), wide(d0, 8, 128), wide(2 * d1 * d2, 8, 128),
             sems((plan.n,)), sems((plan.n,)), sems((plan.n, 2)),
             sems((2, d0, max(d1, d2), max(e1, e2))), sems((2, d0, max(e1, e2))), sems((2, d0, max(e1, e2))),
-            sems((d0,)), sems((d0,)), sems((1,)), sems((1,)),
+            sems((d0, 2)), sems((d0, 2)), sems((1,)), sems((1,)),
             sems((d0,)), sems((d0,)), sems((2 * d1 * d2,)), sems((2 * d1 * d2,)),
         ],
         compiler_params=pltpu.CompilerParams(collective_id=1, has_side_effects=True, vmem_limit_bytes=20 * 2**20),
@@ -1025,11 +1026,11 @@
     input_fine, input_coarse, upstream_fine, upstream_coarse, extents, master, first_moment, second_moment, average
 ):
     plan = Plan(lax.axis_size("fsdp"), master.shape[0])
-    vec, inp, upf, wu, wdn, wc6, wf = gather_call(
+    vec, inp, upf, rows = gather_call(
         plan, master, input_fine.reshape(PIX, C1), upstream_fine.reshape(PIX, C1)
     )
     out_fine, out_coarse, gi_fine, gi_coarse, *handed = layer_call(
-        plan, extents, vec, inp, wu, wdn, wc6, wf, upf,
+        plan, extents, vec, inp, rows, upf,
         input_coarse.reshape(CPIX, C2), upstream_coarse.reshape(CPIX, C2),
     )
     grad, tile = reduce_call(plan, *handed)

time: 99.7 us -> 99.9 us (level)
  no operation moved by 1% of the time
where the time goes in v10:
time: 99.9 us; the launch traced here: 99.7 us
  Pallas kernels  98.1 us (98%)
    pallas_call x1, Pallas kernels, layer_call(): pl.pallas_call(functools.partial(layer_kernel, plan), out_shape=[jax.Shap...  48.3 us
    pallas_call x1, Pallas kernels, reduce_call(): pl.pallas_call(functools.partial(reduce_kernel, plan), out_shape=[jax.Sha...  27.3 us
    pallas_call x1, Pallas kernels, gather_call(): pl.pallas_call(functools.partial(gather_kernel, plan), out_shape=outs, in...  21.1 us

profile of v10, /device:TPU:0, one launch (start us, length us, event | category | flops | bytes accessed | tf_op | source)
XLA Modules:
  0.0 99.7 jit_solution(5989228448353524226)
XLA Ops:
  0.6 0.0 copy-start.6
  0.7 0.0 copy-start.5
  0.7 0.0 copy-start.4
  0.7 0.7 slice.3.tail_ref
  1.4 21.1 %gather_weights.1 = (f32[8,128]{1,0:T(8,128)S(1)}, bf16[2304,256]{1,0:T(8,128)(2,1)S(1)}, bf16[2304,256]{1,0:T(8,128)(2,1)S(1)}, f32[8352,128]{1,0:T(8,128)S(1)}) custom-call(f32[66608]{0:T(1024)} %master_ref.1, f32[48]{0:T(128)S(1)} %slice.3.tail_ref, bf16[2304,256]{1,0:T(8,128)(2,1)} %bitcast.11, bf16[2304,256]{1,0:T(8,128)(2,1)} %bitcast.12), custom_call_target="tpu_custom_call" | custom-call | tf_op jit(solution)/shard_map/gather_weights/pallas_call | solution.py:724
  22.5 0.0 copy-done.6
  22.5 0.0 copy-done.5
  22.5 0.0 copy-done.4
  22.6 48.3 %layer.1 = (f32[2304,256]{1,0:T(8,128)}, f32[576,128]{1,0:T(8,128)}, f32[2304,256]{1,0:T(8,128)}, f32[576,128]{1,0:T(8,128)}, bf16[4,1248,256]{2,1,0:T(8,128)(2,...) custom-call(s32[1,2]{1,0:T(1,128)S(1)} %copy-done.6, ...), custom_call_target="tpu_custom_call" | custom-call | tf_op jit(solution)/shard_map/layer/pallas_call | solution.py:475
  70.9 0.0 copy-start
  70.9 0.0 copy-start.1
  70.9 0.0 copy-start.2
  70.9 0.0 copy-start.3
  70.9 27.3 %reduce_gradients.1 = (f32[544,128]{1,0:T(8,128)S(1)}, f32[8,128]{1,0:T(8,128)S(1)}) custom-call(bf16[4,1248,256]{2,1,0:T(8,128)(2,1)S(1)} %get-tuple-element.38.u_ref, bf16[2,1344,256]{2,1,0:T(8,128)(2,1)S(1)} %get-tuple-element.39.g_ref, f32[544,128]{1,0:T(8,128)S(1)} %get-tuple-element.40.join_ref, bf16[7,544,128]{2,1,0:T(8,128)(2,1)S(1)} %get-tuple-element.41.blocks_ref), custom_call_target="tpu_custom_call" | custom-call | tf_op jit(solution)/shard_map/reduce_gradients/pallas_call | solution.py:952
  98.2 0.0 copy-done
  98.2 0.0 copy-done.1
  98.2 0.0 copy-done.2
  98.2 0.0 copy-done.3
  98.2 1.4 %update.1 = (f32[1,1]{1,0:T(1,128)}, f32[66608]{0:T(1024)}, f32[66608]{0:T(1024)}, f32[66608]{0:T(1024)}, f32[66608]{0:T(1024)}, /*index=5*/f32[768]{0:T(1024)}) custom-call(f32[544,128]{1,0:T(8,128)S(1)} %get-tuple-element.42.grad_ref, f32[8,128]{1,0:T(8,128)S(1)} %get-tuple-element.43.tile_ref, f32[66608]{0:T(1024)S(1)} %copy-done, f32[66608]{0:T(1024)S(1)} %copy-done.1, ...), custom_call_target="tpu_custom_call" | custom-call | tf_op jit(solution)/shard_map/update/pallas_call | solution.py:1015
Async XLA Ops:
  0.6 21.9 %copy-start.6 = (s32[1,2]{1,0:T(1,128)S(1)}, s32[1,2]{1,0:T(1,128)}, u32[]{:S(2)}) copy-start(s32[1,2]{1,0:T(1,128)} %ext_ref.1) | copy-start | bytes 28
  0.7 21.9 %copy-start.5 = (bf16[1,24,24,128]{3,2,1,0:T(8,128)(2,1)S(1)}, bf16[1,24,24,128]{3,2,1,0:T(8,128)(2,1)}, u32[]{:S(2)}) copy-start(bf16[1,24,24,128]{3,2,1,0:T(8,128)(2,1)} %param.12) | copy-start | bytes 442372
  0.7 21.9 %copy-start.4 = (bf16[1,24,24,128]{3,2,1,0:T(8,128)(2,1)S(1)}, bf16[1,24,24,128]{3,2,1,0:T(8,128)(2,1)}, u32[]{:S(2)}) copy-start(bf16[1,24,24,128]{3,2,1,0:T(8,128)(2,1)} %param.10) | copy-start | bytes 442372
  70.9 27.3 %copy-start = (f32[66608]{0:T(1024)S(1)}, f32[66608]{0:T(1024)}, u32[]{:S(2)}) copy-start(f32[66608]{0:T(1024)} %master_ref.1) | copy-start | bytes 799300
  70.9 27.3 %copy-start.1 = (f32[66608]{0:T(1024)S(1)}, f32[66608]{0:T(1024)}, u32[]{:S(2)}) copy-start(f32[66608]{0:T(1024)} %first_ref.1) | copy-start | bytes 799300
  70.9 27.3 %copy-start.2 = (f32[66608]{0:T(1024)S(1)}, f32[66608]{0:T(1024)}, u32[]{:S(2)}) copy-start(f32[66608]{0:T(1024)} %second_ref.1) | copy-start | bytes 799300
  70.9 27.3 %copy-start.3 = (f32[66608]{0:T(1024)S(1)}, f32[66608]{0:T(1024)}, u32[]{:S(2)}) copy-start(f32[66608]{0:T(1024)} %average_ref.1) | copy-start | bytes 799300
